TPU v7x, 32 devices: a whole 2x2x4 slice. The times are simulated.
32 devices in a mesh: row: 4 (over z), col: 8 (over y, x, core).
Axes of the slice: x: 2, y: 2, z: 4, core: 2. Of those that a mesh axis runs over, the one named last changes fastest.
Arguments:
- embeddings: bfloat16 [10240, 256], P(('row', 'col')), may hold values from -90 to 90
- start_vectors: float32 [32, 10240], P(None, ('row', 'col')), may hold values from -6 to 6
Outputs:
- vectors: float32 [32, 10240], P(None, ('row', 'col'))
- degrees: float32 [10240], P(('row', 'col'))
All inputs are finite; a program needn't handle non-finite values.
Results may differ from a plain program's by a relative error of at most 0.015.
Values may be sent and summed in bfloat16 or wider, within the bound.
No kernel may reach another device: no remote copies, remote signals or barrier semaphores. Data moves between devices by JAX's collectives and lax.ppermute only.
A program may use at most 128 MiB of HBM per device.

v0:
```python
import math

import jax
import jax.numpy as jnp
from jax import lax
from jax.sharding import PartitionSpec as P

ITERS = 2


def normalize(embeddings):
    values = embeddings.astype(jnp.float32)
    power = jnp.mean(values * values, axis=1, keepdims=True)
    width = embeddings.shape[1]
    return (values * lax.rsqrt(power + 1e-06) / jnp.sqrt(jnp.float32(width))).astype(jnp.bfloat16)


def build_tile(row_emb, col_emb):
    total_rows = row_emb.shape[0]
    step_rows = math.gcd(total_rows, 512)
    pieces = row_emb.reshape(total_rows // step_rows, step_rows, row_emb.shape[1])

    def one_piece(piece):
        inner = lax.dot_general(
            piece, col_emb, (((1,), (1,)), ((), ())), preferred_element_type=jnp.float32
        )
        return jnp.exp(8.0 * (inner - 1.0)).astype(jnp.bfloat16)

    return lax.map(one_piece, pieces).reshape(total_rows, col_emb.shape[0])


def local(embeddings, start_vectors):
    own_unit = normalize(embeddings)
    row_emb = lax.all_gather(own_unit, "col", axis=0, tiled=True)
    col_emb = lax.all_gather(own_unit, "row", axis=0, tiled=True)
    tile = build_tile(row_emb, col_emb)
    partial_rows = jnp.sum(tile, axis=1, dtype=jnp.float32)
    degrees = lax.psum_scatter(partial_rows, "col", scatter_dimension=0, tiled=True)
    scale = 1.0 / jnp.sqrt(degrees)
    current = start_vectors
    for step in range(ITERS):
        scaled = (current * scale[None, :]).astype(jnp.bfloat16)
        partial_value = lax.dot_general(
            lax.all_gather(scaled, "row", axis=1, tiled=True),
            tile,
            (((1,), (1,)), ((), ())),
            preferred_element_type=jnp.float32,
        )
        summed = lax.psum_scatter(
            partial_value.astype(jnp.bfloat16), "col", scatter_dimension=1, tiled=True
        ).astype(jnp.float32)
        image = summed * scale[None, :]
        local_gram = jnp.dot(image, image.T, precision=lax.Precision.HIGHEST)
        gram = lax.psum(local_gram, ("row", "col"))
        lower = jnp.linalg.cholesky(gram)
        current = lax.linalg.triangular_solve(lower, image, left_side=True, lower=True)
    return (current, degrees)


def solution(mesh):
    return jax.shard_map(
        local,
        mesh=mesh,
        in_specs=(P(("row", "col"), None), P(None, ("row", "col"))),
        out_specs=(P(None, ("row", "col")), P(("row", "col"))),
        check_vma=False,
    )
```

profile of v0, /device:TPU:0, one launch (start us, length us, event | category | flops | bytes accessed | tf_op | source)
XLA Modules:
  0.0 290.0 jit_solution(8660918627550217993)
XLA Ops:
  7.2 0.0 all-gather.4.cloned.1.call-start
  7.2 1.1 fusion.10
  8.3 1.7 fusion.12
  10.0 0.0 all-gather.4.cloned.1.call-update
  10.0 0.0 reduce-scatter.7.cloned.1.call-start
  10.1 1.2 dynamic-slice
  12.0 19.8 %all_gather.13 = bf16[1280,256]{1,0:T(8,128)(2,1)S(1)} all-gather(bf16[320,256]{1,0:T(8,128)(2,1)} %fusion.12), channel_id=1, replica_groups=mesh['row'=4,'col'=8] {'row'}, dimensions={0}, use_global_device_ids=true | all-gather | bytes 819200 | tf_op jit(solution)/shard_map/all_gather | solution.py:35
  31.8 5.7 %all-gather.4.cloned.1.call-done = bf16[2560,256]{1,0:T(8,128)(2,1)} async-done(((bf16[320,256]{1,0:T(8,128)(2,1)}), bf16[2560,256]{1,0:T(8,128)(2,1)}) %all-gather.4.cloned.1.call-update) | async-done | bytes 1310736 | tf_op jit(solution)/shard_map/all_gather | solution.py:34
  37.5 13.1 %while.12 = (s32[]{:T(128)}, bf16[5,512,1280]{2,1,0:T(8,128)(2,1)}, bf16[5,512,256]{2,1,0:T(8,128)(2,1)}, bf16[1280,256]{1,0:T(8,128)(2,1)S(1)}, s32[]{:T(128)}) while((s32[]{:T(128)}, bf16[5,512,1280]{2,1,0:T(8,128)(2,1)}, bf16[5,512,256]{2,1,0:T(8,128)(2,1)}, bf16[1280,256]{1,0:T(8,128)(2,1)S(1)}, s32[]{:T(128)}) %tuple.42), condition=%wide.region_2.3_spmd, body=%wide.region_1.2_spmd.sunk | while | flops 337510400 | bytes 2229309 | solution.py:29
  37.5 2.6 fusion.40
  40.1 2.6 fusion.40
  42.7 2.6 fusion.40
  45.3 2.6 fusion.40
  48.0 2.6 fusion.40
  50.6 3.8 %convert_reduce_fusion = f32[5,512]{1,0:T(8,128)S(1)} fusion(bf16[5,512,1280]{2,1,0:T(8,128)(2,1)} %get-tuple-element.57), kind=kLoop, calls=%fused_computation.9 | loop fusion | flops 6551040 | bytes 6563840 | tf_op jit(solution)/shard_map/reduce_sum | solution.py:37
  54.4 23.5 %all-reduce = f32[2560]{0:T(1024)S(1)} all-reduce(f32[2560]{0:T(1024)S(1)} %reduce_sum.22), channel_id=2, replica_groups=mesh['row'=4,'col'=8] {'col'}, use_global_device_ids=true, to_apply=%region_4.5.clone | all-reduce | flops 2560 | bytes 20480
  77.9 0.7 fusion.29
  78.6 13.4 %all-gather = bf16[4,320,32]{1,2,0:T(8,128)(2,1)S(1)} all-gather(bf16[1,320,32]{1,2,0:T(8,128)(2,1)S(1)} %fusion.16), channel_id=1, replica_groups=mesh['row'=4,'col'=8] {'row'}, dimensions={0}, use_global_device_ids=true | all-gather | bytes 102400 | tf_op jit(solution)/shard_map/all_gather | solution.py:44
  91.9 0.1 copy.14
  92.0 0.1 reshape.36
  92.1 4.8 %convolution_convert_fusion.1 = bf16[32,2560]{1,0:T(8,128)(2,1)S(1)} fusion(bf16[1280,32]{0,1:T(8,128)(2,1)S(1)} %reshape.36, bf16[2560,1280]{1,0:T(8,128)(2,1)} %bitcast.55), kind=kOutput, calls=%fused_computation.11 | convolution fusion | flops 209797120 | bytes 6799360 | tf_op jit(solution)/shard_map/dot_general | solution.py:43
  97.0 1.1 copy.22
  98.1 0.0 reduce-scatter.9.cloned.1.call-start
  98.1 34.6 %reduce-scatter.7.cloned.1.call-done = bf16[320,32]{1,0:T(8,128)(2,1)} async-done(((bf16[2560,32]{1,0:T(8,128)(2,1)}), bf16[320,32]{1,0:T(8,128)(2,1)}) %reduce-scatter.7.cloned.1.call-update) | async-done | bytes 20496
  132.8 1.0 copy.23
  133.7 0.2 fusion.15
  133.9 39.4 %psum.14 = f32[32,32]{0,1:T(8,128)S(1)} all-reduce(f32[32,32]{0,1:T(8,128)S(1)} %fusion.15), channel_id=1, replica_groups=mesh['row'=4,'col'=8] {'row','col'}, use_global_device_ids=true, to_apply=%region_6.7 | all-reduce | flops 1024 | bytes 8192 | tf_op jit(solution)/shard_map/psum | solution.py:54
  173.3 0.1 copy.16
  173.4 2.9 %cholesky.44 = f32[32,32]{1,0:T(8,128)S(1)} custom-call(f32[32,32]{1,0:T(8,128)S(1)} %fusion.26), custom_call_target="Cholesky" | custom-call | tf_op jit(solution)/shard_map/jit(cholesky)/cholesky | solution.py:55
  176.4 0.6 compare_reduce_fusion.1
  177.0 0.7 fusion.21
  177.7 2.4 custom-call.6
  180.1 0.3 fusion.9
  180.4 13.4 %all-gather.1 = bf16[4,320,32]{1,2,0:T(8,128)(2,1)S(1)} all-gather(bf16[1,320,32]{1,2,0:T(8,128)(2,1)S(1)} %fusion.9), channel_id=1, replica_groups=mesh['row'=4,'col'=8] {'row'}, dimensions={0}, use_global_device_ids=true | all-gather | bytes 102400 | tf_op jit(solution)/shard_map/all_gather | solution.py:44
  193.8 0.1 copy.17
  193.8 0.1 reshape.38
  194.0 4.8 %convolution_convert_fusion = bf16[32,2560]{1,0:T(8,128)(2,1)S(1)} fusion(bf16[1280,32]{0,1:T(8,128)(2,1)S(1)} %reshape.38, bf16[2560,1280]{1,0:T(8,128)(2,1)} %bitcast.56), kind=kOutput, calls=%fused_computation.10 | convolution fusion | flops 209797120 | bytes 6799360 | tf_op jit(solution)/shard_map/dot_general | solution.py:43
  198.8 1.1 copy.24
  199.9 35.2 %reduce-scatter.9.cloned.1.call-done = bf16[320,32]{1,0:T(8,128)(2,1)} async-done(((bf16[2560,32]{1,0:T(8,128)(2,1)}), bf16[320,32]{1,0:T(8,128)(2,1)}) %reduce-scatter.9.cloned.1.call-update) | async-done | bytes 20496
  235.2 1.0 copy.25
  236.1 0.2 fusion.14
  236.3 39.4 %psum.15 = f32[32,32]{0,1:T(8,128)S(1)} all-reduce(f32[32,32]{0,1:T(8,128)S(1)} %fusion.14), channel_id=1, replica_groups=mesh['row'=4,'col'=8] {'row','col'}, use_global_device_ids=true, to_apply=%region_10.13 | all-reduce | flops 1024 | bytes 8192 | tf_op jit(solution)/shard_map/psum | solution.py:54
  275.8 0.1 copy.19
  275.8 2.9 %cholesky.55 = f32[32,32]{1,0:T(8,128)S(1)} custom-call(f32[32,32]{1,0:T(8,128)S(1)} %fusion.24), custom_call_target="Cholesky" | custom-call | tf_op jit(solution)/shard_map/jit(cholesky)/cholesky | solution.py:55
  278.8 0.6 compare_reduce_fusion
  279.4 0.7 fusion.22
  280.1 2.4 custom-call.7
  282.5 0.9 fusion.13
  (12 shorter events, 0.1 us)
Async XLA Ops:
  7.2 30.3 %all-gather.4.cloned.1.call-start = ((), (), s32[]{:S(2)}) async-start(), calls=%async_computation.2 | async-start | bytes 1474560 | tf_op jit(solution)/shard_map/all_gather | solution.py:34
  10.0 122.8 %reduce-scatter.7.cloned.1.call-start = ((), (), s32[]{:S(2)}) async-start(), calls=%async_computation.3 | async-start | bytes 737280
  50.6 28.0 %copy-start = (f32[32,320]{1,0:T(8,128)S(1)}, f32[32,320]{1,0:T(8,128)}, u32[]{:S(2)}) copy-start(f32[32,320]{1,0:T(8,128)} %param.8) | copy-start | bytes 122884
  98.1 137.1 %reduce-scatter.9.cloned.1.call-start = ((), (), s32[]{:S(2)}) async-start(), calls=%async_computation.4 | async-start | bytes 737280
Sparse Core Ops, SparseCore 0:
  10.1 27.2 all-gather.3
  98.2 34.5 reduce-scatter.6
  200.0 35.0 reduce-scatter.8
where the time goes:
time: 291 us; the launch traced here: 290 us
  blocking collectives  149 us (51%)
  waiting for transfers between devices  75.6 us (26%)
  matrix products  24.4 us (8%)
  other arithmetic  19.9 us (7%)
  between operations  14.5 us (5%)
  local copies, waits for them, and re-layouts  6.52 us (2%)
    psum x2, blocking collectives, local(): gram = lax.psum(local_gram, ('row', 'col'))  78.8 us
    unnamed x5, waiting for transfers between devices  69.9 us
    all_gather x2, blocking collectives, local(): lax.all_gather(scaled, 'row', axis=1, tiled=True)  26.8 us
    unnamed x1, blocking collectives  23.5 us
    all_gather x1, blocking collectives, local(): col_emb = lax.all_gather(own_unit, 'row', axis=0, tiled=True)  19.8 us
    dot_general x5, matrix products, one_piece(): lax.dot_general(piece, col_emb, (((1,), (1,)), ((), ())), preferred_eleme...  13.1 us
    dot_general x2, matrix products, local(): lax.dot_general(lax.all_gather(scaled, 'row', axis=1, tiled=True), tile,...  9.68 us
    another operation x6, other arithmetic, local(): lower = jnp.linalg.cholesky(gram)  7.19 us
  transfers between devices with their start and end apart: 3, of which 3 were waited for; matrix products, arithmetic and copies ran while one was open for 0% of the time, Pallas kernels for 0%

commit v1 on v0

v1 whole, which is shorter than its diff:
```python
import functools
import math

import jax
import jax.numpy as jnp
from jax import lax
from jax.experimental import pallas as pl
from jax.experimental.pallas import tpu as pltpu
from jax.sharding import PartitionSpec as P

VMEM = pl.BlockSpec(memory_space=pltpu.VMEM)
NT = (((1,), (1,)), ((), ()))
HIGH = lax.Precision.HIGHEST


def lanes(width):
    return -(-width // 128) * 128


def call(kernel, out_shapes, scratch=(), flops=0):
    count = len(out_shapes)
    mib = 1024 * 1024

    def run(*operands):
        needs = sum(math.prod(o.shape) * jnp.dtype(o.dtype).itemsize for o in operands)
        needs += sum(math.prod(s) * jnp.dtype(d).itemsize for s, d in out_shapes)
        limit = min(56 * mib, 2 * needs // mib * mib + 8 * mib)
        return pl.pallas_call(
            kernel,
            out_shape=[jax.ShapeDtypeStruct(s, d) for s, d in out_shapes],
            in_specs=[VMEM] * len(operands),
            out_specs=[VMEM] * count,
            scratch_shapes=list(scratch),
            compiler_params=pltpu.CompilerParams(vmem_limit_bytes=limit),
            cost_estimate=pl.CostEstimate(flops=flops, bytes_accessed=0, transcendentals=0),
        )(*operands)

    return run


def side_by_side(blocks):
    return jnp.concatenate(blocks, axis=1) if len(blocks) > 1 else blocks[0]


def cut(value, width):
    return [value[:, i : i + width] for i in range(0, value.shape[1], width)]


def two_parts(value):
    high = value.astype(jnp.bfloat16)
    return high, (value - high.astype(jnp.float32)).astype(jnp.bfloat16)


def unit_rows(ref, gain):
    values = ref[...].astype(jnp.float32)
    power = jnp.mean(values * values, axis=1, keepdims=True)
    factor = lax.rsqrt(power + 1e-06) * (gain / math.sqrt(ref.shape[1]))
    return (values * factor).astype(jnp.bfloat16)


def own_kernel(emb_ref, start_ref, unit_ref, out_ref):
    unit_ref[...] = unit_rows(emb_ref, 1.0)
    out_ref[...] = start_ref[...].astype(out_ref.dtype)


def affinity(rows_ref, parts, own, fold_ref, more_ref=None):
    def row_block(start):
        piece = rows_ref[pl.ds(start, own), :]
        fold = 0.0 if more_ref is None else more_ref[pl.ds(start, own), :]
        for lanes_ref, first, tile_ref in parts:
            total = tile_ref.shape[1]
            for j in range(0, total, 256):
                stop = min(j + 256, total)
                inner = lax.dot_general(
                    piece, lanes_ref[first + j : first + stop, :], NT,
                    preferred_element_type=jnp.float32,
                )
                values = jnp.exp(inner - 8.0)
                tile_ref[pl.ds(start, own), j:stop] = values.astype(jnp.bfloat16)
                for part in cut(values, 128):
                    gap = 128 - part.shape[1]
                    if gap:
                        part = side_by_side([part, jnp.zeros((own, gap), jnp.float32)])
                    fold = fold + part
        fold_ref[pl.ds(start, own), :] = fold

    count = rows_ref.shape[0] // own
    if count <= 4:
        for i in range(count):
            row_block(i * own)
    else:
        pl.loop(0, count)(lambda i: row_block(pl.multiple_of(i * own, own)))


def unfold(fold):
    ones = jnp.ones((8, fold.shape[1]), jnp.float32)
    sums = lax.dot_general(ones, fold, NT, precision=HIGH, preferred_element_type=jnp.float32)
    return sums[0:1, :]


def main_kernel(rows, unit_ref, *refs):
    row_refs, lane_refs = refs[: rows - 1], refs[rows - 1 : -6]
    rows_ref, even_ref, odd_ref, even_tile_ref, odd_tile_ref, fold_ref = refs[-6:]
    own = unit_ref.shape[0]
    rows_ref[0:own, :] = unit_ref[...] * 8
    even_ref[0:own, :] = unit_ref[...]
    for i, ref in enumerate(row_refs, 1):
        rows_ref[i * own : (i + 1) * own, :] = unit_rows(ref, 8.0)
    half = (len(lane_refs) + 1) // 2
    for i, ref in enumerate(lane_refs, 1):
        target, at = (even_ref, i) if i < half else (odd_ref, i - half)
        target[at * own : (at + 1) * own, :] = unit_rows(ref, 1.0)
    parts = [(even_ref, 0, even_tile_ref), (odd_ref, 0, odd_tile_ref)]
    affinity(rows_ref, parts, own, fold_ref)


def rest_kernel(rows_ref, fold_in_ref, even_in_ref, odd_in_ref, *refs):
    row_ref, even_ref, odd_ref, start_ref = refs[:4]
    side_tile_ref, even_last_ref, odd_last_ref, sums_ref, send_ref = refs[4:9]
    last_ref, even_all, odd_all, side_all, fold_ref, fold_last_ref = refs[9:]
    own = row_ref.shape[0]
    high = even_in_ref.shape[0]
    sides = ((even_in_ref, even_ref, even_all), (odd_in_ref, odd_ref, odd_all))
    for i, (before, fresh, whole) in enumerate(sides):
        unit = unit_rows(fresh, 1.0)
        whole[0:high, :] = before[...]
        whole[high : high + own, :] = unit
        side_all[i * own : (i + 1) * own, :] = unit
    affinity(rows_ref, [(side_all, 0, side_tile_ref)], own, fold_ref, fold_in_ref)
    last_ref[...] = unit_rows(row_ref, 8.0)
    parts = [(even_all, 0, even_last_ref), (odd_all, 0, odd_last_ref)]
    affinity(last_ref, parts, own, fold_last_ref)
    lines = cut(unfold(fold_ref[...]), own) + [unfold(fold_last_ref[...])]
    sums = jnp.concatenate(lines, axis=0)
    sums_ref[...] = sums
    parts = [start_ref[...].astype(jnp.float32)]
    parts += [part.astype(jnp.float32) for part in two_parts(sums)]
    space = send_ref.shape[0] - sum(p.shape[0] for p in parts)
    if space:
        parts.append(jnp.zeros((space, own), jnp.float32))
    send_ref[...] = jnp.concatenate(parts, axis=0).astype(jnp.bfloat16)


def side_span(odd, own):
    low = own // 128 * 128 if odd else 0
    return low, (2 * own if odd else lanes(own)), odd * own - low


def lane_products(left, last, tiles, odd, own):
    main_ref, side_ref, last_ref = tiles

    def product(value, ref, low, high):
        return side_by_side(
            [
                jnp.dot(value, ref[:, i : min(i + 256, high)], preferred_element_type=jnp.float32)
                for i in range(low, high, 256)
            ]
        )

    low, high, at = side_span(odd, own)
    blocks = cut(product(left, main_ref, 0, main_ref.shape[1]), own)
    blocks.append(product(left, side_ref, low, high)[:, at : at + own])
    more = cut(product(last, last_ref, 0, last_ref.shape[1]), own)
    return [x + y for x, y in zip(blocks, more)]


def with_tail(block, tail, width):
    space = width - block.shape[1] - tail.shape[1]
    parts = [block, tail]
    if space:
        parts.append(jnp.zeros((block.shape[0], space), jnp.float32))
    return side_by_side(parts)


def gram_tail(gram):
    return side_by_side([p.astype(jnp.float32) for p in two_parts(gram)])


def gram_of(piece, own):
    count = piece.shape[0]
    return piece[:, own : own + count] + piece[:, own + count : own + 2 * count]


def scale_tail(scale, count, space):
    lines = []
    for part in two_parts(scale):
        for piece in cut(part.astype(jnp.float32), space):
            gap = space - piece.shape[1]
            lines.append(side_by_side([piece, jnp.zeros((1, gap), jnp.float32)]) if gap else piece)
    lines.append(jnp.zeros((count - len(lines), space), jnp.float32))
    return jnp.concatenate(lines, axis=0)


def scale_of(tail, own):
    lines = -(-own // tail.shape[1])
    parts = [
        side_by_side([tail[k + i : k + i + 1] for i in range(lines)])[:, :own]
        for k in (0, lines)
    ]
    return parts[0] + parts[1]


def first_kernel(*refs):
    tiles, refs = refs[:3], refs[3:]
    sums_ref, start_ref, came_refs = refs[0], refs[1], refs[2:-5]
    pieces_ref, left_ref, left_last_ref, degrees_ref, scale_ref = refs[-5:]
    count, own = start_ref.shape
    rows = sums_ref.shape[0]
    sums, starts = [sums_ref[...]], [start_ref[...].astype(jnp.float32)]
    for ref in came_refs:
        came = ref[...].astype(jnp.float32)
        starts.append(came[:count])
        high, low = (came[count + i * rows : count + (i + 1) * rows] for i in range(2))
        sums.append(high + low)
    degrees = []
    for j in range(rows):
        degrees.append(sum(s[j ^ m : (j ^ m) + 1, :] for m, s in enumerate(sums)))
    degrees_ref[...] = degrees[0]
    scales = [1.0 / jnp.sqrt(d) for d in degrees]
    scale_ref[...] = scales[0]
    scaled = [(start * scale).astype(jnp.bfloat16) for start, scale in zip(starts, scales)]
    left_ref[...] = side_by_side(scaled[:-1])
    left_last_ref[...] = scaled[-1]
    blocks = lane_products(left_ref[...], left_last_ref[...], tiles, 1, own)
    for i, block in enumerate(blocks):
        pieces_ref[i] = block.astype(jnp.bfloat16)


def same_kernel(*refs):
    tiles, (left_ref, left_last_ref, pieces_ref) = refs[:3], refs[3:]
    blocks = lane_products(left_ref[...], left_last_ref[...], tiles, 0, pieces_ref.shape[2])
    for i, block in enumerate(blocks):
        pieces_ref[i] = block


def join_kernel(pieces_ref, other_ref, scale_ref, out_ref):
    blocks = [pieces_ref[i] + other_ref[i].astype(jnp.float32) for i in range(pieces_ref.shape[0])]
    space = out_ref.shape[1] - len(blocks) * blocks[0].shape[1]
    blocks.append(scale_tail(scale_ref[...], blocks[0].shape[0], space))
    out_ref[...] = side_by_side(blocks).astype(out_ref.dtype)


def lanes_image_kernel(own, *refs):
    parts_refs, out_ref = refs[:-1], refs[-1]
    half = len(parts_refs)
    count = parts_refs[0].shape[0]
    total, scales = [0.0] * half, [None] * half
    for m, ref in enumerate(parts_refs):
        part = ref[...].astype(jnp.float32)
        blocks = cut(part[:, : half * own], own)
        for j in range(half):
            total[j] = total[j] + blocks[j ^ m]
        scales[m] = scale_of(part[:, half * own :], own)
    gram, scaled = 0.0, []
    for j in range(half):
        image = total[j] * scales[j]
        gram = gram + lax.dot_general(
            image, image, NT, precision=HIGH, preferred_element_type=jnp.float32
        )
        scaled.append(image * scales[j])
    tail = gram_tail(gram)
    for j in range(half):
        high, low = two_parts(scaled[j])
        here = tail if j == 0 else jnp.zeros_like(tail)
        whole = with_tail(high.astype(jnp.float32), here, out_ref.shape[2])
        out_ref[j, 0:count, :] = whole.astype(jnp.bfloat16)
        whole = with_tail(low.astype(jnp.float32), jnp.zeros_like(tail), out_ref.shape[2])
        out_ref[j, count : 2 * count, :] = whole.astype(jnp.bfloat16)


def row_products(image_ref, tiles, odd, own):
    main_ref, side_ref, last_ref = tiles
    count = image_ref.shape[1] // 2
    lefts = [image_ref[i, :, 0:own] for i in range(image_ref.shape[0])]
    low, high, at = side_span(odd, own)
    padded = [lefts[-1]]
    for gap, place in ((at, 0), (high - low - at - own, len(padded) + 1)):
        if gap:
            padded.insert(place, jnp.zeros((2 * count, gap), jnp.bfloat16))
    main, whole = side_by_side(lefts[:-1]), side_by_side(lefts)
    values = []
    for pairs in (
        ((main, main_ref, 0, main.shape[1]), (side_by_side(padded), side_ref, low, high)),
        ((whole, last_ref, 0, whole.shape[1]),),
    ):
        total = pairs[0][1].shape[0]
        for i in range(0, total, 256):
            value = sum(
                lax.dot_general(
                    left, ref[i : min(i + 256, total), start:stop], NT,
                    preferred_element_type=jnp.float32,
                )
                for left, ref, start, stop in pairs
            )
            values.append(value[:count] + value[count:])
    return side_by_side(values)


def own_lanes_kernel(own, *refs):
    tiles, (image_ref, out_ref) = refs[:3], refs[3:]
    out_ref[...] = row_products(image_ref, tiles, 0, own)


def other_lanes_kernel(own, *refs):
    tiles, (own_image_ref, image_ref, line_ref), out_refs = refs[:3], refs[3:6], refs[6:]
    count = line_ref.shape[0]
    value = line_ref[...] + row_products(image_ref, tiles, 1, own)
    gram = 0.0
    for ref in (own_image_ref, image_ref):
        gram = gram + gram_of(ref[0, 0:count, :].astype(jnp.float32), own)
    tail = gram_tail(gram)
    for block, ref in zip(cut(value, own), out_refs):
        ref[...] = with_tail(block, tail, ref.shape[1]).astype(ref.dtype)


def eliminate(both, width, block=8):
    count, total = both.shape
    block = math.gcd(count, block)
    repeat = total // 128
    ids = lax.broadcasted_iota(jnp.int32, (count, 128), 0)
    roots = jnp.zeros((count, 128), jnp.float32)

    def wide(value):
        return side_by_side([value] * repeat)

    def down(value):
        return jnp.concatenate([value] * (count // 8), axis=0)

    for k in range(0, count, block):
        columns = [
            jnp.broadcast_to(both[:, width + k + t : width + k + t + 1], (count, 128))
            for t in range(block)
        ]
        corner = {
            (s, t): jnp.broadcast_to(columns[t][k + s : k + s + 1, :], (8, 128))
            for t in range(block)
            for s in range(t, block)
        }
        lines = [
            jnp.broadcast_to(both[k + t : k + t + 1, :], (8, total)) for t in range(block)
        ]
        for t in range(block):
            pivot = corner[t, t]
            inverse = 1.0 / pivot
            roots = jnp.where(ids == k + t, down(1.0 / jnp.sqrt(pivot)), roots)
            lower = {s: corner[s, t] * inverse for s in range(t + 1, block)}
            factor = columns[t] * down(inverse)
            for u in range(t + 1, block):
                columns[u] = columns[u] - factor * down(corner[u, t])
                lines[u] = lines[u] - wide(lower[u]) * lines[t]
                for s in range(u, block):
                    corner[s, u] = corner[s, u] - lower[s] * corner[u, t]
            factor = jnp.where(ids > k + t, factor, 0.0)
            both = both - wide(factor) * down(lines[t])
    return both * wide(roots)


def pack_square(square):
    count = square.shape[0]
    fold = max(1, min(count // 8, 128 // count))
    high = count // fold
    return jnp.concatenate([square[i * high : (i + 1) * high] for i in range(fold)], axis=1)


def unpack_square(packed, count):
    high = packed.shape[0]
    fold = count // high
    return jnp.concatenate(
        [packed[:, i * count : (i + 1) * count] for i in range(fold)], axis=0
    )


def image_kernel(*refs):
    pieces_refs, (scale_ref, image_ref, gram_ref, grams_ref) = refs[:-4], refs[-4:]
    width = scale_ref.shape[1]
    both = sum(ref[...].astype(jnp.float32) for ref in pieces_refs)
    gram_ref[...] = gram_of(both, width)
    image = both[:, :width] * scale_ref[...]
    image_ref[...] = image
    gram = lax.dot_general(image, image, NT, precision=HIGH, preferred_element_type=jnp.float32)
    packed = pack_square(gram)
    for i in range(grams_ref.shape[0]):
        grams_ref[i] = packed


def filled(parts):
    width = sum(p.shape[1] for p in parts)
    space = lanes(width) - width
    if space:
        parts = parts + [jnp.zeros((parts[0].shape[0], space), jnp.float32)]
    return side_by_side(parts)


def middle_kernel(image_ref, gram_ref, out_ref, inverse_ref):
    count, own = image_ref.shape
    rows = lax.broadcasted_iota(jnp.int32, (count, count), 0)
    unit = (rows == lax.broadcasted_iota(jnp.int32, (count, count), 1)).astype(jnp.float32)
    whole = eliminate(filled([image_ref[...], gram_ref[...], unit]), own)
    out_ref[...] = whole[:, :own]
    inverse_ref[...] = whole[:, own + count : own + 2 * count]


def last_kernel(image_ref, inverse_ref, grams_ref, out_ref):
    count, own = image_ref.shape
    inverse = inverse_ref[...]
    gram = unpack_square(jnp.sum(grams_ref[...], axis=0), count)
    gram = jnp.dot(inverse, gram, precision=HIGH, preferred_element_type=jnp.float32)
    gram = lax.dot_general(gram, inverse, NT, precision=HIGH, preferred_element_type=jnp.float32)
    out_ref[...] = eliminate(filled([image_ref[...], gram]), own)[:, :own]


NAMES = ("row_high", "row_low", "col_high", "col_mid", "core")
ROW_SET, LANE_SET = ("row_high", "col_mid"), ("row_low", "col_high", "core")


def swap(value, axes, offset):
    size = lax.axis_size(axes)
    return lax.ppermute(value, axes, [(i, i ^ offset) for i in range(size)])


def local(embeddings, start_vectors):
    rows, cols = lax.axis_size(ROW_SET), lax.axis_size(LANE_SET)
    own, width = embeddings.shape
    count = start_vectors.shape[0]
    f32, bf16 = jnp.float32, jnp.bfloat16
    half = cols // 2
    even = [*range(0, cols, 2)]
    padded = lanes(own + 1)

    unit, starts = call(own_kernel, [((own, width), bf16), ((count, own), bf16)])(
        embeddings, start_vectors
    )
    row_blocks, lane_blocks = {0: embeddings}, {0: embeddings}
    tops = [m for m in range(1, rows) if m.bit_count() == 1]
    bits = [1 << i for i in range(cols.bit_length() - 2, -1, -1)]
    for m in bits:
        lane_blocks[m] = swap(embeddings, LANE_SET, m)
    unit, lane_blocks[bits[0]] = lax.optimization_barrier((unit, lane_blocks[bits[0]]))
    for m in even:
        if m.bit_count() > 1:
            lane_blocks[m] = swap(lane_blocks[m & (m - 1)], LANE_SET, m & -m)
    first = [(lane_blocks, m, lane_blocks[m]) for m in bits[:0:-1]]
    first += [(row_blocks, m, swap(embeddings, ROW_SET, m)) for m in tops]
    blocks, unit, starts = lax.optimization_barrier(([f[2] for f in first], unit, starts))
    for (where, m, _), block in zip(first, blocks):
        where[m] = block
    for m in even[1:-1]:
        lane_blocks[m + 1] = swap(lane_blocks[m], LANE_SET, 1)
    for m in range(rows):
        if m.bit_count() > 1:
            row_blocks[m] = swap(row_blocks[m & (m - 1)], ROW_SET, m & -m)

    high, deep = (rows - 1) * own, (half - 1) * own
    unit, farthest = lax.optimization_barrier((unit, lane_blocks[even[-1]]))
    main_rows, even_lanes, odd_lanes, even_main, odd_main, fold = call(
        functools.partial(main_kernel, rows - 1),
        [
            ((high, width), bf16),
            ((deep, width), bf16),
            ((deep, width), bf16),
            ((high, deep), bf16),
            ((high, deep), bf16),
            ((high, 128), f32),
        ],
        flops=4 * high * deep * width,
    )(
        unit,
        *[row_blocks[m] for m in range(1, rows - 1)],
        *[lane_blocks[m] for m in even[1:-1]],
        *[lane_blocks[m + 1] for m in even[:-1]],
    )
    lines = count + -(-2 * rows // 8) * 8
    side, even_last, odd_last, sums, send = call(
        rest_kernel,
        [
            ((high, 2 * own), bf16),
            ((own, half * own), bf16),
            ((own, half * own), bf16),
            ((rows, own), f32),
            ((lines, own), bf16),
        ],
        [
            pltpu.VMEM((own, width), bf16),
            pltpu.VMEM((half * own, width), bf16),
            pltpu.VMEM((half * own, width), bf16),
            pltpu.VMEM((2 * own, width), bf16),
            pltpu.VMEM((high, 128), f32),
            pltpu.VMEM((own, 128), f32),
        ],
        flops=4 * (high + half * own) * own * width,
    )(
        main_rows,
        fold,
        even_lanes,
        odd_lanes,
        row_blocks[rows - 1],
        farthest,
        swap(farthest, LANE_SET, 1),
        starts,
    )
    even_tiles = (even_main, side, even_last)
    odd_tiles = (odd_main, side, odd_last)

    came = [swap(send, ROW_SET, m) for m in range(1, rows)]
    other, left, left_last, degrees, scale = call(
        first_kernel,
        [
            ((half, count, own), bf16),
            ((count, high), bf16),
            ((count, own), bf16),
            ((1, own), f32),
            ((1, own), f32),
        ],
    )(*odd_tiles, sums, starts, *came)
    other = swap(other, LANE_SET, 1)
    (pieces,) = call(
        same_kernel,
        [((half, count, own), f32)],
        flops=2 * count * rows * half * own * own,
    )(*even_tiles, left, left_last)
    (parts,) = call(join_kernel, [((count, lanes(half * own + 128)), bf16)])(pieces, other, scale)
    parts = [parts] + [swap(parts, LANE_SET, m) for m in even[1:]]

    (image,) = call(functools.partial(lanes_image_kernel, own), [((half, 2 * count, padded), bf16)])(*parts)
    other = swap(image, LANE_SET, 1)
    (value,) = call(
        functools.partial(own_lanes_kernel, own),
        [((count, rows * own), f32)],
        flops=4 * count * rows * half * own * own,
    )(*even_tiles, image)
    wide = lanes(own + 2 * count)
    pieces = call(
        functools.partial(other_lanes_kernel, own),
        [((count, wide), f32 if m == 0 else bf16) for m in range(rows)],
    )(*odd_tiles, image, other, value)
    moved = [swap(pieces[m], ROW_SET, m) for m in range(rows - 1, 0, -1)]
    fold = max(1, min(count // 8, 128 // count))
    image, gram, grams = call(
        image_kernel,
        [
            ((count, own), f32),
            ((count, count), f32),
            ((rows * cols, count // fold, count * fold), f32),
        ],
    )(pieces[0], *moved, scale)
    grams = lax.all_to_all(grams, NAMES, 0, 0, tiled=True)
    image, inverse = call(middle_kernel, [((count, own), f32), ((count, count), f32)])(image, gram)
    (vectors,) = call(last_kernel, [((count, own), f32)])(image, inverse, grams)
    return (vectors, degrees.reshape(own))


def solution(mesh):
    row_size, col_size = mesh.shape["row"], mesh.shape["col"]
    devices = mesh.devices.reshape(row_size // 2, 2, 2, col_size // 4, 2)
    return jax.shard_map(
        local,
        mesh=jax.sharding.Mesh(devices, NAMES),
        in_specs=(P(NAMES, None), P(None, NAMES)),
        out_specs=(P(None, NAMES), P(NAMES)),
        check_vma=False,
    )
```

time: 291 us -> 66.7 us (0.23)
  blocking collectives: 149 us -> 0 us
  waiting for transfers between devices: 75.6 us -> 21 us
  starting transfers between devices: 0.12 us -> 29.7 us
  matrix products: 24.4 us -> 0 us
  other arithmetic: 19.9 us -> 0.6 us
  between operations: 14.5 us -> 0.72 us
  Pallas kernels: 0 us -> 12.7 us
  local copies, waits for them, and re-layouts: 6.52 us -> 1.74 us
    psum x2 -> x0, blocking collectives: 78.8 us -> none  [local(): gram = lax.psum(local_gram, ('row', 'col'))]
    unnamed x5 -> x0, waiting for transfers between devices: 69.9 us -> none
    all_gather x3 -> x0, blocking collectives: 46.6 us -> none  [the longest x2 26.8 us: local(): lax.all_gather(scaled, 'row', axis=1, tiled=True)]
    ppermute x0 -> x21, starting transfers between devices: none -> 25.2 us  [swap(): return lax.ppermute(value, axes, [(i, i ^ offset) for i in range(size)])]
    unnamed x1 -> x0, blocking collectives: 23.5 us -> none
    dot_general x9 -> x0, matrix products: 23.2 us -> none  [the longest x5 13.1 us: one_piece(): lax.dot_general(piece, col_emb, (((1,), (1,)), ((), ())), preferred_eleme...]
    ppermute x0 -> x21, waiting for transfers between devices: none -> 14.5 us  [swap(): return lax.ppermute(value, axes, [(i, i ^ offset) for i in range(size)])]
    another operation x10 -> x0, other arithmetic: 13.4 us -> none  [the longest x6 7.19 us: local(): lower = jnp.linalg.cholesky(gram)]
  transfers between devices with their start and end apart: 3 -> 22, of which waited for: 3 -> 16; matrix products, arithmetic and copies ran while one was open for 0% -> 1% of each run, Pallas kernels for 0% -> 8%
where the time goes in v1:
time: 66.7 us; the launch traced here: 66.5 us
  starting transfers between devices  29.7 us (45%)
  waiting for transfers between devices  21 us (31%)
  Pallas kernels  12.7 us (19%)
  local copies, waits for them, and re-layouts  1.74 us (3%)
  between operations  0.72 us (1%)
    ppermute x21, starting transfers between devices, swap(): return lax.ppermute(value, axes, [(i, i ^ offset) for i in range(size)])  25.2 us
    ppermute x21, waiting for transfers between devices, swap(): return lax.ppermute(value, axes, [(i, i ^ offset) for i in range(size)])  14.5 us
    pallas_call x12, Pallas kernels, run(): pl.pallas_call(kernel, out_shape=[jax.ShapeDtypeStruct(s, d) for s, d in...  12.7 us
    all_to_all x1, waiting for transfers between devices, local(): grams = lax.all_to_all(grams, NAMES, 0, 0, tiled=True)  6.55 us
    all_to_all x1, starting transfers between devices, local(): grams = lax.all_to_all(grams, NAMES, 0, 0, tiled=True)  4.51 us
    unnamed x4, local copies, waits for them, and re-layouts  1.74 us
  transfers between devices with their start and end apart: 22, of which 16 were waited for; matrix products, arithmetic and copies ran while one was open for 1% of the time, Pallas kernels for 8%

profile of v1, /device:TPU:0, one launch (start us, length us, event | category | flops | bytes accessed | tf_op | source)
XLA Modules:
  0.0 66.5 jit_solution(5173867953146012345)
XLA Ops:
  0.6 3.1 %collective-permute-start.4 = (bf16[320,256]{1,0:T(8,128)(2,1)}, bf16[320,256]{1,0:T(8,128)(2,1)S(1)}, u32[]{:S(2)}, u32[]{:S(2)}) collective-permute-start(bf16[320,256]{1,0:T(8,128)(2,1)} %emb_ref.1), channel_id=1, source_target_pairs={{0,8},{1,9},{4,12},{5,13},{8,0},{9,1},{12,4},{13,5},{2,10},{3,11},... | collective-permute-start | bytes 491528 | tf_op jit(solution)/shard_map/ppermute | solution.py:418
  3.7 2.6 %collective-permute-start.3 = (bf16[320,256]{1,0:T(8,128)(2,1)}, bf16[320,256]{1,0:T(8,128)(2,1)S(1)}, u32[]{:S(2)}, u32[]{:S(2)}) collective-permute-start(bf16[320,256]{1,0:T(8,128)(2,1)} %emb_ref.1), channel_id=1, source_target_pairs={{0,16},{2,18},{16,0},{18,2},{1,17},{3,19},{17,1},{19,3},{4,20},{6,... | collective-permute-start | bytes 491528 | tf_op jit(solution)/shard_map/ppermute | solution.py:418
  6.3 1.5 %collective-permute-start.2 = (bf16[320,256]{1,0:T(8,128)(2,1)}, bf16[320,256]{1,0:T(8,128)(2,1)S(1)}, u32[]{:S(2)}, u32[]{:S(2)}) collective-permute-start(bf16[320,256]{1,0:T(8,128)(2,1)} %emb_ref.1), channel_id=1, source_target_pairs={{0,2},{2,0},{16,18},{18,16},{1,3},{3,1},{17,19},{19,17},{4,6},{6,4... | collective-permute-start | bytes 491528 | tf_op jit(solution)/shard_map/ppermute | solution.py:418
  7.8 1.5 %collective-permute-start.1 = (bf16[320,256]{1,0:T(8,128)(2,1)}, bf16[320,256]{1,0:T(8,128)(2,1)S(1)}, u32[]{:S(2)}, u32[]{:S(2)}) collective-permute-start(bf16[320,256]{1,0:T(8,128)(2,1)} %emb_ref.1), channel_id=1, source_target_pairs={{0,4},{1,5},{4,0},{5,1},{8,12},{9,13},{12,8},{13,9},{2,6},{3,7},{6... | collective-permute-start | bytes 491528 | tf_op jit(solution)/shard_map/ppermute | solution.py:418
  9.3 0.9 %copy-done = bf16[320,256]{1,0:T(8,128)(2,1)S(1)} copy-done((bf16[320,256]{1,0:T(8,128)(2,1)S(1)}, bf16[320,256]{1,0:T(8,128)(2,1)}, u32[]{:S(2)}) %copy-start) | copy-done | bytes 163864
  10.3 0.8 %copy-done.1 = f32[32,320]{1,0:T(8,128)S(1)} copy-done((f32[32,320]{1,0:T(8,128)S(1)}, f32[32,320]{1,0:T(8,128)}, u32[]{:S(2)}) %copy-start.1) | copy-done | bytes 40984
  11.1 0.1 shard_map.41
  11.2 0.1 collective-permute-done.4.refs_3_
  11.3 1.8 %collective-permute-start.5 = (bf16[320,256]{1,0:T(8,128)(2,1)S(1)}, bf16[320,256]{1,0:T(8,128)(2,1)S(1)}, u32[]{:S(2)}, u32[]{:S(2)}) collective-permute-start(bf16[320,256]{1,0:T(8,128)(2,1)S(1)} %collective-permute-done.4.refs_3_), channel_id=1, source_target_pairs={{0,4},{1,5},{4,0},{5,1},{8,12},{9,13},{12,8},{13,9},{2,6},{3,7},{6... | collective-permute-start | bytes 491528 | tf_op jit(solution)/shard_map/ppermute | solution.py:418
  13.2 0.9 %collective-permute-done.3.refs_1_ = bf16[320,256]{1,0:T(8,128)(2,1)S(1)} collective-permute-done((bf16[320,256]{1,0:T(8,128)(2,1)}, bf16[320,256]{1,0:T(8,128)(2,1)S(1)}, u32[]{:S(2)}, u32[]{:S(2)}) %collective-permute-start.3) | collective-permute-done | bytes 163872 | tf_op jit(solution)/shard_map/ppermute | solution.py:418
  14.1 0.1 collective-permute-start.6
  14.2 0.5 collective-permute-start.7
  14.7 1.5 %collective-permute-start.8 = (bf16[320,256]{1,0:T(8,128)(2,1)S(1)}, bf16[320,256]{1,0:T(8,128)(2,1)S(1)}, u32[]{:S(2)}, u32[]{:S(2)}) collective-permute-start(bf16[320,256]{1,0:T(8,128)(2,1)S(1)} %collective-permute-done.3.refs_1_), channel_id=1, source_target_pairs={{0,2},{2,0},{16,18},{18,16},{1,3},{3,1},{17,19},{19,17},{4,6},{6,4... | collective-permute-start | bytes 491528 | tf_op jit(solution)/shard_map/ppermute | solution.py:418
  16.1 1.7 %collective-permute-done.5.refs_1_ = bf16[320,256]{1,0:T(8,128)(2,1)S(1)} collective-permute-done((bf16[320,256]{1,0:T(8,128)(2,1)S(1)}, bf16[320,256]{1,0:T(8,128)(2,1)S(1)}, u32[]{:S(2)}, u32[]{:S(2)}) %collective-permute-start.5) | collective-permute-done | bytes 163872 | tf_op jit(solution)/shard_map/ppermute | solution.py:418
  17.9 1.8 %shard_map.42 = (bf16[960,256]{1,0:T(8,128)(2,1)S(1)}, bf16[960,256]{1,0:T(8,128)(2,1)S(1)}, bf16[960,256]{1,0:T(8,128)(2,1)S(1)}, bf16[960,960]{1,0:T(8,128)(2,...) custom-call(bf16[320,256]{1,0:T(8,128)(2,1)S(1)} %get-tuple-element.44.unit_ref, ...), custom_call_target="tpu_custom_call" | custom-call | flops 943718400 | tf_op jit(solution)/shard_map/pallas_call | solution.py:28
  19.7 1.1 %collective-permute-done.8.refs_0_ = bf16[320,256]{1,0:T(8,128)(2,1)S(1)} collective-permute-done((bf16[320,256]{1,0:T(8,128)(2,1)S(1)}, bf16[320,256]{1,0:T(8,128)(2,1)S(1)}, u32[]{:S(2)}, u32[]{:S(2)}) %collective-permute-start.8) | collective-permute-done | bytes 163872 | tf_op jit(solution)/shard_map/ppermute | solution.py:418
  20.8 1.9 %shard_map.43 = (bf16[960,640]{1,0:T(8,128)(2,1)S(1)}, bf16[320,1280]{1,0:T(8,128)(2,1)S(1)}, bf16[320,1280]{1,0:T(8,128)(2,1)S(1)}, f32[4,320]{1,0:T(4,128)S(1)}, bf16[40,320]{1,0:T(8,128)(2,1)S(1)}) custom-call(bf16[960,256]{1,0:T(8,128)(2,1)S(1)} %get-tuple-element.50.rows_ref, f32[960,128]{1,0:T(8,128)S(1)} %get-tuple-element.51.fold_in_ref, ...), custom_call_target="tpu_custom_call" | custom-call | flops 734003200 | tf_op jit(solution)/shard_map/pallas_call | solution.py:28
  22.7 1.3 %collective-permute-start.12 = (bf16[40,320]{1,0:T(8,128)(2,1)S(1)}, bf16[40,320]{1,0:T(8,128)(2,1)S(1)}, u32[]{:S(2)}, u32[]{:S(2)}) collective-permute-start(bf16[40,320]{1,0:T(8,128)(2,1)S(1)} %get-tuple-element.61), channel_id=1, source_target_pairs={{0,18},{2,16},{16,2},{18,0},{1,19},{3,17},{17,3},{19,1},{4,22},{6,... | collective-permute-start | bytes 76808 | tf_op jit(solution)/shard_map/ppermute | solution.py:418
  24.0 2.6 %collective-permute-start.11 = (bf16[40,320]{1,0:T(8,128)(2,1)S(1)}, bf16[40,320]{1,0:T(8,128)(2,1)S(1)}, u32[]{:S(2)}, u32[]{:S(2)}) collective-permute-start(bf16[40,320]{1,0:T(8,128)(2,1)S(1)} %get-tuple-element.61), channel_id=1, source_target_pairs={{0,16},{2,18},{16,0},{18,2},{1,17},{3,19},{17,1},{19,3},{4,20},{6,... | collective-permute-start | bytes 76808 | tf_op jit(solution)/shard_map/ppermute | solution.py:418
  26.6 0.5 collective-permute-start.10
  27.1 1.8 %collective-permute-done.12.refs_7_ = bf16[40,320]{1,0:T(8,128)(2,1)S(1)} collective-permute-done((bf16[40,320]{1,0:T(8,128)(2,1)S(1)}, bf16[40,320]{1,0:T(8,128)(2,1)S(1)}, u32[]{:S(2)}, u32[]{:S(2)}) %collective-permute-start.12) | collective-permute-done | bytes 25632 | tf_op jit(solution)/shard_map/ppermute | solution.py:418
  29.0 0.4 collective-permute-done.11.refs_6_
  29.3 1.2 %collective-permute-done.10.refs_5_ = bf16[40,320]{1,0:T(8,128)(2,1)S(1)} collective-permute-done((bf16[40,320]{1,0:T(8,128)(2,1)S(1)}, bf16[40,320]{1,0:T(8,128)(2,1)S(1)}, u32[]{:S(2)}, u32[]{:S(2)}) %collective-permute-start.10) | collective-permute-done | bytes 25632 | tf_op jit(solution)/shard_map/ppermute | solution.py:418
  30.5 0.8 %shard_map.44 = (bf16[4,32,320]{2,1,0:T(8,128)(2,1)S(1)}, bf16[32,960]{1,0:T(8,128)(2,1)S(1)}, bf16[32,320]{1,0:T(8,128)(2,1)S(1)}, f32[1,320]{1,0:T(1,128)S(1)}, f32[1,320]{1,0:T(1,128)S(1)}) custom-call(bf16[960,960]{1,0:T(8,128)(2,1)S(1)} %get-tuple-element.49.refs_0_, bf16[960,640]{1,0:T(8,128)(2,1)S(1)} %get-tuple-element.56.refs_1_, ...), custom_call_target="tpu_custom_call" | custom-call | tf_op jit(solution)/shard_map/pallas_call | solution.py:28
  31.4 0.8 %shard_map.45.pieces_ref = f32[4,32,320]{2,1,0:T(8,128)S(1)} custom-call(bf16[960,960]{1,0:T(8,128)(2,1)S(1)} %get-tuple-element.58.refs_0_, bf16[960,640]{1,0:T(8,128)(2,1)S(1)} %get-tuple-element.56.refs_1_, bf16[320,1280]{1,0:T(8,128)(2,1)S(1)} %get-tuple-element.59.refs_2_, bf16[32,960]{1,0:T(8,128)(2,1)S(1)} %get-tuple-element.62.refs_3_, ...), custom_call_target="tpu_custom_call" | custom-call | flops 104857600 | tf_op jit(solution)/shard_map/pallas_call | solution.py:28
  32.1 0.5 collective-permute-done.13.other_ref
  32.6 0.1 shard_map.46.refs_0_
  32.7 2.0 %collective-permute-start.16 = (bf16[32,1408]{1,0:T(8,128)(2,1)S(1)}, bf16[32,1408]{1,0:T(8,128)(2,1)S(1)}, u32[]{:S(2)}, u32[]{:S(2)}) collective-permute-start(bf16[32,1408]{1,0:T(8,128)(2,1)S(1)} %shard_map.46.refs_0_), channel_id=1, source_target_pairs={{0,12},{1,13},{4,8},{5,9},{8,4},{9,5},{12,0},{13,1},{2,14},{3,15},... | collective-permute-start | bytes 270344 | tf_op jit(solution)/shard_map/ppermute | solution.py:418
  34.8 1.0 %collective-permute-start.15 = (bf16[32,1408]{1,0:T(8,128)(2,1)S(1)}, bf16[32,1408]{1,0:T(8,128)(2,1)S(1)}, u32[]{:S(2)}, u32[]{:S(2)}) collective-permute-start(bf16[32,1408]{1,0:T(8,128)(2,1)S(1)} %shard_map.46.refs_0_), channel_id=1, source_target_pairs={{0,8},{1,9},{4,12},{5,13},{8,0},{9,1},{12,4},{13,5},{2,10},{3,11},... | collective-permute-start | bytes 270344 | tf_op jit(solution)/shard_map/ppermute | solution.py:418
  35.8 0.5 collective-permute-start.14
  36.3 2.9 %collective-permute-done.16.refs_3_ = bf16[32,1408]{1,0:T(8,128)(2,1)S(1)} collective-permute-done((bf16[32,1408]{1,0:T(8,128)(2,1)S(1)}, bf16[32,1408]{1,0:T(8,128)(2,1)S(1)}, u32[]{:S(2)}, u32[]{:S(2)}) %collective-permute-start.16) | collective-permute-done | bytes 90144 | tf_op jit(solution)/shard_map/ppermute | solution.py:418
  39.2 1.2 %collective-permute-done.15.refs_2_ = bf16[32,1408]{1,0:T(8,128)(2,1)S(1)} collective-permute-done((bf16[32,1408]{1,0:T(8,128)(2,1)S(1)}, bf16[32,1408]{1,0:T(8,128)(2,1)S(1)}, u32[]{:S(2)}, u32[]{:S(2)}) %collective-permute-start.15) | collective-permute-done | bytes 90144 | tf_op jit(solution)/shard_map/ppermute | solution.py:418
  40.4 0.1 collective-permute-done.14.refs_1_
  40.5 0.7 shard_map.47.refs_3_
  41.2 1.2 %shard_map.48.refs_5_ = f32[32,1280]{1,0:T(8,128)S(1)} custom-call(bf16[960,960]{1,0:T(8,128)(2,1)S(1)} %get-tuple-element.58.refs_0_, bf16[960,640]{1,0:T(8,128)(2,1)S(1)} %get-tuple-element.56.refs_1_, bf16[320,1280]{1,0:T(8,128)(2,1)S(1)} %get-tuple-element.59.refs_2_, bf16[4,64,384]{2,1,0:T(8,128)(2,1)S(1)} %shard_map.47.refs_3_), custom_call_target="tpu_custom_call" | custom-call | flops 209715200 | tf_op jit(solution)/shard_map/pallas_call | solution.py:28
  42.5 0.2 collective-permute-done.17.refs_4_
  42.7 1.3 %shard_map.49 = (f32[32,384]{1,0:T(8,128)S(1)}, bf16[32,384]{1,0:T(8,128)(2,1)S(1)}, bf16[32,384]{1,0:T(8,128)(2,1)S(1)}, bf16[32,384]{1,0:T(8,128)(2,1)S(1)}) custom-call(bf16[960,960]{1,0:T(8,128)(2,1)S(1)} %get-tuple-element.49.refs_0_, bf16[960,640]{1,0:T(8,128)(2,1)S(1)} %get-tuple-element.56.refs_1_, bf16[320,1280]{1,0:T(8,128)(2,1)S(1)} %get-tuple-element.57.refs_2_, ...), custom_call_target="tpu_custom_call" | custom-call | tf_op jit(solution)/shard_map/pallas_call | solution.py:28
  44.0 1.2 %collective-permute-start.18 = (bf16[32,384]{1,0:T(8,128)(2,1)S(1)}, bf16[32,384]{1,0:T(8,128)(2,1)S(1)}, u32[]{:S(2)}, u32[]{:S(2)}) collective-permute-start(bf16[32,384]{1,0:T(8,128)(2,1)S(1)} %get-tuple-element.67), channel_id=1, source_target_pairs={{0,18},{2,16},{16,2},{18,0},{1,19},{3,17},{17,3},{19,1},{4,22},{6,... | collective-permute-start | bytes 73736 | tf_op jit(solution)/shard_map/ppermute | solution.py:418
  45.2 1.8 %collective-permute-start.19 = (bf16[32,384]{1,0:T(8,128)(2,1)S(1)}, bf16[32,384]{1,0:T(8,128)(2,1)S(1)}, u32[]{:S(2)}, u32[]{:S(2)}) collective-permute-start(bf16[32,384]{1,0:T(8,128)(2,1)S(1)} %get-tuple-element.68), channel_id=1, source_target_pairs={{0,16},{2,18},{16,0},{18,2},{1,17},{3,19},{17,1},{19,3},{4,20},{6,... | collective-permute-start | bytes 73736 | tf_op jit(solution)/shard_map/ppermute | solution.py:418
  47.0 1.5 %collective-permute-start.20 = (bf16[32,384]{1,0:T(8,128)(2,1)S(1)}, bf16[32,384]{1,0:T(8,128)(2,1)S(1)}, u32[]{:S(2)}, u32[]{:S(2)}) collective-permute-start(bf16[32,384]{1,0:T(8,128)(2,1)S(1)} %get-tuple-element.69), channel_id=1, source_target_pairs={{0,2},{2,0},{16,18},{18,16},{1,3},{3,1},{17,19},{19,17},{4,6},{6,4... | collective-permute-start | bytes 73736 | tf_op jit(solution)/shard_map/ppermute | solution.py:418
  48.4 1.4 %collective-permute-done.18.refs_1_ = bf16[32,384]{1,0:T(8,128)(2,1)S(1)} collective-permute-done((bf16[32,384]{1,0:T(8,128)(2,1)S(1)}, bf16[32,384]{1,0:T(8,128)(2,1)S(1)}, u32[]{:S(2)}, u32[]{:S(2)}) %collective-permute-start.18) | collective-permute-done | bytes 24608 | tf_op jit(solution)/shard_map/ppermute | solution.py:418
  49.9 0.9 %collective-permute-done.20.refs_3_ = bf16[32,384]{1,0:T(8,128)(2,1)S(1)} collective-permute-done((bf16[32,384]{1,0:T(8,128)(2,1)S(1)}, bf16[32,384]{1,0:T(8,128)(2,1)S(1)}, u32[]{:S(2)}, u32[]{:S(2)}) %collective-permute-start.20) | collective-permute-done | bytes 24608 | tf_op jit(solution)/shard_map/ppermute | solution.py:418
  50.8 0.9 %shard_map.50 = (f32[32,320]{1,0:T(8,128)S(1)}, f32[32,32]{1,0:T(8,128)S(1)}, f32[32,8,128]{2,1,0:T(8,128)}) custom-call(f32[32,384]{1,0:T(8,128)S(1)} %get-tuple-element.66.refs_0_, bf16[32,384]{1,0:T(8,128)(2,1)S(1)} %collective-permute-done.18.refs_1_, bf16[32,384]{1,0:T(8,128)(2,1)S(1)} %collective-permute-done.19.refs_2_, ...), custom_call_target="tpu_custom_call" | custom-call | tf_op jit(solution)/shard_map/pallas_call | solution.py:28
  51.7 4.5 %all-to-all-start = ((f32[32,8,128]{2,1,0:T(8,128)}), f32[32,8,128]{2,1,0:T(8,128)S(1)}, u32[]{:S(2)}, u32[]{:S(2)}) async-start(f32[32,8,128]{2,1,0:T(8,128)} %get-tuple-element.74), calls=%async_computation | async-start | bytes 262144 | tf_op jit(solution)/shard_map/all_to_all | solution.py:546
  56.2 0.6 reduce
  56.8 1.1 %shard_map.51 = (f32[32,320]{1,0:T(8,128)S(1)}, f32[32,32]{1,0:T(8,128)S(1)}) custom-call(f32[32,320]{1,0:T(8,128)S(1)} %get-tuple-element.70.image_ref, f32[32,32]{1,0:T(8,128)S(1)} %get-tuple-element.71.gram_ref), custom_call_target="tpu_custom_call" | custom-call | tf_op jit(solution)/shard_map/pallas_call | solution.py:28
  57.9 6.6 %all-to-all-done.grams_ref = f32[32,8,128]{2,1,0:T(8,128)S(1)} async-done(((f32[32,8,128]{2,1,0:T(8,128)}), f32[32,8,128]{2,1,0:T(8,128)S(1)}, u32[]{:S(2)}, u32[]{:S(2)}) %all-to-all-start) | async-done | bytes 131104 | tf_op jit(solution)/shard_map/all_to_all | solution.py:546
  64.4 2.0 %shard_map.52 = f32[32,320]{1,0:T(8,128)} custom-call(f32[32,320]{1,0:T(8,128)S(1)} %get-tuple-element.72.image_ref, f32[32,32]{1,0:T(8,128)S(1)} %get-tuple-element.73.inverse_ref, f32[32,8,128]{2,1,0:T(8,128)S(1)} %all-to-all-done.grams_ref), custom_call_target="tpu_custom_call" | custom-call | tf_op jit(solution)/shard_map/pallas_call | solution.py:28
  (13 shorter events, 0.2 us)
Async XLA Ops:
  0.6 10.7 %collective-permute-start.4 = (bf16[320,256]{1,0:T(8,128)(2,1)}, bf16[320,256]{1,0:T(8,128)(2,1)S(1)}, u32[]{:S(2)}, u32[]{:S(2)}) collective-permute-start(bf16[320,256]{1,0:T(8,128)(2,1)} %emb_ref.1), channel_id=1, source_target_pairs={{0,8},{1,9},{4,12},{5,13},{8,0},{9,1},{12,4},{13,5},{2,10},{3,11},... | collective-permute-start | bytes 491528 | tf_op jit(solution)/shard_map/ppermute | solution.py:418
  3.7 10.3 %collective-permute-start.3 = (bf16[320,256]{1,0:T(8,128)(2,1)}, bf16[320,256]{1,0:T(8,128)(2,1)S(1)}, u32[]{:S(2)}, u32[]{:S(2)}) collective-permute-start(bf16[320,256]{1,0:T(8,128)(2,1)} %emb_ref.1), channel_id=1, source_target_pairs={{0,16},{2,18},{16,0},{18,2},{1,17},{3,19},{17,1},{19,3},{4,20},{6,... | collective-permute-start | bytes 491528 | tf_op jit(solution)/shard_map/ppermute | solution.py:418
  6.3 7.8 %collective-permute-start.2 = (bf16[320,256]{1,0:T(8,128)(2,1)}, bf16[320,256]{1,0:T(8,128)(2,1)S(1)}, u32[]{:S(2)}, u32[]{:S(2)}) collective-permute-start(bf16[320,256]{1,0:T(8,128)(2,1)} %emb_ref.1), channel_id=1, source_target_pairs={{0,2},{2,0},{16,18},{18,16},{1,3},{3,1},{17,19},{19,17},{4,6},{6,4... | collective-permute-start | bytes 491528 | tf_op jit(solution)/shard_map/ppermute | solution.py:418
  7.8 6.3 %collective-permute-start.1 = (bf16[320,256]{1,0:T(8,128)(2,1)}, bf16[320,256]{1,0:T(8,128)(2,1)S(1)}, u32[]{:S(2)}, u32[]{:S(2)}) collective-permute-start(bf16[320,256]{1,0:T(8,128)(2,1)} %emb_ref.1), channel_id=1, source_target_pairs={{0,4},{1,5},{4,0},{5,1},{8,12},{9,13},{12,8},{13,9},{2,6},{3,7},{6... | collective-permute-start | bytes 491528 | tf_op jit(solution)/shard_map/ppermute | solution.py:418
  9.3 4.8 %collective-permute-start = (bf16[320,256]{1,0:T(8,128)(2,1)}, bf16[320,256]{1,0:T(8,128)(2,1)S(1)}, u32[]{:S(2)}, u32[]{:S(2)}) collective-permute-start(bf16[320,256]{1,0:T(8,128)(2,1)} %emb_ref.1), channel_id=1, source_target_pairs={{0,1},{1,0},{4,5},{5,4},{8,9},{9,8},{12,13},{13,12},{2,3},{3,2},{6... | collective-permute-start | bytes 491528 | tf_op jit(solution)/shard_map/ppermute | solution.py:418
  9.3 0.9 %copy-start = (bf16[320,256]{1,0:T(8,128)(2,1)S(1)}, bf16[320,256]{1,0:T(8,128)(2,1)}, u32[]{:S(2)}) copy-start(bf16[320,256]{1,0:T(8,128)(2,1)} %emb_ref.1) | copy-start | bytes 491524
  10.3 0.8 %copy-start.1 = (f32[32,320]{1,0:T(8,128)S(1)}, f32[32,320]{1,0:T(8,128)}, u32[]{:S(2)}) copy-start(f32[32,320]{1,0:T(8,128)} %start_ref.1) | copy-start | bytes 122884
  11.3 6.5 %collective-permute-start.5 = (bf16[320,256]{1,0:T(8,128)(2,1)S(1)}, bf16[320,256]{1,0:T(8,128)(2,1)S(1)}, u32[]{:S(2)}, u32[]{:S(2)}) collective-permute-start(bf16[320,256]{1,0:T(8,128)(2,1)S(1)} %collective-permute-done.4.refs_3_), channel_id=1, source_target_pairs={{0,4},{1,5},{4,0},{5,1},{8,12},{9,13},{12,8},{13,9},{2,6},{3,7},{6... | collective-permute-start | bytes 491528 | tf_op jit(solution)/shard_map/ppermute | solution.py:418
  14.1 3.8 %collective-permute-start.6 = (bf16[320,256]{1,0:T(8,128)(2,1)S(1)}, bf16[320,256]{1,0:T(8,128)(2,1)S(1)}, u32[]{:S(2)}, u32[]{:S(2)}) collective-permute-start(bf16[320,256]{1,0:T(8,128)(2,1)S(1)} %collective-permute-done.1.refs_2_), channel_id=1, source_target_pairs={{0,1},{1,0},{4,5},{5,4},{8,9},{9,8},{12,13},{13,12},{2,3},{3,2},{6... | collective-permute-start | bytes 491528 | tf_op jit(solution)/shard_map/ppermute | solution.py:418
  14.2 3.7 %collective-permute-start.7 = (bf16[320,256]{1,0:T(8,128)(2,1)S(1)}, bf16[320,256]{1,0:T(8,128)(2,1)S(1)}, u32[]{:S(2)}, u32[]{:S(2)}) collective-permute-start(bf16[320,256]{1,0:T(8,128)(2,1)S(1)} %collective-permute-done.4.refs_3_), channel_id=1, source_target_pairs={{0,1},{1,0},{4,5},{5,4},{8,9},{9,8},{12,13},{13,12},{2,3},{3,2},{6... | collective-permute-start | bytes 491528 | tf_op jit(solution)/shard_map/ppermute | solution.py:418
  14.7 6.2 %collective-permute-start.8 = (bf16[320,256]{1,0:T(8,128)(2,1)S(1)}, bf16[320,256]{1,0:T(8,128)(2,1)S(1)}, u32[]{:S(2)}, u32[]{:S(2)}) collective-permute-start(bf16[320,256]{1,0:T(8,128)(2,1)S(1)} %collective-permute-done.3.refs_1_), channel_id=1, source_target_pairs={{0,2},{2,0},{16,18},{18,16},{1,3},{3,1},{17,19},{19,17},{4,6},{6,4... | collective-permute-start | bytes 491528 | tf_op jit(solution)/shard_map/ppermute | solution.py:418
  17.9 3.0 %collective-permute-start.9 = (bf16[320,256]{1,0:T(8,128)(2,1)S(1)}, bf16[320,256]{1,0:T(8,128)(2,1)S(1)}, u32[]{:S(2)}, u32[]{:S(2)}) collective-permute-start(bf16[320,256]{1,0:T(8,128)(2,1)S(1)} %collective-permute-done.5.refs_1_), channel_id=1, source_target_pairs={{0,1},{1,0},{4,5},{5,4},{8,9},{9,8},{12,13},{13,12},{2,3},{3,2},{6... | collective-permute-start | bytes 491528 | tf_op jit(solution)/shard_map/ppermute | solution.py:418
  22.7 6.2 %collective-permute-start.12 = (bf16[40,320]{1,0:T(8,128)(2,1)S(1)}, bf16[40,320]{1,0:T(8,128)(2,1)S(1)}, u32[]{:S(2)}, u32[]{:S(2)}) collective-permute-start(bf16[40,320]{1,0:T(8,128)(2,1)S(1)} %get-tuple-element.61), channel_id=1, source_target_pairs={{0,18},{2,16},{16,2},{18,0},{1,19},{3,17},{17,3},{19,1},{4,22},{6,... | collective-permute-start | bytes 76808 | tf_op jit(solution)/shard_map/ppermute | solution.py:418
  24.0 5.3 %collective-permute-start.11 = (bf16[40,320]{1,0:T(8,128)(2,1)S(1)}, bf16[40,320]{1,0:T(8,128)(2,1)S(1)}, u32[]{:S(2)}, u32[]{:S(2)}) collective-permute-start(bf16[40,320]{1,0:T(8,128)(2,1)S(1)} %get-tuple-element.61), channel_id=1, source_target_pairs={{0,16},{2,18},{16,0},{18,2},{1,17},{3,19},{17,1},{19,3},{4,20},{6,... | collective-permute-start | bytes 76808 | tf_op jit(solution)/shard_map/ppermute | solution.py:418
  26.6 3.9 %collective-permute-start.10 = (bf16[40,320]{1,0:T(8,128)(2,1)S(1)}, bf16[40,320]{1,0:T(8,128)(2,1)S(1)}, u32[]{:S(2)}, u32[]{:S(2)}) collective-permute-start(bf16[40,320]{1,0:T(8,128)(2,1)S(1)} %get-tuple-element.61), channel_id=1, source_target_pairs={{0,2},{2,0},{16,18},{18,16},{1,3},{3,1},{17,19},{19,17},{4,6},{6,4... | collective-permute-start | bytes 76808 | tf_op jit(solution)/shard_map/ppermute | solution.py:418
  31.3 1.4 %collective-permute-start.13 = (bf16[4,32,320]{2,1,0:T(8,128)(2,1)S(1)}, bf16[4,32,320]{2,1,0:T(8,128)(2,1)S(1)}, u32[]{:S(2)}, u32[]{:S(2)}) collective-permute-start(bf16[4,32,320]{2,1,0:T(8,128)(2,1)S(1)} %get-tuple-element.64), channel_id=1, source_target_pairs={{0,1},{1,0},{4,5},{5,4},{8,9},{9,8},{12,13},{13,12},{2,3},{3,2},{6... | collective-permute-start | bytes 245768 | tf_op jit(solution)/shard_map/ppermute | solution.py:418
  32.7 6.4 %collective-permute-start.16 = (bf16[32,1408]{1,0:T(8,128)(2,1)S(1)}, bf16[32,1408]{1,0:T(8,128)(2,1)S(1)}, u32[]{:S(2)}, u32[]{:S(2)}) collective-permute-start(bf16[32,1408]{1,0:T(8,128)(2,1)S(1)} %shard_map.46.refs_0_), channel_id=1, source_target_pairs={{0,12},{1,13},{4,8},{5,9},{8,4},{9,5},{12,0},{13,1},{2,14},{3,15},... | collective-permute-start | bytes 270344 | tf_op jit(solution)/shard_map/ppermute | solution.py:418
  34.8 5.6 %collective-permute-start.15 = (bf16[32,1408]{1,0:T(8,128)(2,1)S(1)}, bf16[32,1408]{1,0:T(8,128)(2,1)S(1)}, u32[]{:S(2)}, u32[]{:S(2)}) collective-permute-start(bf16[32,1408]{1,0:T(8,128)(2,1)S(1)} %shard_map.46.refs_0_), channel_id=1, source_target_pairs={{0,8},{1,9},{4,12},{5,13},{8,0},{9,1},{12,4},{13,5},{2,10},{3,11},... | collective-permute-start | bytes 270344 | tf_op jit(solution)/shard_map/ppermute | solution.py:418
  35.8 4.7 %collective-permute-start.14 = (bf16[32,1408]{1,0:T(8,128)(2,1)S(1)}, bf16[32,1408]{1,0:T(8,128)(2,1)S(1)}, u32[]{:S(2)}, u32[]{:S(2)}) collective-permute-start(bf16[32,1408]{1,0:T(8,128)(2,1)S(1)} %shard_map.46.refs_0_), channel_id=1, source_target_pairs={{0,4},{1,5},{4,0},{5,1},{8,12},{9,13},{12,8},{13,9},{2,6},{3,7},{6... | collective-permute-start | bytes 270344 | tf_op jit(solution)/shard_map/ppermute | solution.py:418
  41.2 1.5 %collective-permute-start.17 = (bf16[4,64,384]{2,1,0:T(8,128)(2,1)S(1)}, bf16[4,64,384]{2,1,0:T(8,128)(2,1)S(1)}, u32[]{:S(2)}, u32[]{:S(2)}) collective-permute-start(bf16[4,64,384]{2,1,0:T(8,128)(2,1)S(1)} %shard_map.47.refs_3_), channel_id=1, source_target_pairs={{0,1},{1,0},{4,5},{5,4},{8,9},{9,8},{12,13},{13,12},{2,3},{3,2},{6... | collective-permute-start | bytes 589832 | tf_op jit(solution)/shard_map/ppermute | solution.py:418
  44.0 5.8 %collective-permute-start.18 = (bf16[32,384]{1,0:T(8,128)(2,1)S(1)}, bf16[32,384]{1,0:T(8,128)(2,1)S(1)}, u32[]{:S(2)}, u32[]{:S(2)}) collective-permute-start(bf16[32,384]{1,0:T(8,128)(2,1)S(1)} %get-tuple-element.67), channel_id=1, source_target_pairs={{0,18},{2,16},{16,2},{18,0},{1,19},{3,17},{17,3},{19,1},{4,22},{6,... | collective-permute-start | bytes 73736 | tf_op jit(solution)/shard_map/ppermute | solution.py:418
  45.2 4.7 %collective-permute-start.19 = (bf16[32,384]{1,0:T(8,128)(2,1)S(1)}, bf16[32,384]{1,0:T(8,128)(2,1)S(1)}, u32[]{:S(2)}, u32[]{:S(2)}) collective-permute-start(bf16[32,384]{1,0:T(8,128)(2,1)S(1)} %get-tuple-element.68), channel_id=1, source_target_pairs={{0,16},{2,18},{16,0},{18,2},{1,17},{3,19},{17,1},{19,3},{4,20},{6,... | collective-permute-start | bytes 73736 | tf_op jit(solution)/shard_map/ppermute | solution.py:418
  47.0 3.8 %collective-permute-start.20 = (bf16[32,384]{1,0:T(8,128)(2,1)S(1)}, bf16[32,384]{1,0:T(8,128)(2,1)S(1)}, u32[]{:S(2)}, u32[]{:S(2)}) collective-permute-start(bf16[32,384]{1,0:T(8,128)(2,1)S(1)} %get-tuple-element.69), channel_id=1, source_target_pairs={{0,2},{2,0},{16,18},{18,16},{1,3},{3,1},{17,19},{19,17},{4,6},{6,4... | collective-permute-start | bytes 73736 | tf_op jit(solution)/shard_map/ppermute | solution.py:418
  51.7 12.7 %all-to-all-start = ((f32[32,8,128]{2,1,0:T(8,128)}), f32[32,8,128]{2,1,0:T(8,128)S(1)}, u32[]{:S(2)}, u32[]{:S(2)}) async-start(f32[32,8,128]{2,1,0:T(8,128)} %get-tuple-element.74), calls=%async_computation | async-start | bytes 262144 | tf_op jit(solution)/shard_map/all_to_all | solution.py:546

commit v2 on v1

--- a/solution.py
+++ b/solution.py
@@ -106,7 +106,7 @@
     even_ref[0:own, :] = unit_ref[...]
     for i, ref in enumerate(row_refs, 1):
         rows_ref[i * own : (i + 1) * own, :] = unit_rows(ref, 8.0)
-    half = (len(lane_refs) + 1) // 2
+    half = even_ref.shape[0] // own
     for i, ref in enumerate(lane_refs, 1):
         target, at = (even_ref, i) if i < half else (odd_ref, i - half)
         target[at * own : (at + 1) * own, :] = unit_rows(ref, 1.0)
@@ -114,21 +114,17 @@
     affinity(rows_ref, parts, own, fold_ref)
 
 
-def rest_kernel(rows_ref, fold_in_ref, even_in_ref, odd_in_ref, *refs):
-    row_ref, even_ref, odd_ref, start_ref = refs[:4]
-    side_tile_ref, even_last_ref, odd_last_ref, sums_ref, send_ref = refs[4:9]
-    last_ref, even_all, odd_all, side_all, fold_ref, fold_last_ref = refs[9:]
+def rest_kernel(rows_ref, fold_in_ref, even_ref, odd_in_ref, *refs):
+    row_ref, fresh_ref, start_ref = refs[:3]
+    side_tile_ref, even_last_ref, odd_last_ref, sums_ref, send_ref = refs[3:8]
+    last_ref, odd_ref, fold_ref, fold_last_ref = refs[8:]
     own = row_ref.shape[0]
-    high = even_in_ref.shape[0]
-    sides = ((even_in_ref, even_ref, even_all), (odd_in_ref, odd_ref, odd_all))
-    for i, (before, fresh, whole) in enumerate(sides):
-        unit = unit_rows(fresh, 1.0)
-        whole[0:high, :] = before[...]
-        whole[high : high + own, :] = unit
-        side_all[i * own : (i + 1) * own, :] = unit
-    affinity(rows_ref, [(side_all, 0, side_tile_ref)], own, fold_ref, fold_in_ref)
+    high = odd_in_ref.shape[0]
+    odd_ref[0:high, :] = odd_in_ref[...]
+    odd_ref[high : high + own, :] = unit_rows(fresh_ref, 1.0)
+    affinity(rows_ref, [(odd_ref, high, side_tile_ref)], own, fold_ref, fold_in_ref)
     last_ref[...] = unit_rows(row_ref, 8.0)
-    parts = [(even_all, 0, even_last_ref), (odd_all, 0, odd_last_ref)]
+    parts = [(even_ref, 0, even_last_ref), (odd_ref, 0, odd_last_ref)]
     affinity(last_ref, parts, own, fold_last_ref)
     lines = cut(unfold(fold_ref[...]), own) + [unfold(fold_last_ref[...])]
     sums = jnp.concatenate(lines, axis=0)
@@ -141,27 +137,17 @@
     send_ref[...] = jnp.concatenate(parts, axis=0).astype(jnp.bfloat16)
 
 
-def side_span(odd, own):
-    low = own // 128 * 128 if odd else 0
-    return low, (2 * own if odd else lanes(own)), odd * own - low
-
-
-def lane_products(left, last, tiles, odd, own):
-    main_ref, side_ref, last_ref = tiles
-
-    def product(value, ref, low, high):
+def lane_products(left, last, tiles, own):
+    def product(value, ref):
         return side_by_side(
             [
-                jnp.dot(value, ref[:, i : min(i + 256, high)], preferred_element_type=jnp.float32)
-                for i in range(low, high, 256)
+                jnp.dot(value, ref[:, i : i + 256], preferred_element_type=jnp.float32)
+                for i in range(0, ref.shape[1], 256)
             ]
         )
 
-    low, high, at = side_span(odd, own)
-    blocks = cut(product(left, main_ref, 0, main_ref.shape[1]), own)
-    blocks.append(product(left, side_ref, low, high)[:, at : at + own])
-    more = cut(product(last, last_ref, 0, last_ref.shape[1]), own)
-    return [x + y for x, y in zip(blocks, more)]
+    blocks = [block for ref in tiles[:-1] for block in cut(product(left, ref), own)]
+    return [x + y for x, y in zip(blocks, cut(product(last, tiles[-1]), own))]
 
 
 def with_tail(block, tail, width):
@@ -221,14 +207,14 @@
     scaled = [(start * scale).astype(jnp.bfloat16) for start, scale in zip(starts, scales)]
     left_ref[...] = side_by_side(scaled[:-1])
     left_last_ref[...] = scaled[-1]
-    blocks = lane_products(left_ref[...], left_last_ref[...], tiles, 1, own)
+    blocks = lane_products(left_ref[...], left_last_ref[...], tiles, own)
     for i, block in enumerate(blocks):
         pieces_ref[i] = block.astype(jnp.bfloat16)
 
 
 def same_kernel(*refs):
-    tiles, (left_ref, left_last_ref, pieces_ref) = refs[:3], refs[3:]
-    blocks = lane_products(left_ref[...], left_last_ref[...], tiles, 0, pieces_ref.shape[2])
+    tiles, (left_ref, left_last_ref, pieces_ref) = refs[:2], refs[2:]
+    blocks = lane_products(left_ref[...], left_last_ref[...], tiles, pieces_ref.shape[2])
     for i, block in enumerate(blocks):
         pieces_ref[i] = block
 
@@ -268,43 +254,33 @@
         out_ref[j, count : 2 * count, :] = whole.astype(jnp.bfloat16)
 
 
-def row_products(image_ref, tiles, odd, own):
-    main_ref, side_ref, last_ref = tiles
+def row_products(image_ref, tiles, own):
     count = image_ref.shape[1] // 2
-    lefts = [image_ref[i, :, 0:own] for i in range(image_ref.shape[0])]
-    low, high, at = side_span(odd, own)
-    padded = [lefts[-1]]
-    for gap, place in ((at, 0), (high - low - at - own, len(padded) + 1)):
-        if gap:
-            padded.insert(place, jnp.zeros((2 * count, gap), jnp.bfloat16))
-    main, whole = side_by_side(lefts[:-1]), side_by_side(lefts)
+    whole = side_by_side([image_ref[i, :, 0:own] for i in range(image_ref.shape[0])])
     values = []
-    for pairs in (
-        ((main, main_ref, 0, main.shape[1]), (side_by_side(padded), side_ref, low, high)),
-        ((whole, last_ref, 0, whole.shape[1]),),
-    ):
-        total = pairs[0][1].shape[0]
+    for refs in (tiles[:-1], tiles[-1:]):
+        total = refs[0].shape[0]
         for i in range(0, total, 256):
-            value = sum(
-                lax.dot_general(
-                    left, ref[i : min(i + 256, total), start:stop], NT,
+            value, at = 0.0, 0
+            for ref in refs:
+                value = value + lax.dot_general(
+                    whole[:, at : at + ref.shape[1]], ref[i : min(i + 256, total), :], NT,
                     preferred_element_type=jnp.float32,
                 )
-                for left, ref, start, stop in pairs
-            )
+                at += ref.shape[1]
             values.append(value[:count] + value[count:])
     return side_by_side(values)
 
 
 def own_lanes_kernel(own, *refs):
-    tiles, (image_ref, out_ref) = refs[:3], refs[3:]
-    out_ref[...] = row_products(image_ref, tiles, 0, own)
+    tiles, (image_ref, out_ref) = refs[:2], refs[2:]
+    out_ref[...] = row_products(image_ref, tiles, own)
 
 
 def other_lanes_kernel(own, *refs):
     tiles, (own_image_ref, image_ref, line_ref), out_refs = refs[:3], refs[3:6], refs[6:]
     count = line_ref.shape[0]
-    value = line_ref[...] + row_products(image_ref, tiles, 1, own)
+    value = line_ref[...] + row_products(image_ref, tiles, own)
     gram = 0.0
     for ref in (own_image_ref, image_ref):
         gram = gram + gram_of(ref[0, 0:count, :].astype(jnp.float32), own)
@@ -452,28 +428,29 @@
 
     high, deep = (rows - 1) * own, (half - 1) * own
     unit, farthest = lax.optimization_barrier((unit, lane_blocks[even[-1]]))
+    lane_blocks[even[-1]] = farthest
     main_rows, even_lanes, odd_lanes, even_main, odd_main, fold = call(
         functools.partial(main_kernel, rows - 1),
         [
             ((high, width), bf16),
+            ((half * own, width), bf16),
             ((deep, width), bf16),
-            ((deep, width), bf16),
-            ((high, deep), bf16),
+            ((high, half * own), bf16),
             ((high, deep), bf16),
             ((high, 128), f32),
         ],
-        flops=4 * high * deep * width,
+        flops=2 * high * (half * own + deep) * width,
     )(
         unit,
         *[row_blocks[m] for m in range(1, rows - 1)],
-        *[lane_blocks[m] for m in even[1:-1]],
+        *[lane_blocks[m] for m in even[1:]],
         *[lane_blocks[m + 1] for m in even[:-1]],
     )
     lines = count + -(-2 * rows // 8) * 8
-    side, even_last, odd_last, sums, send = call(
+    odd_side, even_last, odd_last, sums, send = call(
         rest_kernel,
         [
-            ((high, 2 * own), bf16),
+            ((high, own), bf16),
             ((own, half * own), bf16),
             ((own, half * own), bf16),
             ((rows, own), f32),
@@ -482,24 +459,21 @@
         [
             pltpu.VMEM((own, width), bf16),
             pltpu.VMEM((half * own, width), bf16),
-            pltpu.VMEM((half * own, width), bf16),
-            pltpu.VMEM((2 * own, width), bf16),
             pltpu.VMEM((high, 128), f32),
             pltpu.VMEM((own, 128), f32),
         ],
-        flops=4 * (high + half * own) * own * width,
+        flops=2 * (high + cols * own) * own * width,
     )(
         main_rows,
         fold,
         even_lanes,
         odd_lanes,
         row_blocks[rows - 1],
-        farthest,
         swap(farthest, LANE_SET, 1),
         starts,
     )
-    even_tiles = (even_main, side, even_last)
-    odd_tiles = (odd_main, side, odd_last)
+    even_tiles = (even_main, even_last)
+    odd_tiles = (odd_main, odd_side, odd_last)
 
     came = [swap(send, ROW_SET, m) for m in range(1, rows)]
     other, left, left_last, degrees, scale = call(

time: 66.7 us -> 66.6 us (level)
  no operation moved by 1% of the time
where the time goes in v2:
time: 66.6 us; the launch traced here: 66.4 us
  starting transfers between devices  29.7 us (45%)
  waiting for transfers between devices  20.9 us (31%)
  Pallas kernels  12.7 us (19%)
  local copies, waits for them, and re-layouts  1.74 us (3%)
  between operations  0.73 us (1%)
    ppermute x21, starting transfers between devices, swap(): return lax.ppermute(value, axes, [(i, i ^ offset) for i in range(size)])  25.2 us
    ppermute x21, waiting for transfers between devices, swap(): return lax.ppermute(value, axes, [(i, i ^ offset) for i in range(size)])  14.4 us
    pallas_call x12, Pallas kernels, run(): pl.pallas_call(kernel, out_shape=[jax.ShapeDtypeStruct(s, d) for s, d in...  12.7 us
    all_to_all x1, waiting for transfers between devices, local(): grams = lax.all_to_all(grams, NAMES, 0, 0, tiled=True)  6.55 us
    all_to_all x1, starting transfers between devices, local(): grams = lax.all_to_all(grams, NAMES, 0, 0, tiled=True)  4.51 us
    unnamed x4, local copies, waits for them, and re-layouts  1.74 us
  transfers between devices with their start and end apart: 22, of which 16 were waited for; matrix products, arithmetic and copies ran while one was open for 1% of the time, Pallas kernels for 8%

profile of v2, /device:TPU:0, one launch (start us, length us, event | category | flops | bytes accessed | tf_op | source)
XLA Modules:
  0.0 66.4 jit_solution(18431810463184513560)
XLA Ops:
  0.6 3.1 %collective-permute-start.4 = (bf16[320,256]{1,0:T(8,128)(2,1)}, bf16[320,256]{1,0:T(8,128)(2,1)S(1)}, u32[]{:S(2)}, u32[]{:S(2)}) collective-permute-start(bf16[320,256]{1,0:T(8,128)(2,1)} %emb_ref.1), channel_id=1, source_target_pairs={{0,8},{1,9},{4,12},{5,13},{8,0},{9,1},{12,4},{13,5},{2,10},{3,11},... | collective-permute-start | bytes 491528 | tf_op jit(solution)/shard_map/ppermute | solution.py:394
  3.7 2.6 %collective-permute-start.3 = (bf16[320,256]{1,0:T(8,128)(2,1)}, bf16[320,256]{1,0:T(8,128)(2,1)S(1)}, u32[]{:S(2)}, u32[]{:S(2)}) collective-permute-start(bf16[320,256]{1,0:T(8,128)(2,1)} %emb_ref.1), channel_id=1, source_target_pairs={{0,16},{2,18},{16,0},{18,2},{1,17},{3,19},{17,1},{19,3},{4,20},{6,... | collective-permute-start | bytes 491528 | tf_op jit(solution)/shard_map/ppermute | solution.py:394
  6.3 1.5 %collective-permute-start.2 = (bf16[320,256]{1,0:T(8,128)(2,1)}, bf16[320,256]{1,0:T(8,128)(2,1)S(1)}, u32[]{:S(2)}, u32[]{:S(2)}) collective-permute-start(bf16[320,256]{1,0:T(8,128)(2,1)} %emb_ref.1), channel_id=1, source_target_pairs={{0,2},{2,0},{16,18},{18,16},{1,3},{3,1},{17,19},{19,17},{4,6},{6,4... | collective-permute-start | bytes 491528 | tf_op jit(solution)/shard_map/ppermute | solution.py:394
  7.8 1.5 %collective-permute-start.1 = (bf16[320,256]{1,0:T(8,128)(2,1)}, bf16[320,256]{1,0:T(8,128)(2,1)S(1)}, u32[]{:S(2)}, u32[]{:S(2)}) collective-permute-start(bf16[320,256]{1,0:T(8,128)(2,1)} %emb_ref.1), channel_id=1, source_target_pairs={{0,4},{1,5},{4,0},{5,1},{8,12},{9,13},{12,8},{13,9},{2,6},{3,7},{6... | collective-permute-start | bytes 491528 | tf_op jit(solution)/shard_map/ppermute | solution.py:394
  9.3 0.9 %copy-done = bf16[320,256]{1,0:T(8,128)(2,1)S(1)} copy-done((bf16[320,256]{1,0:T(8,128)(2,1)S(1)}, bf16[320,256]{1,0:T(8,128)(2,1)}, u32[]{:S(2)}) %copy-start) | copy-done | bytes 163864
  10.3 0.8 %copy-done.1 = f32[32,320]{1,0:T(8,128)S(1)} copy-done((f32[32,320]{1,0:T(8,128)S(1)}, f32[32,320]{1,0:T(8,128)}, u32[]{:S(2)}) %copy-start.1) | copy-done | bytes 40984
  11.1 0.1 shard_map.41
  11.2 0.1 collective-permute-done.4.refs_3_
  11.3 1.8 %collective-permute-start.5 = (bf16[320,256]{1,0:T(8,128)(2,1)S(1)}, bf16[320,256]{1,0:T(8,128)(2,1)S(1)}, u32[]{:S(2)}, u32[]{:S(2)}) collective-permute-start(bf16[320,256]{1,0:T(8,128)(2,1)S(1)} %collective-permute-done.4.refs_3_), channel_id=1, source_target_pairs={{0,4},{1,5},{4,0},{5,1},{8,12},{9,13},{12,8},{13,9},{2,6},{3,7},{6... | collective-permute-start | bytes 491528 | tf_op jit(solution)/shard_map/ppermute | solution.py:394
  13.2 0.9 %collective-permute-done.3.refs_1_ = bf16[320,256]{1,0:T(8,128)(2,1)S(1)} collective-permute-done((bf16[320,256]{1,0:T(8,128)(2,1)}, bf16[320,256]{1,0:T(8,128)(2,1)S(1)}, u32[]{:S(2)}, u32[]{:S(2)}) %collective-permute-start.3) | collective-permute-done | bytes 163872 | tf_op jit(solution)/shard_map/ppermute | solution.py:394
  14.2 0.5 collective-permute-start.7
  14.7 1.5 %collective-permute-start.8 = (bf16[320,256]{1,0:T(8,128)(2,1)S(1)}, bf16[320,256]{1,0:T(8,128)(2,1)S(1)}, u32[]{:S(2)}, u32[]{:S(2)}) collective-permute-start(bf16[320,256]{1,0:T(8,128)(2,1)S(1)} %collective-permute-done.3.refs_1_), channel_id=1, source_target_pairs={{0,2},{2,0},{16,18},{18,16},{1,3},{3,1},{17,19},{19,17},{4,6},{6,4... | collective-permute-start | bytes 491528 | tf_op jit(solution)/shard_map/ppermute | solution.py:394
  16.1 1.7 %collective-permute-done.5.refs_4_ = bf16[320,256]{1,0:T(8,128)(2,1)S(1)} collective-permute-done((bf16[320,256]{1,0:T(8,128)(2,1)S(1)}, bf16[320,256]{1,0:T(8,128)(2,1)S(1)}, u32[]{:S(2)}, u32[]{:S(2)}) %collective-permute-start.5) | collective-permute-done | bytes 163872 | tf_op jit(solution)/shard_map/ppermute | solution.py:394
  17.9 2.1 %shard_map.42 = (bf16[960,256]{1,0:T(8,128)(2,1)S(1)}, bf16[1280,256]{1,0:T(8,128)(2,1)S(1)}, bf16[960,256]{1,0:T(8,128)(2,1)S(1)}, bf16[960,1280]{1,0:T(8,128)(...) custom-call(bf16[320,256]{1,0:T(8,128)(2,1)S(1)} %get-tuple-element.44.unit_ref, ...), custom_call_target="tpu_custom_call" | custom-call | flops 1101004800 | tf_op jit(solution)/shard_map/pallas_call | solution.py:28
  20.0 0.9 %collective-permute-done.8.refs_0_ = bf16[320,256]{1,0:T(8,128)(2,1)S(1)} collective-permute-done((bf16[320,256]{1,0:T(8,128)(2,1)S(1)}, bf16[320,256]{1,0:T(8,128)(2,1)S(1)}, u32[]{:S(2)}, u32[]{:S(2)}) %collective-permute-start.8) | collective-permute-done | bytes 163872 | tf_op jit(solution)/shard_map/ppermute | solution.py:394
  20.8 1.7 %shard_map.43 = (bf16[960,320]{1,0:T(8,128)(2,1)S(1)}, bf16[320,1280]{1,0:T(8,128)(2,1)S(1)}, bf16[320,1280]{1,0:T(8,128)(2,1)S(1)}, f32[4,320]{1,0:T(4,128)S(1)}, bf16[40,320]{1,0:T(8,128)(2,1)S(1)}) custom-call(bf16[960,256]{1,0:T(8,128)(2,1)S(1)} %get-tuple-element.51.rows_ref, f32[960,128]{1,0:T(8,128)S(1)} %get-tuple-element.52.fold_in_ref, ...), custom_call_target="tpu_custom_call" | custom-call | flops 576716800 | tf_op jit(solution)/shard_map/pallas_call | solution.py:28
  22.5 1.3 %collective-permute-start.12 = (bf16[40,320]{1,0:T(8,128)(2,1)S(1)}, bf16[40,320]{1,0:T(8,128)(2,1)S(1)}, u32[]{:S(2)}, u32[]{:S(2)}) collective-permute-start(bf16[40,320]{1,0:T(8,128)(2,1)S(1)} %get-tuple-element.61), channel_id=1, source_target_pairs={{0,18},{2,16},{16,2},{18,0},{1,19},{3,17},{17,3},{19,1},{4,22},{6,... | collective-permute-start | bytes 76808 | tf_op jit(solution)/shard_map/ppermute | solution.py:394
  23.9 2.6 %collective-permute-start.11 = (bf16[40,320]{1,0:T(8,128)(2,1)S(1)}, bf16[40,320]{1,0:T(8,128)(2,1)S(1)}, u32[]{:S(2)}, u32[]{:S(2)}) collective-permute-start(bf16[40,320]{1,0:T(8,128)(2,1)S(1)} %get-tuple-element.61), channel_id=1, source_target_pairs={{0,16},{2,18},{16,0},{18,2},{1,17},{3,19},{17,1},{19,3},{4,20},{6,... | collective-permute-start | bytes 76808 | tf_op jit(solution)/shard_map/ppermute | solution.py:394
  26.5 0.5 collective-permute-start.10
  27.0 1.8 %collective-permute-done.12.refs_7_ = bf16[40,320]{1,0:T(8,128)(2,1)S(1)} collective-permute-done((bf16[40,320]{1,0:T(8,128)(2,1)S(1)}, bf16[40,320]{1,0:T(8,128)(2,1)S(1)}, u32[]{:S(2)}, u32[]{:S(2)}) %collective-permute-start.12) | collective-permute-done | bytes 25632 | tf_op jit(solution)/shard_map/ppermute | solution.py:394
  28.8 0.4 collective-permute-done.11.refs_6_
  29.2 1.2 %collective-permute-done.10.refs_5_ = bf16[40,320]{1,0:T(8,128)(2,1)S(1)} collective-permute-done((bf16[40,320]{1,0:T(8,128)(2,1)S(1)}, bf16[40,320]{1,0:T(8,128)(2,1)S(1)}, u32[]{:S(2)}, u32[]{:S(2)}) %collective-permute-start.10) | collective-permute-done | bytes 25632 | tf_op jit(solution)/shard_map/ppermute | solution.py:394
  30.4 0.8 %shard_map.44 = (bf16[4,32,320]{2,1,0:T(8,128)(2,1)S(1)}, bf16[32,960]{1,0:T(8,128)(2,1)S(1)}, bf16[32,320]{1,0:T(8,128)(2,1)S(1)}, f32[1,320]{1,0:T(1,128)S(1)}, f32[1,320]{1,0:T(1,128)S(1)}) custom-call(bf16[960,960]{1,0:T(8,128)(2,1)S(1)} %get-tuple-element.50.refs_0_, bf16[960,320]{1,0:T(8,128)(2,1)S(1)} %get-tuple-element.56.refs_1_, ...), custom_call_target="tpu_custom_call" | custom-call | tf_op jit(solution)/shard_map/pallas_call | solution.py:28
  31.2 0.7 %shard_map.45.pieces_ref = f32[4,32,320]{2,1,0:T(8,128)S(1)} custom-call(bf16[960,1280]{1,0:T(8,128)(2,1)S(1)} %get-tuple-element.58.refs_0_, bf16[320,1280]{1,0:T(8,128)(2,1)S(1)} %get-tuple-element.59.refs_1_, bf16[32,960]{1,0:T(8,128)(2,1)S(1)} %get-tuple-element.62.refs_2_, bf16[32,320]{1,0:T(8,128)(2,1)S(1)} %get-tuple-element.63.refs_3_), custom_call_target="tpu_custom_call" | custom-call | flops 104857600 | tf_op jit(solution)/shard_map/pallas_call | solution.py:28
  31.9 0.6 collective-permute-done.13.other_ref
  32.5 0.1 shard_map.46.refs_0_
  32.6 2.0 %collective-permute-start.16 = (bf16[32,1408]{1,0:T(8,128)(2,1)S(1)}, bf16[32,1408]{1,0:T(8,128)(2,1)S(1)}, u32[]{:S(2)}, u32[]{:S(2)}) collective-permute-start(bf16[32,1408]{1,0:T(8,128)(2,1)S(1)} %shard_map.46.refs_0_), channel_id=1, source_target_pairs={{0,12},{1,13},{4,8},{5,9},{8,4},{9,5},{12,0},{13,1},{2,14},{3,15},... | collective-permute-start | bytes 270344 | tf_op jit(solution)/shard_map/ppermute | solution.py:394
  34.6 1.0 %collective-permute-start.15 = (bf16[32,1408]{1,0:T(8,128)(2,1)S(1)}, bf16[32,1408]{1,0:T(8,128)(2,1)S(1)}, u32[]{:S(2)}, u32[]{:S(2)}) collective-permute-start(bf16[32,1408]{1,0:T(8,128)(2,1)S(1)} %shard_map.46.refs_0_), channel_id=1, source_target_pairs={{0,8},{1,9},{4,12},{5,13},{8,0},{9,1},{12,4},{13,5},{2,10},{3,11},... | collective-permute-start | bytes 270344 | tf_op jit(solution)/shard_map/ppermute | solution.py:394
  35.6 0.5 collective-permute-start.14
  36.2 2.9 %collective-permute-done.16.refs_3_ = bf16[32,1408]{1,0:T(8,128)(2,1)S(1)} collective-permute-done((bf16[32,1408]{1,0:T(8,128)(2,1)S(1)}, bf16[32,1408]{1,0:T(8,128)(2,1)S(1)}, u32[]{:S(2)}, u32[]{:S(2)}) %collective-permute-start.16) | collective-permute-done | bytes 90144 | tf_op jit(solution)/shard_map/ppermute | solution.py:394
  39.0 1.2 %collective-permute-done.15.refs_2_ = bf16[32,1408]{1,0:T(8,128)(2,1)S(1)} collective-permute-done((bf16[32,1408]{1,0:T(8,128)(2,1)S(1)}, bf16[32,1408]{1,0:T(8,128)(2,1)S(1)}, u32[]{:S(2)}, u32[]{:S(2)}) %collective-permute-start.15) | collective-permute-done | bytes 90144 | tf_op jit(solution)/shard_map/ppermute | solution.py:394
  40.2 0.1 collective-permute-done.14.refs_1_
  40.4 0.7 shard_map.47.refs_2_.refs_3_
  41.1 1.2 %shard_map.48.refs_5_ = f32[32,1280]{1,0:T(8,128)S(1)} custom-call(bf16[960,1280]{1,0:T(8,128)(2,1)S(1)} %get-tuple-element.58.refs_0_, bf16[320,1280]{1,0:T(8,128)(2,1)S(1)} %get-tuple-element.59.refs_1_, bf16[4,64,384]{2,1,0:T(8,128)(2,1)S(1)} %shard_map.47.refs_2_.refs_3_), custom_call_target="tpu_custom_call" | custom-call | flops 209715200 | tf_op jit(solution)/shard_map/pallas_call | solution.py:28
  42.2 0.3 collective-permute-done.17.refs_4_
  42.5 1.4 %shard_map.49 = (f32[32,384]{1,0:T(8,128)S(1)}, bf16[32,384]{1,0:T(8,128)(2,1)S(1)}, bf16[32,384]{1,0:T(8,128)(2,1)S(1)}, bf16[32,384]{1,0:T(8,128)(2,1)S(1)}) custom-call(bf16[960,960]{1,0:T(8,128)(2,1)S(1)} %get-tuple-element.50.refs_0_, bf16[960,320]{1,0:T(8,128)(2,1)S(1)} %get-tuple-element.56.refs_1_, bf16[320,1280]{1,0:T(8,128)(2,1)S(1)} %get-tuple-element.57.refs_2_, ...), custom_call_target="tpu_custom_call" | custom-call | tf_op jit(solution)/shard_map/pallas_call | solution.py:28
  43.9 1.2 %collective-permute-start.18 = (bf16[32,384]{1,0:T(8,128)(2,1)S(1)}, bf16[32,384]{1,0:T(8,128)(2,1)S(1)}, u32[]{:S(2)}, u32[]{:S(2)}) collective-permute-start(bf16[32,384]{1,0:T(8,128)(2,1)S(1)} %get-tuple-element.67), channel_id=1, source_target_pairs={{0,18},{2,16},{16,2},{18,0},{1,19},{3,17},{17,3},{19,1},{4,22},{6,... | collective-permute-start | bytes 73736 | tf_op jit(solution)/shard_map/ppermute | solution.py:394
  45.1 1.8 %collective-permute-start.19 = (bf16[32,384]{1,0:T(8,128)(2,1)S(1)}, bf16[32,384]{1,0:T(8,128)(2,1)S(1)}, u32[]{:S(2)}, u32[]{:S(2)}) collective-permute-start(bf16[32,384]{1,0:T(8,128)(2,1)S(1)} %get-tuple-element.68), channel_id=1, source_target_pairs={{0,16},{2,18},{16,0},{18,2},{1,17},{3,19},{17,1},{19,3},{4,20},{6,... | collective-permute-start | bytes 73736 | tf_op jit(solution)/shard_map/ppermute | solution.py:394
  46.9 1.5 %collective-permute-start.20 = (bf16[32,384]{1,0:T(8,128)(2,1)S(1)}, bf16[32,384]{1,0:T(8,128)(2,1)S(1)}, u32[]{:S(2)}, u32[]{:S(2)}) collective-permute-start(bf16[32,384]{1,0:T(8,128)(2,1)S(1)} %get-tuple-element.69), channel_id=1, source_target_pairs={{0,2},{2,0},{16,18},{18,16},{1,3},{3,1},{17,19},{19,17},{4,6},{6,4... | collective-permute-start | bytes 73736 | tf_op jit(solution)/shard_map/ppermute | solution.py:394
  48.4 1.4 %collective-permute-done.18.refs_1_ = bf16[32,384]{1,0:T(8,128)(2,1)S(1)} collective-permute-done((bf16[32,384]{1,0:T(8,128)(2,1)S(1)}, bf16[32,384]{1,0:T(8,128)(2,1)S(1)}, u32[]{:S(2)}, u32[]{:S(2)}) %collective-permute-start.18) | collective-permute-done | bytes 24608 | tf_op jit(solution)/shard_map/ppermute | solution.py:394
  49.7 0.1 collective-permute-done.19.refs_2_
  49.8 0.9 %collective-permute-done.20.refs_3_ = bf16[32,384]{1,0:T(8,128)(2,1)S(1)} collective-permute-done((bf16[32,384]{1,0:T(8,128)(2,1)S(1)}, bf16[32,384]{1,0:T(8,128)(2,1)S(1)}, u32[]{:S(2)}, u32[]{:S(2)}) %collective-permute-start.20) | collective-permute-done | bytes 24608 | tf_op jit(solution)/shard_map/ppermute | solution.py:394
  50.7 0.9 %shard_map.50 = (f32[32,320]{1,0:T(8,128)S(1)}, f32[32,32]{1,0:T(8,128)S(1)}, f32[32,8,128]{2,1,0:T(8,128)}) custom-call(f32[32,384]{1,0:T(8,128)S(1)} %get-tuple-element.66.refs_0_, bf16[32,384]{1,0:T(8,128)(2,1)S(1)} %collective-permute-done.18.refs_1_, bf16[32,384]{1,0:T(8,128)(2,1)S(1)} %collective-permute-done.19.refs_2_, ...), custom_call_target="tpu_custom_call" | custom-call | tf_op jit(solution)/shard_map/pallas_call | solution.py:28
  51.6 4.5 %all-to-all-start = ((f32[32,8,128]{2,1,0:T(8,128)}), f32[32,8,128]{2,1,0:T(8,128)S(1)}, u32[]{:S(2)}, u32[]{:S(2)}) async-start(f32[32,8,128]{2,1,0:T(8,128)} %get-tuple-element.74), calls=%async_computation | async-start | bytes 262144 | tf_op jit(solution)/shard_map/all_to_all | solution.py:520
  56.1 0.6 reduce
  56.7 1.1 %shard_map.51 = (f32[32,320]{1,0:T(8,128)S(1)}, f32[32,32]{1,0:T(8,128)S(1)}) custom-call(f32[32,320]{1,0:T(8,128)S(1)} %get-tuple-element.70.image_ref, f32[32,32]{1,0:T(8,128)S(1)} %get-tuple-element.71.gram_ref), custom_call_target="tpu_custom_call" | custom-call | tf_op jit(solution)/shard_map/pallas_call | solution.py:28
  57.8 6.6 %all-to-all-done.grams_ref = f32[32,8,128]{2,1,0:T(8,128)S(1)} async-done(((f32[32,8,128]{2,1,0:T(8,128)}), f32[32,8,128]{2,1,0:T(8,128)S(1)}, u32[]{:S(2)}, u32[]{:S(2)}) %all-to-all-start) | async-done | bytes 131104 | tf_op jit(solution)/shard_map/all_to_all | solution.py:520
  64.4 2.0 %shard_map.52 = f32[32,320]{1,0:T(8,128)} custom-call(f32[32,320]{1,0:T(8,128)S(1)} %get-tuple-element.72.image_ref, f32[32,32]{1,0:T(8,128)S(1)} %get-tuple-element.73.inverse_ref, f32[32,8,128]{2,1,0:T(8,128)S(1)} %all-to-all-done.grams_ref), custom_call_target="tpu_custom_call" | custom-call | tf_op jit(solution)/shard_map/pallas_call | solution.py:28
  (13 shorter events, 0.2 us)
Async XLA Ops:
  0.6 10.7 %collective-permute-start.4 = (bf16[320,256]{1,0:T(8,128)(2,1)}, bf16[320,256]{1,0:T(8,128)(2,1)S(1)}, u32[]{:S(2)}, u32[]{:S(2)}) collective-permute-start(bf16[320,256]{1,0:T(8,128)(2,1)} %emb_ref.1), channel_id=1, source_target_pairs={{0,8},{1,9},{4,12},{5,13},{8,0},{9,1},{12,4},{13,5},{2,10},{3,11},... | collective-permute-start | bytes 491528 | tf_op jit(solution)/shard_map/ppermute | solution.py:394
  3.7 10.3 %collective-permute-start.3 = (bf16[320,256]{1,0:T(8,128)(2,1)}, bf16[320,256]{1,0:T(8,128)(2,1)S(1)}, u32[]{:S(2)}, u32[]{:S(2)}) collective-permute-start(bf16[320,256]{1,0:T(8,128)(2,1)} %emb_ref.1), channel_id=1, source_target_pairs={{0,16},{2,18},{16,0},{18,2},{1,17},{3,19},{17,1},{19,3},{4,20},{6,... | collective-permute-start | bytes 491528 | tf_op jit(solution)/shard_map/ppermute | solution.py:394
  6.3 7.8 %collective-permute-start.2 = (bf16[320,256]{1,0:T(8,128)(2,1)}, bf16[320,256]{1,0:T(8,128)(2,1)S(1)}, u32[]{:S(2)}, u32[]{:S(2)}) collective-permute-start(bf16[320,256]{1,0:T(8,128)(2,1)} %emb_ref.1), channel_id=1, source_target_pairs={{0,2},{2,0},{16,18},{18,16},{1,3},{3,1},{17,19},{19,17},{4,6},{6,4... | collective-permute-start | bytes 491528 | tf_op jit(solution)/shard_map/ppermute | solution.py:394
  7.8 6.3 %collective-permute-start.1 = (bf16[320,256]{1,0:T(8,128)(2,1)}, bf16[320,256]{1,0:T(8,128)(2,1)S(1)}, u32[]{:S(2)}, u32[]{:S(2)}) collective-permute-start(bf16[320,256]{1,0:T(8,128)(2,1)} %emb_ref.1), channel_id=1, source_target_pairs={{0,4},{1,5},{4,0},{5,1},{8,12},{9,13},{12,8},{13,9},{2,6},{3,7},{6... | collective-permute-start | bytes 491528 | tf_op jit(solution)/shard_map/ppermute | solution.py:394
  9.3 4.8 %collective-permute-start = (bf16[320,256]{1,0:T(8,128)(2,1)}, bf16[320,256]{1,0:T(8,128)(2,1)S(1)}, u32[]{:S(2)}, u32[]{:S(2)}) collective-permute-start(bf16[320,256]{1,0:T(8,128)(2,1)} %emb_ref.1), channel_id=1, source_target_pairs={{0,1},{1,0},{4,5},{5,4},{8,9},{9,8},{12,13},{13,12},{2,3},{3,2},{6... | collective-permute-start | bytes 491528 | tf_op jit(solution)/shard_map/ppermute | solution.py:394
  9.3 0.9 %copy-start = (bf16[320,256]{1,0:T(8,128)(2,1)S(1)}, bf16[320,256]{1,0:T(8,128)(2,1)}, u32[]{:S(2)}) copy-start(bf16[320,256]{1,0:T(8,128)(2,1)} %emb_ref.1) | copy-start | bytes 491524
  10.3 0.8 %copy-start.1 = (f32[32,320]{1,0:T(8,128)S(1)}, f32[32,320]{1,0:T(8,128)}, u32[]{:S(2)}) copy-start(f32[32,320]{1,0:T(8,128)} %start_ref.1) | copy-start | bytes 122884
  11.3 6.5 %collective-permute-start.5 = (bf16[320,256]{1,0:T(8,128)(2,1)S(1)}, bf16[320,256]{1,0:T(8,128)(2,1)S(1)}, u32[]{:S(2)}, u32[]{:S(2)}) collective-permute-start(bf16[320,256]{1,0:T(8,128)(2,1)S(1)} %collective-permute-done.4.refs_3_), channel_id=1, source_target_pairs={{0,4},{1,5},{4,0},{5,1},{8,12},{9,13},{12,8},{13,9},{2,6},{3,7},{6... | collective-permute-start | bytes 491528 | tf_op jit(solution)/shard_map/ppermute | solution.py:394
  14.1 3.8 %collective-permute-start.6 = (bf16[320,256]{1,0:T(8,128)(2,1)S(1)}, bf16[320,256]{1,0:T(8,128)(2,1)S(1)}, u32[]{:S(2)}, u32[]{:S(2)}) collective-permute-start(bf16[320,256]{1,0:T(8,128)(2,1)S(1)} %collective-permute-done.1.refs_2_), channel_id=1, source_target_pairs={{0,1},{1,0},{4,5},{5,4},{8,9},{9,8},{12,13},{13,12},{2,3},{3,2},{6... | collective-permute-start | bytes 491528 | tf_op jit(solution)/shard_map/ppermute | solution.py:394
  14.2 3.7 %collective-permute-start.7 = (bf16[320,256]{1,0:T(8,128)(2,1)S(1)}, bf16[320,256]{1,0:T(8,128)(2,1)S(1)}, u32[]{:S(2)}, u32[]{:S(2)}) collective-permute-start(bf16[320,256]{1,0:T(8,128)(2,1)S(1)} %collective-permute-done.4.refs_3_), channel_id=1, source_target_pairs={{0,1},{1,0},{4,5},{5,4},{8,9},{9,8},{12,13},{13,12},{2,3},{3,2},{6... | collective-permute-start | bytes 491528 | tf_op jit(solution)/shard_map/ppermute | solution.py:394
  14.7 6.2 %collective-permute-start.8 = (bf16[320,256]{1,0:T(8,128)(2,1)S(1)}, bf16[320,256]{1,0:T(8,128)(2,1)S(1)}, u32[]{:S(2)}, u32[]{:S(2)}) collective-permute-start(bf16[320,256]{1,0:T(8,128)(2,1)S(1)} %collective-permute-done.3.refs_1_), channel_id=1, source_target_pairs={{0,2},{2,0},{16,18},{18,16},{1,3},{3,1},{17,19},{19,17},{4,6},{6,4... | collective-permute-start | bytes 491528 | tf_op jit(solution)/shard_map/ppermute | solution.py:394
  17.9 3.0 %collective-permute-start.9 = (bf16[320,256]{1,0:T(8,128)(2,1)S(1)}, bf16[320,256]{1,0:T(8,128)(2,1)S(1)}, u32[]{:S(2)}, u32[]{:S(2)}) collective-permute-start(bf16[320,256]{1,0:T(8,128)(2,1)S(1)} %collective-permute-done.5.refs_4_), channel_id=1, source_target_pairs={{0,1},{1,0},{4,5},{5,4},{8,9},{9,8},{12,13},{13,12},{2,3},{3,2},{6... | collective-permute-start | bytes 491528 | tf_op jit(solution)/shard_map/ppermute | solution.py:394
  22.5 6.3 %collective-permute-start.12 = (bf16[40,320]{1,0:T(8,128)(2,1)S(1)}, bf16[40,320]{1,0:T(8,128)(2,1)S(1)}, u32[]{:S(2)}, u32[]{:S(2)}) collective-permute-start(bf16[40,320]{1,0:T(8,128)(2,1)S(1)} %get-tuple-element.61), channel_id=1, source_target_pairs={{0,18},{2,16},{16,2},{18,0},{1,19},{3,17},{17,3},{19,1},{4,22},{6,... | collective-permute-start | bytes 76808 | tf_op jit(solution)/shard_map/ppermute | solution.py:394
  23.9 5.3 %collective-permute-start.11 = (bf16[40,320]{1,0:T(8,128)(2,1)S(1)}, bf16[40,320]{1,0:T(8,128)(2,1)S(1)}, u32[]{:S(2)}, u32[]{:S(2)}) collective-permute-start(bf16[40,320]{1,0:T(8,128)(2,1)S(1)} %get-tuple-element.61), channel_id=1, source_target_pairs={{0,16},{2,18},{16,0},{18,2},{1,17},{3,19},{17,1},{19,3},{4,20},{6,... | collective-permute-start | bytes 76808 | tf_op jit(solution)/shard_map/ppermute | solution.py:394
  26.5 3.9 %collective-permute-start.10 = (bf16[40,320]{1,0:T(8,128)(2,1)S(1)}, bf16[40,320]{1,0:T(8,128)(2,1)S(1)}, u32[]{:S(2)}, u32[]{:S(2)}) collective-permute-start(bf16[40,320]{1,0:T(8,128)(2,1)S(1)} %get-tuple-element.61), channel_id=1, source_target_pairs={{0,2},{2,0},{16,18},{18,16},{1,3},{3,1},{17,19},{19,17},{4,6},{6,4... | collective-permute-start | bytes 76808 | tf_op jit(solution)/shard_map/ppermute | solution.py:394
  31.1 1.4 %collective-permute-start.13 = (bf16[4,32,320]{2,1,0:T(8,128)(2,1)S(1)}, bf16[4,32,320]{2,1,0:T(8,128)(2,1)S(1)}, u32[]{:S(2)}, u32[]{:S(2)}) collective-permute-start(bf16[4,32,320]{2,1,0:T(8,128)(2,1)S(1)} %get-tuple-element.64), channel_id=1, source_target_pairs={{0,1},{1,0},{4,5},{5,4},{8,9},{9,8},{12,13},{13,12},{2,3},{3,2},{6... | collective-permute-start | bytes 245768 | tf_op jit(solution)/shard_map/ppermute | solution.py:394
  32.6 6.4 %collective-permute-start.16 = (bf16[32,1408]{1,0:T(8,128)(2,1)S(1)}, bf16[32,1408]{1,0:T(8,128)(2,1)S(1)}, u32[]{:S(2)}, u32[]{:S(2)}) collective-permute-start(bf16[32,1408]{1,0:T(8,128)(2,1)S(1)} %shard_map.46.refs_0_), channel_id=1, source_target_pairs={{0,12},{1,13},{4,8},{5,9},{8,4},{9,5},{12,0},{13,1},{2,14},{3,15},... | collective-permute-start | bytes 270344 | tf_op jit(solution)/shard_map/ppermute | solution.py:394
  34.6 5.6 %collective-permute-start.15 = (bf16[32,1408]{1,0:T(8,128)(2,1)S(1)}, bf16[32,1408]{1,0:T(8,128)(2,1)S(1)}, u32[]{:S(2)}, u32[]{:S(2)}) collective-permute-start(bf16[32,1408]{1,0:T(8,128)(2,1)S(1)} %shard_map.46.refs_0_), channel_id=1, source_target_pairs={{0,8},{1,9},{4,12},{5,13},{8,0},{9,1},{12,4},{13,5},{2,10},{3,11},... | collective-permute-start | bytes 270344 | tf_op jit(solution)/shard_map/ppermute | solution.py:394
  35.6 4.7 %collective-permute-start.14 = (bf16[32,1408]{1,0:T(8,128)(2,1)S(1)}, bf16[32,1408]{1,0:T(8,128)(2,1)S(1)}, u32[]{:S(2)}, u32[]{:S(2)}) collective-permute-start(bf16[32,1408]{1,0:T(8,128)(2,1)S(1)} %shard_map.46.refs_0_), channel_id=1, source_target_pairs={{0,4},{1,5},{4,0},{5,1},{8,12},{9,13},{12,8},{13,9},{2,6},{3,7},{6... | collective-permute-start | bytes 270344 | tf_op jit(solution)/shard_map/ppermute | solution.py:394
  41.0 1.5 %collective-permute-start.17 = (bf16[4,64,384]{2,1,0:T(8,128)(2,1)S(1)}, bf16[4,64,384]{2,1,0:T(8,128)(2,1)S(1)}, u32[]{:S(2)}, u32[]{:S(2)}) collective-permute-start(bf16[4,64,384]{2,1,0:T(8,128)(2,1)S(1)} %shard_map.47.refs_2_.refs_3_), channel_id=1, source_target_pairs={{0,1},{1,0},{4,5},{5,4},{8,9},{9,8},{12,13},{13,12},{2,3},{3,2},{6... | collective-permute-start | bytes 589832 | tf_op jit(solution)/shard_map/ppermute | solution.py:394
  43.9 5.8 %collective-permute-start.18 = (bf16[32,384]{1,0:T(8,128)(2,1)S(1)}, bf16[32,384]{1,0:T(8,128)(2,1)S(1)}, u32[]{:S(2)}, u32[]{:S(2)}) collective-permute-start(bf16[32,384]{1,0:T(8,128)(2,1)S(1)} %get-tuple-element.67), channel_id=1, source_target_pairs={{0,18},{2,16},{16,2},{18,0},{1,19},{3,17},{17,3},{19,1},{4,22},{6,... | collective-permute-start | bytes 73736 | tf_op jit(solution)/shard_map/ppermute | solution.py:394
  45.1 4.7 %collective-permute-start.19 = (bf16[32,384]{1,0:T(8,128)(2,1)S(1)}, bf16[32,384]{1,0:T(8,128)(2,1)S(1)}, u32[]{:S(2)}, u32[]{:S(2)}) collective-permute-start(bf16[32,384]{1,0:T(8,128)(2,1)S(1)} %get-tuple-element.68), channel_id=1, source_target_pairs={{0,16},{2,18},{16,0},{18,2},{1,17},{3,19},{17,1},{19,3},{4,20},{6,... | collective-permute-start | bytes 73736 | tf_op jit(solution)/shard_map/ppermute | solution.py:394
  46.9 3.8 %collective-permute-start.20 = (bf16[32,384]{1,0:T(8,128)(2,1)S(1)}, bf16[32,384]{1,0:T(8,128)(2,1)S(1)}, u32[]{:S(2)}, u32[]{:S(2)}) collective-permute-start(bf16[32,384]{1,0:T(8,128)(2,1)S(1)} %get-tuple-element.69), channel_id=1, source_target_pairs={{0,2},{2,0},{16,18},{18,16},{1,3},{3,1},{17,19},{19,17},{4,6},{6,4... | collective-permute-start | bytes 73736 | tf_op jit(solution)/shard_map/ppermute | solution.py:394
  51.6 12.7 %all-to-all-start = ((f32[32,8,128]{2,1,0:T(8,128)}), f32[32,8,128]{2,1,0:T(8,128)S(1)}, u32[]{:S(2)}, u32[]{:S(2)}) async-start(f32[32,8,128]{2,1,0:T(8,128)} %get-tuple-element.74), calls=%async_computation | async-start | bytes 262144 | tf_op jit(solution)/shard_map/all_to_all | solution.py:520

commit v3 on v2

--- a/solution.py
+++ b/solution.py
@@ -61,6 +61,12 @@
 def own_kernel(emb_ref, start_ref, unit_ref, out_ref):
     unit_ref[...] = unit_rows(emb_ref, 1.0)
     out_ref[...] = start_ref[...].astype(out_ref.dtype)
+
+
+def stack_kernel(first_ref, second_ref, out_ref):
+    half = first_ref.shape[0]
+    out_ref[0:half, :] = first_ref[...]
+    out_ref[half : 2 * half, :] = second_ref[...]
 
 
 def affinity(rows_ref, parts, own, fold_ref, more_ref=None):
@@ -114,10 +120,10 @@
     affinity(rows_ref, parts, own, fold_ref)
 
 
-def rest_kernel(rows_ref, fold_in_ref, even_ref, odd_in_ref, *refs):
-    row_ref, fresh_ref, start_ref = refs[:3]
-    side_tile_ref, even_last_ref, odd_last_ref, sums_ref, send_ref = refs[3:8]
-    last_ref, odd_ref, fold_ref, fold_last_ref = refs[8:]
+def rest_kernel(rows_ref, fold_in_ref, even_ref, odd_in_ref, row_ref, fresh_ref, *refs):
+    start_refs, refs = refs[:-9], refs[-9:]
+    side_tile_ref, even_last_ref, odd_last_ref, sums_ref, send_ref = refs[:5]
+    last_ref, odd_ref, fold_ref, fold_last_ref = refs[5:]
     own = row_ref.shape[0]
     high = odd_in_ref.shape[0]
     odd_ref[0:high, :] = odd_in_ref[...]
@@ -129,7 +135,7 @@
     lines = cut(unfold(fold_ref[...]), own) + [unfold(fold_last_ref[...])]
     sums = jnp.concatenate(lines, axis=0)
     sums_ref[...] = sums
-    parts = [start_ref[...].astype(jnp.float32)]
+    parts = [ref[...].astype(jnp.float32) for ref in start_refs]
     parts += [part.astype(jnp.float32) for part in two_parts(sums)]
     space = send_ref.shape[0] - sum(p.shape[0] for p in parts)
     if space:
@@ -186,18 +192,20 @@
     return parts[0] + parts[1]
 
 
-def first_kernel(*refs):
-    tiles, refs = refs[:3], refs[3:]
-    sums_ref, start_ref, came_refs = refs[0], refs[1], refs[2:-5]
+def first_kernel(held, steps, *refs):
+    tiles, start_refs = refs[:3], refs[3 : 3 + steps]
+    near_ref, sums_refs = refs[3 + steps], refs[4 + steps : -5]
     pieces_ref, left_ref, left_last_ref, degrees_ref, scale_ref = refs[-5:]
-    count, own = start_ref.shape
-    rows = sums_ref.shape[0]
-    sums, starts = [sums_ref[...]], [start_ref[...].astype(jnp.float32)]
-    for ref in came_refs:
-        came = ref[...].astype(jnp.float32)
-        starts.append(came[:count])
-        high, low = (came[count + i * rows : count + (i + 1) * rows] for i in range(2))
-        sums.append(high + low)
+    rows, own = sums_refs[0].shape
+    count = pieces_ref.shape[1]
+    near = near_ref[...].astype(jnp.float32)
+    here = len(held) * count
+    sums = [ref[...] for ref in sums_refs]
+    sums.insert(1, near[here : here + rows] + near[here + rows : here + 2 * rows])
+    blocks = [ref[...].astype(jnp.float32) for ref in start_refs] + [near[:here]]
+    blocks = [b[i : i + count] for b in blocks for i in range(0, b.shape[0], count)]
+    places = held + [m ^ 1 for m in held]
+    starts = [blocks[places.index(j)] for j in range(rows)]
     degrees = []
     for j in range(rows):
         degrees.append(sum(s[j ^ m : (j ^ m) + 1, :] for m, s in enumerate(sums)))
@@ -394,6 +402,11 @@
     return lax.ppermute(value, axes, [(i, i ^ offset) for i in range(size)])
 
 
+def stack(first, second):
+    half, own = first.shape
+    return call(stack_kernel, [((2 * half, own), first.dtype)])(first, second)[0]
+
+
 def local(embeddings, start_vectors):
     rows, cols = lax.axis_size(ROW_SET), lax.axis_size(LANE_SET)
     own, width = embeddings.shape
@@ -426,6 +439,13 @@
         if m.bit_count() > 1:
             row_blocks[m] = swap(row_blocks[m & (m - 1)], ROW_SET, m & -m)
 
+    held, here = [0], [starts]
+    for m in tops[:0:-1]:
+        if len(here) > 1:
+            here = [stack(*here)]
+        here = [here[0], swap(here[0], ROW_SET, m)]
+        held = held + [j ^ m for j in held]
+
     high, deep = (rows - 1) * own, (half - 1) * own
     unit, farthest = lax.optimization_barrier((unit, lane_blocks[even[-1]]))
     lane_blocks[even[-1]] = farthest
@@ -446,7 +466,10 @@
         *[lane_blocks[m] for m in even[1:]],
         *[lane_blocks[m + 1] for m in even[:-1]],
     )
-    lines = count + -(-2 * rows // 8) * 8
+    fold, here[1:], row_blocks[rows - 1] = lax.optimization_barrier(
+        (fold, here[1:], row_blocks[rows - 1])
+    )
+    lines = len(held) * count + -(-2 * rows // 8) * 8
     odd_side, even_last, odd_last, sums, send = call(
         rest_kernel,
         [
@@ -470,14 +493,15 @@
         odd_lanes,
         row_blocks[rows - 1],
         swap(farthest, LANE_SET, 1),
-        starts,
+        *here,
     )
     even_tiles = (even_main, even_last)
     odd_tiles = (odd_main, odd_side, odd_last)
 
-    came = [swap(send, ROW_SET, m) for m in range(1, rows)]
+    near = swap(send, ROW_SET, 1)
+    sums = [sums] + [swap(sums, ROW_SET, m) for m in range(2, rows)]
     other, left, left_last, degrees, scale = call(
-        first_kernel,
+        functools.partial(first_kernel, held, len(here)),
         [
             ((half, count, own), bf16),
             ((count, high), bf16),
@@ -485,7 +509,7 @@
             ((1, own), f32),
             ((1, own), f32),
         ],
-    )(*odd_tiles, sums, starts, *came)
+    )(*odd_tiles, *here, near, *sums)
     other = swap(other, LANE_SET, 1)
     (pieces,) = call(
         same_kernel,

time: 66.6 us -> 66.8 us (level)
  waiting for transfers between devices: 20.9 us -> 21.9 us
  starting transfers between devices: 29.7 us -> 28.9 us
    all_to_all x1, starting transfers between devices: 4.51 us -> 3.35 us  [local(): grams = lax.all_to_all(grams, NAMES, 0, 0, tiled=True)]
    ppermute x21 -> x22, waiting for transfers between devices: 14.4 us -> 15.4 us  [swap(): return lax.ppermute(value, axes, [(i, i ^ offset) for i in range(size)])]
    ppermute x21 -> x22, starting transfers between devices: 25.2 us -> 25.5 us  [swap(): return lax.ppermute(value, axes, [(i, i ^ offset) for i in range(size)])]
  transfers between devices with their start and end apart: 22 -> 23, of which waited for: 16 -> 15; matrix products, arithmetic and copies ran while one was open for 1% -> 1% of each run, Pallas kernels for 8% -> 8%
where the time goes in v3:
time: 66.8 us; the launch traced here: 66.5 us
  starting transfers between devices  28.9 us (43%)
  waiting for transfers between devices  21.9 us (33%)
  Pallas kernels  12.7 us (19%)
  local copies, waits for them, and re-layouts  1.74 us (3%)
  between operations  0.73 us (1%)
    ppermute x22, starting transfers between devices, swap(): return lax.ppermute(value, axes, [(i, i ^ offset) for i in range(size)])  25.5 us
    ppermute x22, waiting for transfers between devices, swap(): return lax.ppermute(value, axes, [(i, i ^ offset) for i in range(size)])  15.4 us
    pallas_call x12, Pallas kernels, run(): pl.pallas_call(kernel, out_shape=[jax.ShapeDtypeStruct(s, d) for s, d in...  12.7 us
    all_to_all x1, waiting for transfers between devices, local(): grams = lax.all_to_all(grams, NAMES, 0, 0, tiled=True)  6.55 us
    all_to_all x1, starting transfers between devices, local(): grams = lax.all_to_all(grams, NAMES, 0, 0, tiled=True)  3.35 us
    unnamed x4, local copies, waits for them, and re-layouts  1.74 us
  transfers between devices with their start and end apart: 23, of which 15 were waited for; matrix products, arithmetic and copies ran while one was open for 1% of the time, Pallas kernels for 8%

profile of v3, /device:TPU:0, one launch (start us, length us, event | category | flops | bytes accessed | tf_op | source)
XLA Modules:
  0.0 66.5 jit_solution(5724913726785150028)
XLA Ops:
  0.6 3.1 %collective-permute-start.4 = (bf16[320,256]{1,0:T(8,128)(2,1)}, bf16[320,256]{1,0:T(8,128)(2,1)S(1)}, u32[]{:S(2)}, u32[]{:S(2)}) collective-permute-start(bf16[320,256]{1,0:T(8,128)(2,1)} %emb_ref.1), channel_id=1, source_target_pairs={{0,8},{1,9},{4,12},{5,13},{8,0},{9,1},{12,4},{13,5},{2,10},{3,11},... | collective-permute-start | bytes 491528 | tf_op jit(solution)/shard_map/ppermute | solution.py:402
  3.7 2.6 %collective-permute-start.3 = (bf16[320,256]{1,0:T(8,128)(2,1)}, bf16[320,256]{1,0:T(8,128)(2,1)S(1)}, u32[]{:S(2)}, u32[]{:S(2)}) collective-permute-start(bf16[320,256]{1,0:T(8,128)(2,1)} %emb_ref.1), channel_id=1, source_target_pairs={{0,16},{2,18},{16,0},{18,2},{1,17},{3,19},{17,1},{19,3},{4,20},{6,... | collective-permute-start | bytes 491528 | tf_op jit(solution)/shard_map/ppermute | solution.py:402
  6.3 1.5 %collective-permute-start.2 = (bf16[320,256]{1,0:T(8,128)(2,1)}, bf16[320,256]{1,0:T(8,128)(2,1)S(1)}, u32[]{:S(2)}, u32[]{:S(2)}) collective-permute-start(bf16[320,256]{1,0:T(8,128)(2,1)} %emb_ref.1), channel_id=1, source_target_pairs={{0,2},{2,0},{16,18},{18,16},{1,3},{3,1},{17,19},{19,17},{4,6},{6,4... | collective-permute-start | bytes 491528 | tf_op jit(solution)/shard_map/ppermute | solution.py:402
  7.8 1.5 %collective-permute-start.1 = (bf16[320,256]{1,0:T(8,128)(2,1)}, bf16[320,256]{1,0:T(8,128)(2,1)S(1)}, u32[]{:S(2)}, u32[]{:S(2)}) collective-permute-start(bf16[320,256]{1,0:T(8,128)(2,1)} %emb_ref.1), channel_id=1, source_target_pairs={{0,4},{1,5},{4,0},{5,1},{8,12},{9,13},{12,8},{13,9},{2,6},{3,7},{6... | collective-permute-start | bytes 491528 | tf_op jit(solution)/shard_map/ppermute | solution.py:402
  9.3 0.9 %copy-done = bf16[320,256]{1,0:T(8,128)(2,1)S(1)} copy-done((bf16[320,256]{1,0:T(8,128)(2,1)S(1)}, bf16[320,256]{1,0:T(8,128)(2,1)}, u32[]{:S(2)}) %copy-start) | copy-done | bytes 163864
  10.3 0.8 %copy-done.1 = f32[32,320]{1,0:T(8,128)S(1)} copy-done((f32[32,320]{1,0:T(8,128)S(1)}, f32[32,320]{1,0:T(8,128)}, u32[]{:S(2)}) %copy-start.1) | copy-done | bytes 40984
  11.1 0.1 shard_map.41
  11.2 0.1 collective-permute-done.4.refs_3_
  11.3 1.8 %collective-permute-start.5 = (bf16[320,256]{1,0:T(8,128)(2,1)S(1)}, bf16[320,256]{1,0:T(8,128)(2,1)S(1)}, u32[]{:S(2)}, u32[]{:S(2)}) collective-permute-start(bf16[320,256]{1,0:T(8,128)(2,1)S(1)} %collective-permute-done.4.refs_3_), channel_id=1, source_target_pairs={{0,4},{1,5},{4,0},{5,1},{8,12},{9,13},{12,8},{13,9},{2,6},{3,7},{6... | collective-permute-start | bytes 491528 | tf_op jit(solution)/shard_map/ppermute | solution.py:402
  13.2 0.9 %collective-permute-done.3.refs_1_ = bf16[320,256]{1,0:T(8,128)(2,1)S(1)} collective-permute-done((bf16[320,256]{1,0:T(8,128)(2,1)}, bf16[320,256]{1,0:T(8,128)(2,1)S(1)}, u32[]{:S(2)}, u32[]{:S(2)}) %collective-permute-start.3) | collective-permute-done | bytes 163872 | tf_op jit(solution)/shard_map/ppermute | solution.py:402
  14.2 0.5 collective-permute-start.7
  14.7 1.5 %collective-permute-start.9 = (bf16[320,256]{1,0:T(8,128)(2,1)S(1)}, bf16[320,256]{1,0:T(8,128)(2,1)S(1)}, u32[]{:S(2)}, u32[]{:S(2)}) collective-permute-start(bf16[320,256]{1,0:T(8,128)(2,1)S(1)} %collective-permute-done.3.refs_1_), channel_id=1, source_target_pairs={{0,2},{2,0},{16,18},{18,16},{1,3},{3,1},{17,19},{19,17},{4,6},{6,4... | collective-permute-start | bytes 491528 | tf_op jit(solution)/shard_map/ppermute | solution.py:402
  16.1 1.7 %collective-permute-done.5.refs_4_ = bf16[320,256]{1,0:T(8,128)(2,1)S(1)} collective-permute-done((bf16[320,256]{1,0:T(8,128)(2,1)S(1)}, bf16[320,256]{1,0:T(8,128)(2,1)S(1)}, u32[]{:S(2)}, u32[]{:S(2)}) %collective-permute-start.5) | collective-permute-done | bytes 163872 | tf_op jit(solution)/shard_map/ppermute | solution.py:402
  17.9 0.3 collective-permute-start.8
  18.2 2.1 %shard_map.42 = (bf16[960,256]{1,0:T(8,128)(2,1)S(1)}, bf16[1280,256]{1,0:T(8,128)(2,1)S(1)}, bf16[960,256]{1,0:T(8,128)(2,1)S(1)}, bf16[960,1280]{1,0:T(8,128)(...) custom-call(bf16[320,256]{1,0:T(8,128)(2,1)S(1)} %get-tuple-element.47.unit_ref, ...), custom_call_target="tpu_custom_call" | custom-call | flops 1101004800 | tf_op jit(solution)/shard_map/pallas_call | solution.py:28
  20.3 2.5 %collective-permute-done.8.refs_1_.refs_4_ = bf16[32,320]{1,0:T(8,128)(2,1)S(1)} collective-permute-done((bf16[32,320]{1,0:T(8,128)(2,1)S(1)}, bf16[32,320]{1,0:T(8,128)(2,1)S(1)}, u32[]{:S(2)}, u32[]{:S(2)}) %collective-permute-start.8) | collective-permute-done | bytes 20512 | tf_op jit(solution)/shard_map/ppermute | solution.py:402
  22.8 1.7 %shard_map.43 = (bf16[960,320]{1,0:T(8,128)(2,1)S(1)}, bf16[320,1280]{1,0:T(8,128)(2,1)S(1)}, bf16[320,1280]{1,0:T(8,128)(2,1)S(1)}, f32[4,320]{1,0:T(4,128)S(1)}, bf16[72,320]{1,0:T(8,128)(2,1)S(1)}) custom-call(bf16[960,256]{1,0:T(8,128)(2,1)S(1)} %get-tuple-element.54.rows_ref, f32[960,128]{1,0:T(8,128)S(1)} %get-tuple-element.57.fold_in_ref, ...), custom_call_target="tpu_custom_call" | custom-call | flops 576716800 | tf_op jit(solution)/shard_map/pallas_call | solution.py:28
  24.5 0.7 collective-permute-start.11
  25.2 1.1 %collective-permute-start.13 = (f32[4,320]{1,0:T(4,128)S(1)}, f32[4,320]{1,0:T(4,128)S(1)}, u32[]{:S(2)}, u32[]{:S(2)}) collective-permute-start(f32[4,320]{1,0:T(4,128)S(1)} %get-tuple-element.67.refs_6_), channel_id=1, source_target_pairs={{0,18},{2,16},{16,2},{18,0},{1,19},{3,17},{17,3},{19,1},{4,22},{6,... | collective-permute-start | bytes 15368 | tf_op jit(solution)/shard_map/ppermute | solution.py:402
  26.3 2.7 %collective-permute-start.12 = (f32[4,320]{1,0:T(4,128)S(1)}, f32[4,320]{1,0:T(4,128)S(1)}, u32[]{:S(2)}, u32[]{:S(2)}) collective-permute-start(f32[4,320]{1,0:T(4,128)S(1)} %get-tuple-element.67.refs_6_), channel_id=1, source_target_pairs={{0,16},{2,18},{16,0},{18,2},{1,17},{3,19},{17,1},{19,3},{4,20},{6,... | collective-permute-start | bytes 15368 | tf_op jit(solution)/shard_map/ppermute | solution.py:402
  29.0 1.6 %collective-permute-done.13.refs_8_ = f32[4,320]{1,0:T(4,128)S(1)} collective-permute-done((f32[4,320]{1,0:T(4,128)S(1)}, f32[4,320]{1,0:T(4,128)S(1)}, u32[]{:S(2)}, u32[]{:S(2)}) %collective-permute-start.13) | collective-permute-done | bytes 5152 | tf_op jit(solution)/shard_map/ppermute | solution.py:402
  30.6 0.2 collective-permute-done.12.refs_7_
  30.8 0.8 %shard_map.44 = (bf16[4,32,320]{2,1,0:T(8,128)(2,1)S(1)}, bf16[32,960]{1,0:T(8,128)(2,1)S(1)}, bf16[32,320]{1,0:T(8,128)(2,1)S(1)}, f32[1,320]{1,0:T(1,128)S(1)}, f32[1,320]{1,0:T(1,128)S(1)}) custom-call(bf16[960,960]{1,0:T(8,128)(2,1)S(1)} %get-tuple-element.53.refs_0_, bf16[960,320]{1,0:T(8,128)(2,1)S(1)} %get-tuple-element.62.refs_1_, ...), custom_call_target="tpu_custom_call" | custom-call | tf_op jit(solution)/shard_map/pallas_call | solution.py:28
  31.7 0.7 %shard_map.45.pieces_ref = f32[4,32,320]{2,1,0:T(8,128)S(1)} custom-call(bf16[960,1280]{1,0:T(8,128)(2,1)S(1)} %get-tuple-element.64.refs_0_, bf16[320,1280]{1,0:T(8,128)(2,1)S(1)} %get-tuple-element.65.refs_1_, bf16[32,960]{1,0:T(8,128)(2,1)S(1)} %get-tuple-element.68.refs_2_, bf16[32,320]{1,0:T(8,128)(2,1)S(1)} %get-tuple-element.69.refs_3_), custom_call_target="tpu_custom_call" | custom-call | flops 104857600 | tf_op jit(solution)/shard_map/pallas_call | solution.py:28
  32.4 0.6 collective-permute-done.14.other_ref
  33.0 0.1 shard_map.46.refs_0_
  33.0 2.8 %collective-permute-start.17 = (bf16[32,1408]{1,0:T(8,128)(2,1)S(1)}, bf16[32,1408]{1,0:T(8,128)(2,1)S(1)}, u32[]{:S(2)}, u32[]{:S(2)}) collective-permute-start(bf16[32,1408]{1,0:T(8,128)(2,1)S(1)} %shard_map.46.refs_0_), channel_id=1, source_target_pairs={{0,12},{1,13},{4,8},{5,9},{8,4},{9,5},{12,0},{13,1},{2,14},{3,15},... | collective-permute-start | bytes 270344 | tf_op jit(solution)/shard_map/ppermute | solution.py:402
  35.8 0.1 collective-permute-start.16
  35.9 0.7 %collective-permute-start.15 = (bf16[32,1408]{1,0:T(8,128)(2,1)S(1)}, bf16[32,1408]{1,0:T(8,128)(2,1)S(1)}, u32[]{:S(2)}, u32[]{:S(2)}) collective-permute-start(bf16[32,1408]{1,0:T(8,128)(2,1)S(1)} %shard_map.46.refs_0_), channel_id=1, source_target_pairs={{0,4},{1,5},{4,0},{5,1},{8,12},{9,13},{12,8},{13,9},{2,6},{3,7},{6... | collective-permute-start | bytes 270344 | tf_op jit(solution)/shard_map/ppermute | solution.py:402
  36.6 2.7 %collective-permute-done.17.refs_3_ = bf16[32,1408]{1,0:T(8,128)(2,1)S(1)} collective-permute-done((bf16[32,1408]{1,0:T(8,128)(2,1)S(1)}, bf16[32,1408]{1,0:T(8,128)(2,1)S(1)}, u32[]{:S(2)}, u32[]{:S(2)}) %collective-permute-start.17) | collective-permute-done | bytes 90144 | tf_op jit(solution)/shard_map/ppermute | solution.py:402
  39.3 1.2 %collective-permute-done.16.refs_2_ = bf16[32,1408]{1,0:T(8,128)(2,1)S(1)} collective-permute-done((bf16[32,1408]{1,0:T(8,128)(2,1)S(1)}, bf16[32,1408]{1,0:T(8,128)(2,1)S(1)}, u32[]{:S(2)}, u32[]{:S(2)}) %collective-permute-start.16) | collective-permute-done | bytes 90144 | tf_op jit(solution)/shard_map/ppermute | solution.py:402
  40.5 0.2 collective-permute-done.15.refs_1_
  40.7 0.7 shard_map.47.refs_2_.refs_3_
  41.4 1.2 %shard_map.48.refs_5_ = f32[32,1280]{1,0:T(8,128)S(1)} custom-call(bf16[960,1280]{1,0:T(8,128)(2,1)S(1)} %get-tuple-element.64.refs_0_, bf16[320,1280]{1,0:T(8,128)(2,1)S(1)} %get-tuple-element.65.refs_1_, bf16[4,64,384]{2,1,0:T(8,128)(2,1)S(1)} %shard_map.47.refs_2_.refs_3_), custom_call_target="tpu_custom_call" | custom-call | flops 209715200 | tf_op jit(solution)/shard_map/pallas_call | solution.py:28
  42.6 0.3 collective-permute-done.18.refs_4_
  42.8 1.4 %shard_map.49 = (f32[32,384]{1,0:T(8,128)S(1)}, bf16[32,384]{1,0:T(8,128)(2,1)S(1)}, bf16[32,384]{1,0:T(8,128)(2,1)S(1)}, bf16[32,384]{1,0:T(8,128)(2,1)S(1)}) custom-call(bf16[960,960]{1,0:T(8,128)(2,1)S(1)} %get-tuple-element.53.refs_0_, bf16[960,320]{1,0:T(8,128)(2,1)S(1)} %get-tuple-element.62.refs_1_, bf16[320,1280]{1,0:T(8,128)(2,1)S(1)} %get-tuple-element.63.refs_2_, ...), custom_call_target="tpu_custom_call" | custom-call | tf_op jit(solution)/shard_map/pallas_call | solution.py:28
  44.2 2.9 %collective-permute-start.19 = (bf16[32,384]{1,0:T(8,128)(2,1)S(1)}, bf16[32,384]{1,0:T(8,128)(2,1)S(1)}, u32[]{:S(2)}, u32[]{:S(2)}) collective-permute-start(bf16[32,384]{1,0:T(8,128)(2,1)S(1)} %get-tuple-element.73), channel_id=1, source_target_pairs={{0,18},{2,16},{16,2},{18,0},{1,19},{3,17},{17,3},{19,1},{4,22},{6,... | collective-permute-start | bytes 73736 | tf_op jit(solution)/shard_map/ppermute | solution.py:402
  47.1 1.0 %collective-permute-start.20 = (bf16[32,384]{1,0:T(8,128)(2,1)S(1)}, bf16[32,384]{1,0:T(8,128)(2,1)S(1)}, u32[]{:S(2)}, u32[]{:S(2)}) collective-permute-start(bf16[32,384]{1,0:T(8,128)(2,1)S(1)} %get-tuple-element.74), channel_id=1, source_target_pairs={{0,16},{2,18},{16,0},{18,2},{1,17},{3,19},{17,1},{19,3},{4,20},{6,... | collective-permute-start | bytes 73736 | tf_op jit(solution)/shard_map/ppermute | solution.py:402
  48.1 0.5 collective-permute-start.21
  48.7 1.2 %collective-permute-done.19.refs_1_ = bf16[32,384]{1,0:T(8,128)(2,1)S(1)} collective-permute-done((bf16[32,384]{1,0:T(8,128)(2,1)S(1)}, bf16[32,384]{1,0:T(8,128)(2,1)S(1)}, u32[]{:S(2)}, u32[]{:S(2)}) %collective-permute-start.19) | collective-permute-done | bytes 24608 | tf_op jit(solution)/shard_map/ppermute | solution.py:402
  49.9 1.9 %collective-permute-done.20.refs_2_ = bf16[32,384]{1,0:T(8,128)(2,1)S(1)} collective-permute-done((bf16[32,384]{1,0:T(8,128)(2,1)S(1)}, bf16[32,384]{1,0:T(8,128)(2,1)S(1)}, u32[]{:S(2)}, u32[]{:S(2)}) %collective-permute-start.20) | collective-permute-done | bytes 24608 | tf_op jit(solution)/shard_map/ppermute | solution.py:402
  51.9 0.1 collective-permute-done.21.refs_3_
  52.0 0.9 %shard_map.50 = (f32[32,320]{1,0:T(8,128)S(1)}, f32[32,32]{1,0:T(8,128)S(1)}, f32[32,8,128]{2,1,0:T(8,128)}) custom-call(f32[32,384]{1,0:T(8,128)S(1)} %get-tuple-element.72.refs_0_, bf16[32,384]{1,0:T(8,128)(2,1)S(1)} %collective-permute-done.19.refs_1_, bf16[32,384]{1,0:T(8,128)(2,1)S(1)} %collective-permute-done.20.refs_2_, ...), custom_call_target="tpu_custom_call" | custom-call | tf_op jit(solution)/shard_map/pallas_call | solution.py:28
  52.9 3.4 %all-to-all-start = ((f32[32,8,128]{2,1,0:T(8,128)}), f32[32,8,128]{2,1,0:T(8,128)S(1)}, u32[]{:S(2)}, u32[]{:S(2)}) async-start(f32[32,8,128]{2,1,0:T(8,128)} %get-tuple-element.80), calls=%async_computation | async-start | bytes 262144 | tf_op jit(solution)/shard_map/all_to_all | solution.py:544
  56.3 0.6 reduce
  56.8 1.1 %shard_map.51 = (f32[32,320]{1,0:T(8,128)S(1)}, f32[32,32]{1,0:T(8,128)S(1)}) custom-call(f32[32,320]{1,0:T(8,128)S(1)} %get-tuple-element.76.image_ref, f32[32,32]{1,0:T(8,128)S(1)} %get-tuple-element.77.gram_ref), custom_call_target="tpu_custom_call" | custom-call | tf_op jit(solution)/shard_map/pallas_call | solution.py:28
  57.9 6.6 %all-to-all-done.grams_ref = f32[32,8,128]{2,1,0:T(8,128)S(1)} async-done(((f32[32,8,128]{2,1,0:T(8,128)}), f32[32,8,128]{2,1,0:T(8,128)S(1)}, u32[]{:S(2)}, u32[]{:S(2)}) %all-to-all-start) | async-done | bytes 131104 | tf_op jit(solution)/shard_map/all_to_all | solution.py:544
  64.5 2.0 %shard_map.52 = f32[32,320]{1,0:T(8,128)} custom-call(f32[32,320]{1,0:T(8,128)S(1)} %get-tuple-element.78.image_ref, f32[32,32]{1,0:T(8,128)S(1)} %get-tuple-element.79.inverse_ref, f32[32,8,128]{2,1,0:T(8,128)S(1)} %all-to-all-done.grams_ref), custom_call_target="tpu_custom_call" | custom-call | tf_op jit(solution)/shard_map/pallas_call | solution.py:28
  (15 shorter events, 0.2 us)
Async XLA Ops:
  0.6 10.7 %collective-permute-start.4 = (bf16[320,256]{1,0:T(8,128)(2,1)}, bf16[320,256]{1,0:T(8,128)(2,1)S(1)}, u32[]{:S(2)}, u32[]{:S(2)}) collective-permute-start(bf16[320,256]{1,0:T(8,128)(2,1)} %emb_ref.1), channel_id=1, source_target_pairs={{0,8},{1,9},{4,12},{5,13},{8,0},{9,1},{12,4},{13,5},{2,10},{3,11},... | collective-permute-start | bytes 491528 | tf_op jit(solution)/shard_map/ppermute | solution.py:402
  3.7 10.3 %collective-permute-start.3 = (bf16[320,256]{1,0:T(8,128)(2,1)}, bf16[320,256]{1,0:T(8,128)(2,1)S(1)}, u32[]{:S(2)}, u32[]{:S(2)}) collective-permute-start(bf16[320,256]{1,0:T(8,128)(2,1)} %emb_ref.1), channel_id=1, source_target_pairs={{0,16},{2,18},{16,0},{18,2},{1,17},{3,19},{17,1},{19,3},{4,20},{6,... | collective-permute-start | bytes 491528 | tf_op jit(solution)/shard_map/ppermute | solution.py:402
  6.3 7.8 %collective-permute-start.2 = (bf16[320,256]{1,0:T(8,128)(2,1)}, bf16[320,256]{1,0:T(8,128)(2,1)S(1)}, u32[]{:S(2)}, u32[]{:S(2)}) collective-permute-start(bf16[320,256]{1,0:T(8,128)(2,1)} %emb_ref.1), channel_id=1, source_target_pairs={{0,2},{2,0},{16,18},{18,16},{1,3},{3,1},{17,19},{19,17},{4,6},{6,4... | collective-permute-start | bytes 491528 | tf_op jit(solution)/shard_map/ppermute | solution.py:402
  7.8 6.3 %collective-permute-start.1 = (bf16[320,256]{1,0:T(8,128)(2,1)}, bf16[320,256]{1,0:T(8,128)(2,1)S(1)}, u32[]{:S(2)}, u32[]{:S(2)}) collective-permute-start(bf16[320,256]{1,0:T(8,128)(2,1)} %emb_ref.1), channel_id=1, source_target_pairs={{0,4},{1,5},{4,0},{5,1},{8,12},{9,13},{12,8},{13,9},{2,6},{3,7},{6... | collective-permute-start | bytes 491528 | tf_op jit(solution)/shard_map/ppermute | solution.py:402
  9.3 4.8 %collective-permute-start = (bf16[320,256]{1,0:T(8,128)(2,1)}, bf16[320,256]{1,0:T(8,128)(2,1)S(1)}, u32[]{:S(2)}, u32[]{:S(2)}) collective-permute-start(bf16[320,256]{1,0:T(8,128)(2,1)} %emb_ref.1), channel_id=1, source_target_pairs={{0,1},{1,0},{4,5},{5,4},{8,9},{9,8},{12,13},{13,12},{2,3},{3,2},{6... | collective-permute-start | bytes 491528 | tf_op jit(solution)/shard_map/ppermute | solution.py:402
  9.3 0.9 %copy-start = (bf16[320,256]{1,0:T(8,128)(2,1)S(1)}, bf16[320,256]{1,0:T(8,128)(2,1)}, u32[]{:S(2)}) copy-start(bf16[320,256]{1,0:T(8,128)(2,1)} %emb_ref.1) | copy-start | bytes 491524
  10.3 0.8 %copy-start.1 = (f32[32,320]{1,0:T(8,128)S(1)}, f32[32,320]{1,0:T(8,128)}, u32[]{:S(2)}) copy-start(f32[32,320]{1,0:T(8,128)} %start_ref.1) | copy-start | bytes 122884
  11.3 6.5 %collective-permute-start.5 = (bf16[320,256]{1,0:T(8,128)(2,1)S(1)}, bf16[320,256]{1,0:T(8,128)(2,1)S(1)}, u32[]{:S(2)}, u32[]{:S(2)}) collective-permute-start(bf16[320,256]{1,0:T(8,128)(2,1)S(1)} %collective-permute-done.4.refs_3_), channel_id=1, source_target_pairs={{0,4},{1,5},{4,0},{5,1},{8,12},{9,13},{12,8},{13,9},{2,6},{3,7},{6... | collective-permute-start | bytes 491528 | tf_op jit(solution)/shard_map/ppermute | solution.py:402
  14.1 4.1 %collective-permute-start.6 = (bf16[320,256]{1,0:T(8,128)(2,1)S(1)}, bf16[320,256]{1,0:T(8,128)(2,1)S(1)}, u32[]{:S(2)}, u32[]{:S(2)}) collective-permute-start(bf16[320,256]{1,0:T(8,128)(2,1)S(1)} %collective-permute-done.1.refs_2_), channel_id=1, source_target_pairs={{0,1},{1,0},{4,5},{5,4},{8,9},{9,8},{12,13},{13,12},{2,3},{3,2},{6... | collective-permute-start | bytes 491528 | tf_op jit(solution)/shard_map/ppermute | solution.py:402
  14.2 4.1 %collective-permute-start.7 = (bf16[320,256]{1,0:T(8,128)(2,1)S(1)}, bf16[320,256]{1,0:T(8,128)(2,1)S(1)}, u32[]{:S(2)}, u32[]{:S(2)}) collective-permute-start(bf16[320,256]{1,0:T(8,128)(2,1)S(1)} %collective-permute-done.4.refs_3_), channel_id=1, source_target_pairs={{0,1},{1,0},{4,5},{5,4},{8,9},{9,8},{12,13},{13,12},{2,3},{3,2},{6... | collective-permute-start | bytes 491528 | tf_op jit(solution)/shard_map/ppermute | solution.py:402
  14.7 8.2 %collective-permute-start.9 = (bf16[320,256]{1,0:T(8,128)(2,1)S(1)}, bf16[320,256]{1,0:T(8,128)(2,1)S(1)}, u32[]{:S(2)}, u32[]{:S(2)}) collective-permute-start(bf16[320,256]{1,0:T(8,128)(2,1)S(1)} %collective-permute-done.3.refs_1_), channel_id=1, source_target_pairs={{0,2},{2,0},{16,18},{18,16},{1,3},{3,1},{17,19},{19,17},{4,6},{6,4... | collective-permute-start | bytes 491528 | tf_op jit(solution)/shard_map/ppermute | solution.py:402
  17.9 4.9 %collective-permute-start.10 = (bf16[320,256]{1,0:T(8,128)(2,1)S(1)}, bf16[320,256]{1,0:T(8,128)(2,1)S(1)}, u32[]{:S(2)}, u32[]{:S(2)}) collective-permute-start(bf16[320,256]{1,0:T(8,128)(2,1)S(1)} %collective-permute-done.5.refs_4_), channel_id=1, source_target_pairs={{0,1},{1,0},{4,5},{5,4},{8,9},{9,8},{12,13},{13,12},{2,3},{3,2},{6... | collective-permute-start | bytes 491528 | tf_op jit(solution)/shard_map/ppermute | solution.py:402
  17.9 4.9 %collective-permute-start.8 = (bf16[32,320]{1,0:T(8,128)(2,1)S(1)}, bf16[32,320]{1,0:T(8,128)(2,1)S(1)}, u32[]{:S(2)}, u32[]{:S(2)}) collective-permute-start(bf16[32,320]{1,0:T(8,128)(2,1)S(1)} %get-tuple-element.56.refs_0_.refs_3_), channel_id=1, source_target_pairs={{0,16},{2,18},{16,0},{18,2},{1,17},{3,19},{17,1},{19,3},{4,20},{6,... | collective-permute-start | bytes 61448 | tf_op jit(solution)/shard_map/ppermute | solution.py:402
  24.5 6.3 %collective-permute-start.11 = (bf16[72,320]{1,0:T(8,128)(2,1)S(1)}, bf16[72,320]{1,0:T(8,128)(2,1)S(1)}, u32[]{:S(2)}, u32[]{:S(2)}) collective-permute-start(bf16[72,320]{1,0:T(8,128)(2,1)S(1)} %get-tuple-element.66), channel_id=1, source_target_pairs={{0,2},{2,0},{16,18},{18,16},{1,3},{3,1},{17,19},{19,17},{4,6},{6,4... | collective-permute-start | bytes 138248 | tf_op jit(solution)/shard_map/ppermute | solution.py:402
  25.2 5.4 %collective-permute-start.13 = (f32[4,320]{1,0:T(4,128)S(1)}, f32[4,320]{1,0:T(4,128)S(1)}, u32[]{:S(2)}, u32[]{:S(2)}) collective-permute-start(f32[4,320]{1,0:T(4,128)S(1)} %get-tuple-element.67.refs_6_), channel_id=1, source_target_pairs={{0,18},{2,16},{16,2},{18,0},{1,19},{3,17},{17,3},{19,1},{4,22},{6,... | collective-permute-start | bytes 15368 | tf_op jit(solution)/shard_map/ppermute | solution.py:402
  26.3 4.5 %collective-permute-start.12 = (f32[4,320]{1,0:T(4,128)S(1)}, f32[4,320]{1,0:T(4,128)S(1)}, u32[]{:S(2)}, u32[]{:S(2)}) collective-permute-start(f32[4,320]{1,0:T(4,128)S(1)} %get-tuple-element.67.refs_6_), channel_id=1, source_target_pairs={{0,16},{2,18},{16,0},{18,2},{1,17},{3,19},{17,1},{19,3},{4,20},{6,... | collective-permute-start | bytes 15368 | tf_op jit(solution)/shard_map/ppermute | solution.py:402
  31.6 1.4 %collective-permute-start.14 = (bf16[4,32,320]{2,1,0:T(8,128)(2,1)S(1)}, bf16[4,32,320]{2,1,0:T(8,128)(2,1)S(1)}, u32[]{:S(2)}, u32[]{:S(2)}) collective-permute-start(bf16[4,32,320]{2,1,0:T(8,128)(2,1)S(1)} %get-tuple-element.70), channel_id=1, source_target_pairs={{0,1},{1,0},{4,5},{5,4},{8,9},{9,8},{12,13},{13,12},{2,3},{3,2},{6... | collective-permute-start | bytes 245768 | tf_op jit(solution)/shard_map/ppermute | solution.py:402
  33.0 6.2 %collective-permute-start.17 = (bf16[32,1408]{1,0:T(8,128)(2,1)S(1)}, bf16[32,1408]{1,0:T(8,128)(2,1)S(1)}, u32[]{:S(2)}, u32[]{:S(2)}) collective-permute-start(bf16[32,1408]{1,0:T(8,128)(2,1)S(1)} %shard_map.46.refs_0_), channel_id=1, source_target_pairs={{0,12},{1,13},{4,8},{5,9},{8,4},{9,5},{12,0},{13,1},{2,14},{3,15},... | collective-permute-start | bytes 270344 | tf_op jit(solution)/shard_map/ppermute | solution.py:402
  35.8 4.7 %collective-permute-start.16 = (bf16[32,1408]{1,0:T(8,128)(2,1)S(1)}, bf16[32,1408]{1,0:T(8,128)(2,1)S(1)}, u32[]{:S(2)}, u32[]{:S(2)}) collective-permute-start(bf16[32,1408]{1,0:T(8,128)(2,1)S(1)} %shard_map.46.refs_0_), channel_id=1, source_target_pairs={{0,8},{1,9},{4,12},{5,13},{8,0},{9,1},{12,4},{13,5},{2,10},{3,11},... | collective-permute-start | bytes 270344 | tf_op jit(solution)/shard_map/ppermute | solution.py:402
  35.9 4.8 %collective-permute-start.15 = (bf16[32,1408]{1,0:T(8,128)(2,1)S(1)}, bf16[32,1408]{1,0:T(8,128)(2,1)S(1)}, u32[]{:S(2)}, u32[]{:S(2)}) collective-permute-start(bf16[32,1408]{1,0:T(8,128)(2,1)S(1)} %shard_map.46.refs_0_), channel_id=1, source_target_pairs={{0,4},{1,5},{4,0},{5,1},{8,12},{9,13},{12,8},{13,9},{2,6},{3,7},{6... | collective-permute-start | bytes 270344 | tf_op jit(solution)/shard_map/ppermute | solution.py:402
  41.3 1.5 %collective-permute-start.18 = (bf16[4,64,384]{2,1,0:T(8,128)(2,1)S(1)}, bf16[4,64,384]{2,1,0:T(8,128)(2,1)S(1)}, u32[]{:S(2)}, u32[]{:S(2)}) collective-permute-start(bf16[4,64,384]{2,1,0:T(8,128)(2,1)S(1)} %shard_map.47.refs_2_.refs_3_), channel_id=1, source_target_pairs={{0,1},{1,0},{4,5},{5,4},{8,9},{9,8},{12,13},{13,12},{2,3},{3,2},{6... | collective-permute-start | bytes 589832 | tf_op jit(solution)/shard_map/ppermute | solution.py:402
  44.2 5.7 %collective-permute-start.19 = (bf16[32,384]{1,0:T(8,128)(2,1)S(1)}, bf16[32,384]{1,0:T(8,128)(2,1)S(1)}, u32[]{:S(2)}, u32[]{:S(2)}) collective-permute-start(bf16[32,384]{1,0:T(8,128)(2,1)S(1)} %get-tuple-element.73), channel_id=1, source_target_pairs={{0,18},{2,16},{16,2},{18,0},{1,19},{3,17},{17,3},{19,1},{4,22},{6,... | collective-permute-start | bytes 73736 | tf_op jit(solution)/shard_map/ppermute | solution.py:402
  47.1 4.7 %collective-permute-start.20 = (bf16[32,384]{1,0:T(8,128)(2,1)S(1)}, bf16[32,384]{1,0:T(8,128)(2,1)S(1)}, u32[]{:S(2)}, u32[]{:S(2)}) collective-permute-start(bf16[32,384]{1,0:T(8,128)(2,1)S(1)} %get-tuple-element.74), channel_id=1, source_target_pairs={{0,16},{2,18},{16,0},{18,2},{1,17},{3,19},{17,1},{19,3},{4,20},{6,... | collective-permute-start | bytes 73736 | tf_op jit(solution)/shard_map/ppermute | solution.py:402
  48.1 3.8 %collective-permute-start.21 = (bf16[32,384]{1,0:T(8,128)(2,1)S(1)}, bf16[32,384]{1,0:T(8,128)(2,1)S(1)}, u32[]{:S(2)}, u32[]{:S(2)}) collective-permute-start(bf16[32,384]{1,0:T(8,128)(2,1)S(1)} %get-tuple-element.75), channel_id=1, source_target_pairs={{0,2},{2,0},{16,18},{18,16},{1,3},{3,1},{17,19},{19,17},{4,6},{6,4... | collective-permute-start | bytes 73736 | tf_op jit(solution)/shard_map/ppermute | solution.py:402
  52.9 11.6 %all-to-all-start = ((f32[32,8,128]{2,1,0:T(8,128)}), f32[32,8,128]{2,1,0:T(8,128)S(1)}, u32[]{:S(2)}, u32[]{:S(2)}) async-start(f32[32,8,128]{2,1,0:T(8,128)} %get-tuple-element.80), calls=%async_computation | async-start | bytes 262144 | tf_op jit(solution)/shard_map/all_to_all | solution.py:544

commit v4 on v3

--- a/solution.py
+++ b/solution.py
@@ -447,7 +447,7 @@
         held = held + [j ^ m for j in held]
 
     high, deep = (rows - 1) * own, (half - 1) * own
-    unit, farthest = lax.optimization_barrier((unit, lane_blocks[even[-1]]))
+    unit, here[1:], farthest = lax.optimization_barrier((unit, here[1:], lane_blocks[even[-1]]))
     lane_blocks[even[-1]] = farthest
     main_rows, even_lanes, odd_lanes, even_main, odd_main, fold = call(
         functools.partial(main_kernel, rows - 1),
@@ -465,9 +465,6 @@
         *[row_blocks[m] for m in range(1, rows - 1)],
         *[lane_blocks[m] for m in even[1:]],
         *[lane_blocks[m + 1] for m in even[:-1]],
-    )
-    fold, here[1:], row_blocks[rows - 1] = lax.optimization_barrier(
-        (fold, here[1:], row_blocks[rows - 1])
     )
     lines = len(held) * count + -(-2 * rows // 8) * 8
     odd_side, even_last, odd_last, sums, send = call(

time: 66.8 us -> 67.6 us (1.012)
  transfers between devices with their start and end apart: 23 -> 23, of which waited for: 15 -> 14; matrix products, arithmetic and copies ran while one was open for 1% -> 1% of each run, Pallas kernels for 8% -> 8%
where the time goes in v4:
time: 67.6 us; the launch traced here: 67.3 us
  starting transfers between devices  29.1 us (43%)
  waiting for transfers between devices  22.5 us (33%)
  Pallas kernels  12.7 us (19%)
  local copies, waits for them, and re-layouts  1.74 us (3%)
  between operations  0.76 us (1%)
    ppermute x22, starting transfers between devices, swap(): return lax.ppermute(value, axes, [(i, i ^ offset) for i in range(size)])  25.5 us
    ppermute x22, waiting for transfers between devices, swap(): return lax.ppermute(value, axes, [(i, i ^ offset) for i in range(size)])  15.9 us
    pallas_call x12, Pallas kernels, run(): pl.pallas_call(kernel, out_shape=[jax.ShapeDtypeStruct(s, d) for s, d in...  12.7 us
    all_to_all x1, waiting for transfers between devices, local(): grams = lax.all_to_all(grams, NAMES, 0, 0, tiled=True)  6.55 us
    all_to_all x1, starting transfers between devices, local(): grams = lax.all_to_all(grams, NAMES, 0, 0, tiled=True)  3.59 us
    unnamed x4, local copies, waits for them, and re-layouts  1.74 us
  transfers between devices with their start and end apart: 23, of which 14 were waited for; matrix products, arithmetic and copies ran while one was open for 1% of the time, Pallas kernels for 8%

profile of v4, /device:TPU:0, one launch (start us, length us, event | category | flops | bytes accessed | tf_op | source)
XLA Modules:
  0.0 67.3 jit_solution(1923658276884159449)
XLA Ops:
  0.6 3.1 %collective-permute-start.4 = (bf16[320,256]{1,0:T(8,128)(2,1)}, bf16[320,256]{1,0:T(8,128)(2,1)S(1)}, u32[]{:S(2)}, u32[]{:S(2)}) collective-permute-start(bf16[320,256]{1,0:T(8,128)(2,1)} %emb_ref.1), channel_id=1, source_target_pairs={{0,8},{1,9},{4,12},{5,13},{8,0},{9,1},{12,4},{13,5},{2,10},{3,11},... | collective-permute-start | bytes 491528 | tf_op jit(solution)/shard_map/ppermute | solution.py:402
  3.7 2.6 %collective-permute-start.3 = (bf16[320,256]{1,0:T(8,128)(2,1)}, bf16[320,256]{1,0:T(8,128)(2,1)S(1)}, u32[]{:S(2)}, u32[]{:S(2)}) collective-permute-start(bf16[320,256]{1,0:T(8,128)(2,1)} %emb_ref.1), channel_id=1, source_target_pairs={{0,16},{2,18},{16,0},{18,2},{1,17},{3,19},{17,1},{19,3},{4,20},{6,... | collective-permute-start | bytes 491528 | tf_op jit(solution)/shard_map/ppermute | solution.py:402
  6.3 1.5 %collective-permute-start.2 = (bf16[320,256]{1,0:T(8,128)(2,1)}, bf16[320,256]{1,0:T(8,128)(2,1)S(1)}, u32[]{:S(2)}, u32[]{:S(2)}) collective-permute-start(bf16[320,256]{1,0:T(8,128)(2,1)} %emb_ref.1), channel_id=1, source_target_pairs={{0,2},{2,0},{16,18},{18,16},{1,3},{3,1},{17,19},{19,17},{4,6},{6,4... | collective-permute-start | bytes 491528 | tf_op jit(solution)/shard_map/ppermute | solution.py:402
  7.8 1.5 %collective-permute-start.1 = (bf16[320,256]{1,0:T(8,128)(2,1)}, bf16[320,256]{1,0:T(8,128)(2,1)S(1)}, u32[]{:S(2)}, u32[]{:S(2)}) collective-permute-start(bf16[320,256]{1,0:T(8,128)(2,1)} %emb_ref.1), channel_id=1, source_target_pairs={{0,4},{1,5},{4,0},{5,1},{8,12},{9,13},{12,8},{13,9},{2,6},{3,7},{6... | collective-permute-start | bytes 491528 | tf_op jit(solution)/shard_map/ppermute | solution.py:402
  9.3 0.9 %copy-done = bf16[320,256]{1,0:T(8,128)(2,1)S(1)} copy-done((bf16[320,256]{1,0:T(8,128)(2,1)S(1)}, bf16[320,256]{1,0:T(8,128)(2,1)}, u32[]{:S(2)}) %copy-start) | copy-done | bytes 163864
  10.3 0.8 %copy-done.1 = f32[32,320]{1,0:T(8,128)S(1)} copy-done((f32[32,320]{1,0:T(8,128)S(1)}, f32[32,320]{1,0:T(8,128)}, u32[]{:S(2)}) %copy-start.1) | copy-done | bytes 40984
  11.1 0.1 shard_map.41
  11.2 0.1 collective-permute-done.4.refs_3_
  11.3 1.8 %collective-permute-start.6 = (bf16[320,256]{1,0:T(8,128)(2,1)S(1)}, bf16[320,256]{1,0:T(8,128)(2,1)S(1)}, u32[]{:S(2)}, u32[]{:S(2)}) collective-permute-start(bf16[320,256]{1,0:T(8,128)(2,1)S(1)} %collective-permute-done.4.refs_3_), channel_id=1, source_target_pairs={{0,4},{1,5},{4,0},{5,1},{8,12},{9,13},{12,8},{13,9},{2,6},{3,7},{6... | collective-permute-start | bytes 491528 | tf_op jit(solution)/shard_map/ppermute | solution.py:402
  13.2 0.9 %collective-permute-done.3.refs_1_ = bf16[320,256]{1,0:T(8,128)(2,1)S(1)} collective-permute-done((bf16[320,256]{1,0:T(8,128)(2,1)}, bf16[320,256]{1,0:T(8,128)(2,1)S(1)}, u32[]{:S(2)}, u32[]{:S(2)}) %collective-permute-start.3) | collective-permute-done | bytes 163872 | tf_op jit(solution)/shard_map/ppermute | solution.py:402
  14.1 0.1 collective-permute-start.7
  14.2 0.5 collective-permute-start.8
  14.7 0.3 collective-permute-start.5
  15.0 1.5 %collective-permute-start.9 = (bf16[320,256]{1,0:T(8,128)(2,1)S(1)}, bf16[320,256]{1,0:T(8,128)(2,1)S(1)}, u32[]{:S(2)}, u32[]{:S(2)}) collective-permute-start(bf16[320,256]{1,0:T(8,128)(2,1)S(1)} %collective-permute-done.3.refs_1_), channel_id=1, source_target_pairs={{0,2},{2,0},{16,18},{18,16},{1,3},{3,1},{17,19},{19,17},{4,6},{6,4... | collective-permute-start | bytes 491528 | tf_op jit(solution)/shard_map/ppermute | solution.py:402
  16.5 3.0 %collective-permute-done.5.refs_1_.refs_4_ = bf16[32,320]{1,0:T(8,128)(2,1)S(1)} collective-permute-done((bf16[32,320]{1,0:T(8,128)(2,1)S(1)}, bf16[32,320]{1,0:T(8,128)(2,1)S(1)}, u32[]{:S(2)}, u32[]{:S(2)}) %collective-permute-start.5) | collective-permute-done | bytes 20512 | tf_op jit(solution)/shard_map/ppermute | solution.py:402
  19.5 2.0 %shard_map.42 = (bf16[960,256]{1,0:T(8,128)(2,1)S(1)}, bf16[1280,256]{1,0:T(8,128)(2,1)S(1)}, bf16[960,256]{1,0:T(8,128)(2,1)S(1)}, bf16[960,1280]{1,0:T(8,128)(...) custom-call(bf16[320,256]{1,0:T(8,128)(2,1)S(1)} %get-tuple-element.46.unit_ref, ...), custom_call_target="tpu_custom_call" | custom-call | flops 1101004800 | tf_op jit(solution)/shard_map/pallas_call | solution.py:28
  21.6 1.7 %shard_map.43 = (bf16[960,320]{1,0:T(8,128)(2,1)S(1)}, bf16[320,1280]{1,0:T(8,128)(2,1)S(1)}, bf16[320,1280]{1,0:T(8,128)(2,1)S(1)}, f32[4,320]{1,0:T(4,128)S(1)}, bf16[72,320]{1,0:T(8,128)(2,1)S(1)}) custom-call(bf16[960,256]{1,0:T(8,128)(2,1)S(1)} %get-tuple-element.53.rows_ref, f32[960,128]{1,0:T(8,128)S(1)} %get-tuple-element.54.fold_in_ref, ...), custom_call_target="tpu_custom_call" | custom-call | flops 576716800 | tf_op jit(solution)/shard_map/pallas_call | solution.py:28
  23.3 1.6 %collective-permute-start.11 = (bf16[72,320]{1,0:T(8,128)(2,1)S(1)}, bf16[72,320]{1,0:T(8,128)(2,1)S(1)}, u32[]{:S(2)}, u32[]{:S(2)}) collective-permute-start(bf16[72,320]{1,0:T(8,128)(2,1)S(1)} %get-tuple-element.62), channel_id=1, source_target_pairs={{0,2},{2,0},{16,18},{18,16},{1,3},{3,1},{17,19},{19,17},{4,6},{6,4... | collective-permute-start | bytes 138248 | tf_op jit(solution)/shard_map/ppermute | solution.py:402
  24.9 1.8 %collective-permute-start.13 = (f32[4,320]{1,0:T(4,128)S(1)}, f32[4,320]{1,0:T(4,128)S(1)}, u32[]{:S(2)}, u32[]{:S(2)}) collective-permute-start(f32[4,320]{1,0:T(4,128)S(1)} %get-tuple-element.63.refs_6_), channel_id=1, source_target_pairs={{0,18},{2,16},{16,2},{18,0},{1,19},{3,17},{17,3},{19,1},{4,22},{6,... | collective-permute-start | bytes 15368 | tf_op jit(solution)/shard_map/ppermute | solution.py:402
  26.7 1.1 %collective-permute-start.12 = (f32[4,320]{1,0:T(4,128)S(1)}, f32[4,320]{1,0:T(4,128)S(1)}, u32[]{:S(2)}, u32[]{:S(2)}) collective-permute-start(f32[4,320]{1,0:T(4,128)S(1)} %get-tuple-element.63.refs_6_), channel_id=1, source_target_pairs={{0,16},{2,18},{16,0},{18,2},{1,17},{3,19},{17,1},{19,3},{4,20},{6,... | collective-permute-start | bytes 15368 | tf_op jit(solution)/shard_map/ppermute | solution.py:402
  27.8 2.5 %collective-permute-done.13.refs_8_ = f32[4,320]{1,0:T(4,128)S(1)} collective-permute-done((f32[4,320]{1,0:T(4,128)S(1)}, f32[4,320]{1,0:T(4,128)S(1)}, u32[]{:S(2)}, u32[]{:S(2)}) %collective-permute-start.13) | collective-permute-done | bytes 5152 | tf_op jit(solution)/shard_map/ppermute | solution.py:402
  30.3 0.9 %collective-permute-done.12.refs_7_ = f32[4,320]{1,0:T(4,128)S(1)} collective-permute-done((f32[4,320]{1,0:T(4,128)S(1)}, f32[4,320]{1,0:T(4,128)S(1)}, u32[]{:S(2)}, u32[]{:S(2)}) %collective-permute-start.12) | collective-permute-done | bytes 5152 | tf_op jit(solution)/shard_map/ppermute | solution.py:402
  31.3 0.8 %shard_map.44 = (bf16[4,32,320]{2,1,0:T(8,128)(2,1)S(1)}, bf16[32,960]{1,0:T(8,128)(2,1)S(1)}, bf16[32,320]{1,0:T(8,128)(2,1)S(1)}, f32[1,320]{1,0:T(1,128)S(1)}, f32[1,320]{1,0:T(1,128)S(1)}) custom-call(bf16[960,960]{1,0:T(8,128)(2,1)S(1)} %get-tuple-element.52.refs_0_, bf16[960,320]{1,0:T(8,128)(2,1)S(1)} %get-tuple-element.58.refs_1_, ...), custom_call_target="tpu_custom_call" | custom-call | tf_op jit(solution)/shard_map/pallas_call | solution.py:28
  32.1 0.7 %shard_map.45.pieces_ref = f32[4,32,320]{2,1,0:T(8,128)S(1)} custom-call(bf16[960,1280]{1,0:T(8,128)(2,1)S(1)} %get-tuple-element.60.refs_0_, bf16[320,1280]{1,0:T(8,128)(2,1)S(1)} %get-tuple-element.61.refs_1_, bf16[32,960]{1,0:T(8,128)(2,1)S(1)} %get-tuple-element.64.refs_2_, bf16[32,320]{1,0:T(8,128)(2,1)S(1)} %get-tuple-element.65.refs_3_), custom_call_target="tpu_custom_call" | custom-call | flops 104857600 | tf_op jit(solution)/shard_map/pallas_call | solution.py:28
  32.8 0.6 collective-permute-done.14.other_ref
  33.4 0.1 shard_map.46.refs_0_
  33.5 2.0 %collective-permute-start.17 = (bf16[32,1408]{1,0:T(8,128)(2,1)S(1)}, bf16[32,1408]{1,0:T(8,128)(2,1)S(1)}, u32[]{:S(2)}, u32[]{:S(2)}) collective-permute-start(bf16[32,1408]{1,0:T(8,128)(2,1)S(1)} %shard_map.46.refs_0_), channel_id=1, source_target_pairs={{0,12},{1,13},{4,8},{5,9},{8,4},{9,5},{12,0},{13,1},{2,14},{3,15},... | collective-permute-start | bytes 270344 | tf_op jit(solution)/shard_map/ppermute | solution.py:402
  35.5 1.0 %collective-permute-start.16 = (bf16[32,1408]{1,0:T(8,128)(2,1)S(1)}, bf16[32,1408]{1,0:T(8,128)(2,1)S(1)}, u32[]{:S(2)}, u32[]{:S(2)}) collective-permute-start(bf16[32,1408]{1,0:T(8,128)(2,1)S(1)} %shard_map.46.refs_0_), channel_id=1, source_target_pairs={{0,8},{1,9},{4,12},{5,13},{8,0},{9,1},{12,4},{13,5},{2,10},{3,11},... | collective-permute-start | bytes 270344 | tf_op jit(solution)/shard_map/ppermute | solution.py:402
  36.5 0.5 collective-permute-start.15
  37.1 2.9 %collective-permute-done.17.refs_3_ = bf16[32,1408]{1,0:T(8,128)(2,1)S(1)} collective-permute-done((bf16[32,1408]{1,0:T(8,128)(2,1)S(1)}, bf16[32,1408]{1,0:T(8,128)(2,1)S(1)}, u32[]{:S(2)}, u32[]{:S(2)}) %collective-permute-start.17) | collective-permute-done | bytes 90144 | tf_op jit(solution)/shard_map/ppermute | solution.py:402
  39.9 1.2 %collective-permute-done.16.refs_2_ = bf16[32,1408]{1,0:T(8,128)(2,1)S(1)} collective-permute-done((bf16[32,1408]{1,0:T(8,128)(2,1)S(1)}, bf16[32,1408]{1,0:T(8,128)(2,1)S(1)}, u32[]{:S(2)}, u32[]{:S(2)}) %collective-permute-start.16) | collective-permute-done | bytes 90144 | tf_op jit(solution)/shard_map/ppermute | solution.py:402
  41.1 0.1 collective-permute-done.15.refs_1_
  41.3 0.7 shard_map.47.refs_2_.refs_3_
  42.0 1.2 %shard_map.48.refs_5_ = f32[32,1280]{1,0:T(8,128)S(1)} custom-call(bf16[960,1280]{1,0:T(8,128)(2,1)S(1)} %get-tuple-element.60.refs_0_, bf16[320,1280]{1,0:T(8,128)(2,1)S(1)} %get-tuple-element.61.refs_1_, bf16[4,64,384]{2,1,0:T(8,128)(2,1)S(1)} %shard_map.47.refs_2_.refs_3_), custom_call_target="tpu_custom_call" | custom-call | flops 209715200 | tf_op jit(solution)/shard_map/pallas_call | solution.py:28
  43.1 0.3 collective-permute-done.18.refs_4_
  43.4 1.4 %shard_map.49 = (f32[32,384]{1,0:T(8,128)S(1)}, bf16[32,384]{1,0:T(8,128)(2,1)S(1)}, bf16[32,384]{1,0:T(8,128)(2,1)S(1)}, bf16[32,384]{1,0:T(8,128)(2,1)S(1)}) custom-call(bf16[960,960]{1,0:T(8,128)(2,1)S(1)} %get-tuple-element.52.refs_0_, bf16[960,320]{1,0:T(8,128)(2,1)S(1)} %get-tuple-element.58.refs_1_, bf16[320,1280]{1,0:T(8,128)(2,1)S(1)} %get-tuple-element.59.refs_2_, ...), custom_call_target="tpu_custom_call" | custom-call | tf_op jit(solution)/shard_map/pallas_call | solution.py:28
  44.8 2.1 %collective-permute-start.19 = (bf16[32,384]{1,0:T(8,128)(2,1)S(1)}, bf16[32,384]{1,0:T(8,128)(2,1)S(1)}, u32[]{:S(2)}, u32[]{:S(2)}) collective-permute-start(bf16[32,384]{1,0:T(8,128)(2,1)S(1)} %get-tuple-element.69), channel_id=1, source_target_pairs={{0,18},{2,16},{16,2},{18,0},{1,19},{3,17},{17,3},{19,1},{4,22},{6,... | collective-permute-start | bytes 73736 | tf_op jit(solution)/shard_map/ppermute | solution.py:402
  46.9 1.8 %collective-permute-start.20 = (bf16[32,384]{1,0:T(8,128)(2,1)S(1)}, bf16[32,384]{1,0:T(8,128)(2,1)S(1)}, u32[]{:S(2)}, u32[]{:S(2)}) collective-permute-start(bf16[32,384]{1,0:T(8,128)(2,1)S(1)} %get-tuple-element.70), channel_id=1, source_target_pairs={{0,16},{2,18},{16,0},{18,2},{1,17},{3,19},{17,1},{19,3},{4,20},{6,... | collective-permute-start | bytes 73736 | tf_op jit(solution)/shard_map/ppermute | solution.py:402
  48.7 0.5 collective-permute-start.21
  49.2 1.4 %collective-permute-done.19.refs_1_ = bf16[32,384]{1,0:T(8,128)(2,1)S(1)} collective-permute-done((bf16[32,384]{1,0:T(8,128)(2,1)S(1)}, bf16[32,384]{1,0:T(8,128)(2,1)S(1)}, u32[]{:S(2)}, u32[]{:S(2)}) %collective-permute-start.19) | collective-permute-done | bytes 24608 | tf_op jit(solution)/shard_map/ppermute | solution.py:402
  50.6 1.1 %collective-permute-done.20.refs_2_ = bf16[32,384]{1,0:T(8,128)(2,1)S(1)} collective-permute-done((bf16[32,384]{1,0:T(8,128)(2,1)S(1)}, bf16[32,384]{1,0:T(8,128)(2,1)S(1)}, u32[]{:S(2)}, u32[]{:S(2)}) %collective-permute-start.20) | collective-permute-done | bytes 24608 | tf_op jit(solution)/shard_map/ppermute | solution.py:402
  51.7 0.9 %collective-permute-done.21.refs_3_ = bf16[32,384]{1,0:T(8,128)(2,1)S(1)} collective-permute-done((bf16[32,384]{1,0:T(8,128)(2,1)S(1)}, bf16[32,384]{1,0:T(8,128)(2,1)S(1)}, u32[]{:S(2)}, u32[]{:S(2)}) %collective-permute-start.21) | collective-permute-done | bytes 24608 | tf_op jit(solution)/shard_map/ppermute | solution.py:402
  52.5 0.9 %shard_map.50 = (f32[32,320]{1,0:T(8,128)S(1)}, f32[32,32]{1,0:T(8,128)S(1)}, f32[32,8,128]{2,1,0:T(8,128)}) custom-call(f32[32,384]{1,0:T(8,128)S(1)} %get-tuple-element.68.refs_0_, bf16[32,384]{1,0:T(8,128)(2,1)S(1)} %collective-permute-done.19.refs_1_, bf16[32,384]{1,0:T(8,128)(2,1)S(1)} %collective-permute-done.20.refs_2_, ...), custom_call_target="tpu_custom_call" | custom-call | tf_op jit(solution)/shard_map/pallas_call | solution.py:28
  53.5 3.6 %all-to-all-start = ((f32[32,8,128]{2,1,0:T(8,128)}), f32[32,8,128]{2,1,0:T(8,128)S(1)}, u32[]{:S(2)}, u32[]{:S(2)}) async-start(f32[32,8,128]{2,1,0:T(8,128)} %get-tuple-element.76), calls=%async_computation | async-start | bytes 262144 | tf_op jit(solution)/shard_map/all_to_all | solution.py:541
  57.1 0.6 reduce
  57.7 1.1 %shard_map.51 = (f32[32,320]{1,0:T(8,128)S(1)}, f32[32,32]{1,0:T(8,128)S(1)}) custom-call(f32[32,320]{1,0:T(8,128)S(1)} %get-tuple-element.72.image_ref, f32[32,32]{1,0:T(8,128)S(1)} %get-tuple-element.73.gram_ref), custom_call_target="tpu_custom_call" | custom-call | tf_op jit(solution)/shard_map/pallas_call | solution.py:28
  58.7 6.6 %all-to-all-done.grams_ref = f32[32,8,128]{2,1,0:T(8,128)S(1)} async-done(((f32[32,8,128]{2,1,0:T(8,128)}), f32[32,8,128]{2,1,0:T(8,128)S(1)}, u32[]{:S(2)}, u32[]{:S(2)}) %all-to-all-start) | async-done | bytes 131104 | tf_op jit(solution)/shard_map/all_to_all | solution.py:541
  65.3 2.0 %shard_map.52 = f32[32,320]{1,0:T(8,128)} custom-call(f32[32,320]{1,0:T(8,128)S(1)} %get-tuple-element.74.image_ref, f32[32,32]{1,0:T(8,128)S(1)} %get-tuple-element.75.inverse_ref, f32[32,8,128]{2,1,0:T(8,128)S(1)} %all-to-all-done.grams_ref), custom_call_target="tpu_custom_call" | custom-call | tf_op jit(solution)/shard_map/pallas_call | solution.py:28
  (15 shorter events, 0.2 us)
Async XLA Ops:
  0.6 10.7 %collective-permute-start.4 = (bf16[320,256]{1,0:T(8,128)(2,1)}, bf16[320,256]{1,0:T(8,128)(2,1)S(1)}, u32[]{:S(2)}, u32[]{:S(2)}) collective-permute-start(bf16[320,256]{1,0:T(8,128)(2,1)} %emb_ref.1), channel_id=1, source_target_pairs={{0,8},{1,9},{4,12},{5,13},{8,0},{9,1},{12,4},{13,5},{2,10},{3,11},... | collective-permute-start | bytes 491528 | tf_op jit(solution)/shard_map/ppermute | solution.py:402
  3.7 10.3 %collective-permute-start.3 = (bf16[320,256]{1,0:T(8,128)(2,1)}, bf16[320,256]{1,0:T(8,128)(2,1)S(1)}, u32[]{:S(2)}, u32[]{:S(2)}) collective-permute-start(bf16[320,256]{1,0:T(8,128)(2,1)} %emb_ref.1), channel_id=1, source_target_pairs={{0,16},{2,18},{16,0},{18,2},{1,17},{3,19},{17,1},{19,3},{4,20},{6,... | collective-permute-start | bytes 491528 | tf_op jit(solution)/shard_map/ppermute | solution.py:402
  6.3 7.8 %collective-permute-start.2 = (bf16[320,256]{1,0:T(8,128)(2,1)}, bf16[320,256]{1,0:T(8,128)(2,1)S(1)}, u32[]{:S(2)}, u32[]{:S(2)}) collective-permute-start(bf16[320,256]{1,0:T(8,128)(2,1)} %emb_ref.1), channel_id=1, source_target_pairs={{0,2},{2,0},{16,18},{18,16},{1,3},{3,1},{17,19},{19,17},{4,6},{6,4... | collective-permute-start | bytes 491528 | tf_op jit(solution)/shard_map/ppermute | solution.py:402
  7.8 6.3 %collective-permute-start.1 = (bf16[320,256]{1,0:T(8,128)(2,1)}, bf16[320,256]{1,0:T(8,128)(2,1)S(1)}, u32[]{:S(2)}, u32[]{:S(2)}) collective-permute-start(bf16[320,256]{1,0:T(8,128)(2,1)} %emb_ref.1), channel_id=1, source_target_pairs={{0,4},{1,5},{4,0},{5,1},{8,12},{9,13},{12,8},{13,9},{2,6},{3,7},{6... | collective-permute-start | bytes 491528 | tf_op jit(solution)/shard_map/ppermute | solution.py:402
  9.3 4.8 %collective-permute-start = (bf16[320,256]{1,0:T(8,128)(2,1)}, bf16[320,256]{1,0:T(8,128)(2,1)S(1)}, u32[]{:S(2)}, u32[]{:S(2)}) collective-permute-start(bf16[320,256]{1,0:T(8,128)(2,1)} %emb_ref.1), channel_id=1, source_target_pairs={{0,1},{1,0},{4,5},{5,4},{8,9},{9,8},{12,13},{13,12},{2,3},{3,2},{6... | collective-permute-start | bytes 491528 | tf_op jit(solution)/shard_map/ppermute | solution.py:402
  9.3 0.9 %copy-start = (bf16[320,256]{1,0:T(8,128)(2,1)S(1)}, bf16[320,256]{1,0:T(8,128)(2,1)}, u32[]{:S(2)}) copy-start(bf16[320,256]{1,0:T(8,128)(2,1)} %emb_ref.1) | copy-start | bytes 491524
  10.3 0.8 %copy-start.1 = (f32[32,320]{1,0:T(8,128)S(1)}, f32[32,320]{1,0:T(8,128)}, u32[]{:S(2)}) copy-start(f32[32,320]{1,0:T(8,128)} %start_ref.1) | copy-start | bytes 122884
  11.3 8.2 %collective-permute-start.6 = (bf16[320,256]{1,0:T(8,128)(2,1)S(1)}, bf16[320,256]{1,0:T(8,128)(2,1)S(1)}, u32[]{:S(2)}, u32[]{:S(2)}) collective-permute-start(bf16[320,256]{1,0:T(8,128)(2,1)S(1)} %collective-permute-done.4.refs_3_), channel_id=1, source_target_pairs={{0,4},{1,5},{4,0},{5,1},{8,12},{9,13},{12,8},{13,9},{2,6},{3,7},{6... | collective-permute-start | bytes 491528 | tf_op jit(solution)/shard_map/ppermute | solution.py:402
  14.1 5.4 %collective-permute-start.7 = (bf16[320,256]{1,0:T(8,128)(2,1)S(1)}, bf16[320,256]{1,0:T(8,128)(2,1)S(1)}, u32[]{:S(2)}, u32[]{:S(2)}) collective-permute-start(bf16[320,256]{1,0:T(8,128)(2,1)S(1)} %collective-permute-done.1.refs_2_), channel_id=1, source_target_pairs={{0,1},{1,0},{4,5},{5,4},{8,9},{9,8},{12,13},{13,12},{2,3},{3,2},{6... | collective-permute-start | bytes 491528 | tf_op jit(solution)/shard_map/ppermute | solution.py:402
  14.2 5.4 %collective-permute-start.8 = (bf16[320,256]{1,0:T(8,128)(2,1)S(1)}, bf16[320,256]{1,0:T(8,128)(2,1)S(1)}, u32[]{:S(2)}, u32[]{:S(2)}) collective-permute-start(bf16[320,256]{1,0:T(8,128)(2,1)S(1)} %collective-permute-done.4.refs_3_), channel_id=1, source_target_pairs={{0,1},{1,0},{4,5},{5,4},{8,9},{9,8},{12,13},{13,12},{2,3},{3,2},{6... | collective-permute-start | bytes 491528 | tf_op jit(solution)/shard_map/ppermute | solution.py:402
  14.7 4.9 %collective-permute-start.5 = (bf16[32,320]{1,0:T(8,128)(2,1)S(1)}, bf16[32,320]{1,0:T(8,128)(2,1)S(1)}, u32[]{:S(2)}, u32[]{:S(2)}) collective-permute-start(bf16[32,320]{1,0:T(8,128)(2,1)S(1)} %get-tuple-element.44.refs_0_.refs_3_), channel_id=1, source_target_pairs={{0,16},{2,18},{16,0},{18,2},{1,17},{3,19},{17,1},{19,3},{4,20},{6,... | collective-permute-start | bytes 61448 | tf_op jit(solution)/shard_map/ppermute | solution.py:402
  15.0 6.6 %collective-permute-start.9 = (bf16[320,256]{1,0:T(8,128)(2,1)S(1)}, bf16[320,256]{1,0:T(8,128)(2,1)S(1)}, u32[]{:S(2)}, u32[]{:S(2)}) collective-permute-start(bf16[320,256]{1,0:T(8,128)(2,1)S(1)} %collective-permute-done.3.refs_1_), channel_id=1, source_target_pairs={{0,2},{2,0},{16,18},{18,16},{1,3},{3,1},{17,19},{19,17},{4,6},{6,4... | collective-permute-start | bytes 491528 | tf_op jit(solution)/shard_map/ppermute | solution.py:402
  19.5 2.1 %collective-permute-start.10 = (bf16[320,256]{1,0:T(8,128)(2,1)S(1)}, bf16[320,256]{1,0:T(8,128)(2,1)S(1)}, u32[]{:S(2)}, u32[]{:S(2)}) collective-permute-start(bf16[320,256]{1,0:T(8,128)(2,1)S(1)} %collective-permute-done.6.refs_4_), channel_id=1, source_target_pairs={{0,1},{1,0},{4,5},{5,4},{8,9},{9,8},{12,13},{13,12},{2,3},{3,2},{6... | collective-permute-start | bytes 491528 | tf_op jit(solution)/shard_map/ppermute | solution.py:402
  23.3 7.9 %collective-permute-start.11 = (bf16[72,320]{1,0:T(8,128)(2,1)S(1)}, bf16[72,320]{1,0:T(8,128)(2,1)S(1)}, u32[]{:S(2)}, u32[]{:S(2)}) collective-permute-start(bf16[72,320]{1,0:T(8,128)(2,1)S(1)} %get-tuple-element.62), channel_id=1, source_target_pairs={{0,2},{2,0},{16,18},{18,16},{1,3},{3,1},{17,19},{19,17},{4,6},{6,4... | collective-permute-start | bytes 138248 | tf_op jit(solution)/shard_map/ppermute | solution.py:402
  24.9 5.4 %collective-permute-start.13 = (f32[4,320]{1,0:T(4,128)S(1)}, f32[4,320]{1,0:T(4,128)S(1)}, u32[]{:S(2)}, u32[]{:S(2)}) collective-permute-start(f32[4,320]{1,0:T(4,128)S(1)} %get-tuple-element.63.refs_6_), channel_id=1, source_target_pairs={{0,18},{2,16},{16,2},{18,0},{1,19},{3,17},{17,3},{19,1},{4,22},{6,... | collective-permute-start | bytes 15368 | tf_op jit(solution)/shard_map/ppermute | solution.py:402
  26.7 4.5 %collective-permute-start.12 = (f32[4,320]{1,0:T(4,128)S(1)}, f32[4,320]{1,0:T(4,128)S(1)}, u32[]{:S(2)}, u32[]{:S(2)}) collective-permute-start(f32[4,320]{1,0:T(4,128)S(1)} %get-tuple-element.63.refs_6_), channel_id=1, source_target_pairs={{0,16},{2,18},{16,0},{18,2},{1,17},{3,19},{17,1},{19,3},{4,20},{6,... | collective-permute-start | bytes 15368 | tf_op jit(solution)/shard_map/ppermute | solution.py:402
  32.0 1.4 %collective-permute-start.14 = (bf16[4,32,320]{2,1,0:T(8,128)(2,1)S(1)}, bf16[4,32,320]{2,1,0:T(8,128)(2,1)S(1)}, u32[]{:S(2)}, u32[]{:S(2)}) collective-permute-start(bf16[4,32,320]{2,1,0:T(8,128)(2,1)S(1)} %get-tuple-element.66), channel_id=1, source_target_pairs={{0,1},{1,0},{4,5},{5,4},{8,9},{9,8},{12,13},{13,12},{2,3},{3,2},{6... | collective-permute-start | bytes 245768 | tf_op jit(solution)/shard_map/ppermute | solution.py:402
  33.5 6.4 %collective-permute-start.17 = (bf16[32,1408]{1,0:T(8,128)(2,1)S(1)}, bf16[32,1408]{1,0:T(8,128)(2,1)S(1)}, u32[]{:S(2)}, u32[]{:S(2)}) collective-permute-start(bf16[32,1408]{1,0:T(8,128)(2,1)S(1)} %shard_map.46.refs_0_), channel_id=1, source_target_pairs={{0,12},{1,13},{4,8},{5,9},{8,4},{9,5},{12,0},{13,1},{2,14},{3,15},... | collective-permute-start | bytes 270344 | tf_op jit(solution)/shard_map/ppermute | solution.py:402
  35.5 5.6 %collective-permute-start.16 = (bf16[32,1408]{1,0:T(8,128)(2,1)S(1)}, bf16[32,1408]{1,0:T(8,128)(2,1)S(1)}, u32[]{:S(2)}, u32[]{:S(2)}) collective-permute-start(bf16[32,1408]{1,0:T(8,128)(2,1)S(1)} %shard_map.46.refs_0_), channel_id=1, source_target_pairs={{0,8},{1,9},{4,12},{5,13},{8,0},{9,1},{12,4},{13,5},{2,10},{3,11},... | collective-permute-start | bytes 270344 | tf_op jit(solution)/shard_map/ppermute | solution.py:402
  36.5 4.7 %collective-permute-start.15 = (bf16[32,1408]{1,0:T(8,128)(2,1)S(1)}, bf16[32,1408]{1,0:T(8,128)(2,1)S(1)}, u32[]{:S(2)}, u32[]{:S(2)}) collective-permute-start(bf16[32,1408]{1,0:T(8,128)(2,1)S(1)} %shard_map.46.refs_0_), channel_id=1, source_target_pairs={{0,4},{1,5},{4,0},{5,1},{8,12},{9,13},{12,8},{13,9},{2,6},{3,7},{6... | collective-permute-start | bytes 270344 | tf_op jit(solution)/shard_map/ppermute | solution.py:402
  41.9 1.5 %collective-permute-start.18 = (bf16[4,64,384]{2,1,0:T(8,128)(2,1)S(1)}, bf16[4,64,384]{2,1,0:T(8,128)(2,1)S(1)}, u32[]{:S(2)}, u32[]{:S(2)}) collective-permute-start(bf16[4,64,384]{2,1,0:T(8,128)(2,1)S(1)} %shard_map.47.refs_2_.refs_3_), channel_id=1, source_target_pairs={{0,1},{1,0},{4,5},{5,4},{8,9},{9,8},{12,13},{13,12},{2,3},{3,2},{6... | collective-permute-start | bytes 589832 | tf_op jit(solution)/shard_map/ppermute | solution.py:402
  44.8 5.8 %collective-permute-start.19 = (bf16[32,384]{1,0:T(8,128)(2,1)S(1)}, bf16[32,384]{1,0:T(8,128)(2,1)S(1)}, u32[]{:S(2)}, u32[]{:S(2)}) collective-permute-start(bf16[32,384]{1,0:T(8,128)(2,1)S(1)} %get-tuple-element.69), channel_id=1, source_target_pairs={{0,18},{2,16},{16,2},{18,0},{1,19},{3,17},{17,3},{19,1},{4,22},{6,... | collective-permute-start | bytes 73736 | tf_op jit(solution)/shard_map/ppermute | solution.py:402
  46.9 4.7 %collective-permute-start.20 = (bf16[32,384]{1,0:T(8,128)(2,1)S(1)}, bf16[32,384]{1,0:T(8,128)(2,1)S(1)}, u32[]{:S(2)}, u32[]{:S(2)}) collective-permute-start(bf16[32,384]{1,0:T(8,128)(2,1)S(1)} %get-tuple-element.70), channel_id=1, source_target_pairs={{0,16},{2,18},{16,0},{18,2},{1,17},{3,19},{17,1},{19,3},{4,20},{6,... | collective-permute-start | bytes 73736 | tf_op jit(solution)/shard_map/ppermute | solution.py:402
  48.7 3.8 %collective-permute-start.21 = (bf16[32,384]{1,0:T(8,128)(2,1)S(1)}, bf16[32,384]{1,0:T(8,128)(2,1)S(1)}, u32[]{:S(2)}, u32[]{:S(2)}) collective-permute-start(bf16[32,384]{1,0:T(8,128)(2,1)S(1)} %get-tuple-element.71), channel_id=1, source_target_pairs={{0,2},{2,0},{16,18},{18,16},{1,3},{3,1},{17,19},{19,17},{4,6},{6,4... | collective-permute-start | bytes 73736 | tf_op jit(solution)/shard_map/ppermute | solution.py:402
  53.5 11.8 %all-to-all-start = ((f32[32,8,128]{2,1,0:T(8,128)}), f32[32,8,128]{2,1,0:T(8,128)S(1)}, u32[]{:S(2)}, u32[]{:S(2)}) async-start(f32[32,8,128]{2,1,0:T(8,128)} %get-tuple-element.76), calls=%async_computation | async-start | bytes 262144 | tf_op jit(solution)/shard_map/all_to_all | solution.py:541
